TPU v7x, 32 devices: a whole 2x2x4 slice. The times are simulated.
32 devices in a mesh: section: 2 (over y), fsdp: 16 (over z, x, core).
Axes of the slice: x: 2, y: 2, z: 4, core: 2. Of those that a mesh axis runs over, the one named last changes fastest.
Arguments:
- tokens: bfloat16 [32, 128, 1280], P('fsdp'), may hold values from -6 to 6
- cotangent: bfloat16 [32, 128, 1280], P('fsdp'), may hold values from -6 to 6
- lengths: int32 [32], P('fsdp'), may hold values from 32 to 128, as said below
- qkv_weight: float32 [2, 1280, 3840], P('section', 'fsdp'), may hold values from -0.15625 to 0.15625
- out_weight: float32 [2, 1280, 1280], P('section', 'fsdp'), may hold values from -1 to 1
- up_weight: float32 [2, 1280, 1280], P('section', 'fsdp'), may hold values from -0.15625 to 0.15625
- down_weight: float32 [2, 1280, 1280], P('section', 'fsdp'), may hold values from -0.15625 to 0.15625
- norm_gains: float32 [2, 1280, 2], P('section', 'fsdp'), may hold values from 0.5 to 1.5
- query_gain: float32 [2, 80], P('section'), may hold values from -1 to 1
Outputs:
- output: bfloat16 [32, 128, 1280], P('fsdp', None, 'section')
- d_tokens: bfloat16 [32, 128, 1280], P('fsdp', None, 'section')
- d_qkv_weight: float32 [2, 1280, 3840], P('section', 'fsdp')
- d_out_weight: float32 [2, 1280, 1280], P('section', 'fsdp')
- d_up_weight: float32 [2, 1280, 1280], P('section', 'fsdp')
- d_down_weight: float32 [2, 1280, 1280], P('section', 'fsdp')
- d_norm_gains: float32 [2, 1280, 2], P('section', 'fsdp')
- d_query_gain: float32 [2, 80], P('section')
Inputs may be any that keep to these rules, and one draw needn't show every extreme that they name: `lengths`: live tokens of each sequence, counted from its start; the first sequence is always full (128).
All inputs are finite; a program needn't handle non-finite values.
Results may differ from a plain program's by a relative error of at most 0.019.
Values may be sent and summed in bfloat16 or wider, within the bound.
A program may use at most 192 MiB of HBM per device.

v0:
```python
import math

import jax
import jax.numpy as jnp
from jax import lax
from jax.sharding import PartitionSpec as P

H = 16
HD = 80


NORM_EPS = 1e-06
NEG_FILL = -1e30
LOG_BASE = 1.442695041


def swapped(value, axis, bit):
    return lax.ppermute(value, axis, [(i, i ^ 1 << bit) for i in range(lax.axis_size(axis))])


def causal_allowed(row_count, length):
    row_ids = lax.broadcasted_iota(jnp.int32, (row_count, row_count), 0)
    col_ids = lax.broadcasted_iota(jnp.int32, (row_count, row_count), 1)
    return (col_ids <= row_ids) & (col_ids < length)


def contract_rows(left, right):
    return lax.dot_general(
        left, right, (((0,), (0,)), ((), ())), preferred_element_type=jnp.float32
    )


def contract_cols(left, right):
    return lax.dot_general(
        left, right, (((1,), (1,)), ((), ())), preferred_element_type=jnp.float32
    )


def norm_back(source, recip, grad_flat):
    return recip * grad_flat - source * recip**3 * jnp.mean(grad_flat * source, -1, keepdims=True)


def layer_forward(layer_input, length, weights, query_scale):
    qkv_w, out_w, up_w, down_w, gain_pair = weights
    row_count, width = layer_input.shape
    gain_one = gain_pair[:, 0].astype(jnp.float32)
    gain_two = gain_pair[:, 1].astype(jnp.float32)
    recip_one = lax.rsqrt(jnp.mean(layer_input * layer_input, -1, keepdims=True) + NORM_EPS)
    normed = (layer_input * recip_one * gain_one).astype(jnp.bfloat16)
    proj = jnp.dot(normed, qkv_w, preferred_element_type=jnp.float32)
    query = proj[:, :width].reshape(row_count, H, HD)
    query_b = (query * query_scale).astype(jnp.bfloat16)
    keys_b = proj[:, width : 2 * width].astype(jnp.bfloat16).reshape(row_count, H, HD)
    values_b = proj[:, 2 * width :].astype(jnp.bfloat16).reshape(row_count, H, HD)
    scores = jnp.einsum("qhd,khd->hqk", query_b, keys_b, preferred_element_type=jnp.float32)
    scores = jnp.where(causal_allowed(row_count, length)[None], scores, NEG_FILL)
    row_peak = jnp.max(scores, -1, keepdims=True)
    expd = jnp.exp(scores - row_peak)
    row_total = jnp.sum(expd, -1, keepdims=True)
    probs = expd / row_total
    logsum = (row_peak + jnp.log(row_total))[..., 0]
    attended = (
        jnp.einsum(
            "hqk,khd->qhd", probs.astype(jnp.bfloat16), values_b, preferred_element_type=jnp.float32
        )
        .reshape(row_count, width)
        .astype(jnp.bfloat16)
    )
    middle = layer_input + jnp.dot(attended, out_w, preferred_element_type=jnp.float32)
    recip_two = lax.rsqrt(jnp.mean(middle * middle, -1, keepdims=True) + NORM_EPS)
    normed_two = (middle * recip_two * gain_two).astype(jnp.bfloat16)
    upper = jnp.dot(normed_two, up_w, preferred_element_type=jnp.float32)
    hidden = jax.nn.silu(upper).astype(jnp.bfloat16)
    layer_output = middle + jnp.dot(hidden, down_w, preferred_element_type=jnp.float32)
    saved = (
        layer_input,
        normed,
        query,
        query_b,
        keys_b,
        values_b,
        logsum,
        attended,
        middle,
        normed_two,
        upper,
        hidden,
        recip_one,
        recip_two,
    )
    return (layer_output, saved)


def layer_backward(saved, length, weights, query_scale, grad_output):
    qkv_w, out_w, up_w, down_w, gain_pair = weights
    (
        layer_input,
        normed,
        query,
        query_b,
        keys_b,
        values_b,
        logsum,
        attended,
        middle,
        normed_two,
        upper,
        hidden,
        recip_one,
        recip_two,
    ) = saved
    row_count, width = layer_input.shape
    gain_one = gain_pair[:, 0].astype(jnp.float32)
    gain_two = gain_pair[:, 1].astype(jnp.float32)
    grad_low = grad_output.astype(jnp.bfloat16)
    d_down = contract_rows(hidden, grad_low)
    d_hidden = contract_cols(grad_low, down_w)
    sigmoid_up = jax.nn.sigmoid(upper)
    d_upper = (d_hidden * sigmoid_up * (1.0 + upper * (1.0 - sigmoid_up))).astype(jnp.bfloat16)
    d_up = contract_rows(normed_two, d_upper)
    d_normed_two = contract_cols(d_upper, up_w)
    d_gain_two = jnp.sum(d_normed_two * middle * recip_two, 0)
    d_middle = grad_output + norm_back(middle, recip_two, d_normed_two * gain_two)
    middle_low = d_middle.astype(jnp.bfloat16)
    d_out = contract_rows(attended, middle_low)
    d_attended = contract_cols(middle_low, out_w).astype(jnp.bfloat16).reshape(row_count, H, HD)
    scores = jnp.einsum("qhd,khd->hqk", query_b, keys_b, preferred_element_type=jnp.float32)
    scores = jnp.where(causal_allowed(row_count, length)[None], scores, NEG_FILL)
    probs = jnp.exp(scores - logsum[..., None])
    d_probs = jnp.einsum("qhd,khd->hqk", d_attended, values_b, preferred_element_type=jnp.float32)
    d_values = jnp.einsum(
        "hqk,qhd->khd", probs.astype(jnp.bfloat16), d_attended, preferred_element_type=jnp.float32
    ).astype(jnp.bfloat16)
    d_scores = (probs * (d_probs - jnp.sum(probs * d_probs, -1, keepdims=True))).astype(
        jnp.bfloat16
    )
    d_query_s = jnp.einsum("hqk,khd->qhd", d_scores, keys_b, preferred_element_type=jnp.float32)
    d_keys = jnp.einsum(
        "hqk,qhd->khd", d_scores, query_b, preferred_element_type=jnp.float32
    ).astype(jnp.bfloat16)
    d_scale = jnp.sum(d_query_s * query, (0, 1))
    d_query = (d_query_s * query_scale).astype(jnp.bfloat16)
    d_proj = jnp.concatenate(
        [
            d_query.reshape(row_count, width),
            d_keys.reshape(row_count, width),
            d_values.reshape(row_count, width),
        ],
        -1,
    )
    d_qkv = contract_rows(normed, d_proj)
    d_normed = contract_cols(d_proj, qkv_w)
    d_gain_one = jnp.sum(d_normed * layer_input * recip_one, 0)
    d_input = d_middle + norm_back(layer_input, recip_one, d_normed * gain_one)
    d_gains = jnp.stack([d_gain_one, d_gain_two], -1)
    return (d_input, (d_qkv, d_out, d_up, d_down, d_gains), d_scale)


def shards(
    tokens,
    cotangent,
    lengths,
    qkv_weight,
    out_weight,
    up_weight,
    down_weight,
    norm_gains,
    query_gain,
):
    section_index = lax.axis_index("section")
    micro_count, slot_rows, width = tokens.shape
    half_width = width // 2
    scale_factor = LOG_BASE / math.sqrt(HD)
    query_scale = jax.nn.softplus(query_gain[0]) * scale_factor

    def gather_weights():
        pieces = (
            lax.all_gather(qkv_weight.astype(jnp.bfloat16), "fsdp", axis=1, tiled=True),
            lax.all_gather(out_weight.astype(jnp.bfloat16), "fsdp", axis=1, tiled=True),
            lax.all_gather(up_weight.astype(jnp.bfloat16), "fsdp", axis=1, tiled=True),
            lax.all_gather(down_weight.astype(jnp.bfloat16), "fsdp", axis=1, tiled=True),
            lax.all_gather(norm_gains.astype(jnp.bfloat16), "fsdp", axis=1, tiled=True),
        )
        return tuple((piece[0] for piece in pieces))

    def handoff(value):
        return swapped(value, "section", 0)

    weights = gather_weights()
    received = jnp.zeros((slot_rows, width), jnp.bfloat16)
    kept = []
    result_parts = []
    for tick_index in range(micro_count + 1):
        first_input = tokens[min(tick_index, micro_count - 1)].astype(jnp.float32)
        layer_input = jnp.where(section_index == 0, first_input, received.astype(jnp.float32))
        micro_index = jnp.clip(tick_index - section_index, 0, micro_count - 1)
        length = lengths[micro_index]
        layer_output, saved = layer_forward(layer_input, length, weights, query_scale)
        sent = layer_output.astype(jnp.bfloat16)
        received = handoff(sent)
        kept.append(saved)
        if tick_index >= 1:
            finished = jnp.where(section_index == 1, sent, received)
            result_parts.append(
                lax.dynamic_slice_in_dim(finished, section_index * half_width, half_width, 1)
            )
    output = jnp.stack(result_parts)
    weights = gather_weights()
    row_ids = lax.iota(jnp.int32, slot_rows)
    grad_received = jnp.zeros((slot_rows, width), jnp.bfloat16)
    grad_parts = []
    grad_totals = None
    scale_total = jnp.zeros((HD,), jnp.float32)
    for tick_index in range(micro_count + 1):
        offset = tick_index - 1 + section_index
        micro_index = jnp.clip(offset, 0, micro_count - 1)
        length = lengths[micro_index]
        live_tick = ((offset >= 0) & (offset < micro_count)).astype(jnp.float32)
        live_rows = (row_ids < length).astype(jnp.float32)[:, None]
        top_grad = cotangent[min(tick_index, micro_count - 1)].astype(jnp.float32) * live_rows
        grad_output = jnp.where(section_index == 1, top_grad, grad_received.astype(jnp.float32))
        saved = jax.tree.map(
            lambda early, late: jnp.where(section_index == 0, early, late),
            kept[max(tick_index - 1, 0)],
            kept[min(tick_index + 1, micro_count)],
        )
        d_input, weight_grads, scale_grad = layer_backward(
            saved, length, weights, query_scale, grad_output
        )
        weight_grads = tuple((item * live_tick for item in weight_grads))
        scale_total = scale_total + scale_grad * live_tick
        sent = d_input.astype(jnp.bfloat16)
        grad_received = handoff(sent)
        if tick_index >= 1:
            finished = jnp.where(section_index == 0, sent, grad_received)
            grad_parts.append(
                lax.dynamic_slice_in_dim(finished, section_index * half_width, half_width, 1)
            )
        if grad_totals is None:
            grad_totals = weight_grads
        else:
            grad_totals = tuple((total + piece for total, piece in zip(grad_totals, weight_grads)))
    d_tokens = jnp.stack(grad_parts)
    scattered = (
        lax.psum_scatter(grad_totals[0], "fsdp", scatter_dimension=0, tiled=True),
        lax.psum_scatter(grad_totals[1], "fsdp", scatter_dimension=0, tiled=True),
        lax.psum_scatter(grad_totals[2], "fsdp", scatter_dimension=0, tiled=True),
        lax.psum_scatter(grad_totals[3], "fsdp", scatter_dimension=0, tiled=True),
        lax.psum_scatter(grad_totals[4], "fsdp", scatter_dimension=0, tiled=True),
    )
    owned = tuple((item[None] for item in scattered))
    scale_sum = lax.psum(scale_total, "fsdp")
    d_query_gain = (scale_sum * jax.nn.sigmoid(query_gain[0]) * scale_factor)[None]
    return (output, d_tokens, owned[0], owned[1], owned[2], owned[3], owned[4], d_query_gain)


def solution(mesh):
    in_specs = (
        P("fsdp", None, None),
        P("fsdp", None, None),
        P("fsdp"),
        P("section", "fsdp", None),
        P("section", "fsdp", None),
        P("section", "fsdp", None),
        P("section", "fsdp", None),
        P("section", "fsdp", None),
        P("section", None),
    )
    out_specs = (
        P("fsdp", None, "section"),
        P("fsdp", None, "section"),
        P("section", "fsdp", None),
        P("section", "fsdp", None),
        P("section", "fsdp", None),
        P("section", "fsdp", None),
        P("section", "fsdp", None),
        P("section", None),
    )
    return jax.shard_map(shards, mesh=mesh, in_specs=in_specs, out_specs=out_specs, check_vma=False)
```

profile of v0, /device:TPU:0, one launch (start us, length us, event | category | flops | bytes accessed | tf_op | source)
XLA Modules:
  0.0 912.7 jit_solution(7341860607706191701)
XLA Ops:
  7.3 2.3 convert_element_type.342
  9.6 1.7 convert_element_type.348
  13.1 27.6 %all_gather.20 = bf16[1,1280,2]{2,0,1:T(2,128)(2,1)S(1)} all-gather(bf16[1,80,2]{2,0,1:T(2,128)(2,1)S(1)} %copy.137), channel_id=1, replica_groups=mesh['section'=2,'fsdp'=16] {'fsdp'}, dimensions={1}, use_global_device_ids=true | all-gather | bytes 5440 | tf_op jit(solution)/shard_map/all_gather | solution.py:182
  47.7 52.0 %all-gather.5.cloned.1.call-done = bf16[1,1280,3840]{2,1,0:T(8,128)(2,1)} async-done(((bf16[1,80,3840]{2,1,0:T(8,128)(2,1)}), bf16[1,1280,3840]{2,1,0:T(8,128)(2,1)}) %all-gather.5.cloned.1.call-update) | async-done | bytes 9830416 | tf_op jit(solution)/shard_map/all_gather | solution.py:178
  99.7 5.3 fusion.241
  112.4 34.2 %all-gather.7.cloned.1.call-done = bf16[1,1280,1280]{2,1,0:T(8,128)(2,1)} async-done(((bf16[1,80,1280]{2,1,0:T(8,128)(2,1)}), bf16[1,1280,1280]{2,1,0:T(8,128)(2,1)}) %all-gather.7.cloned.1.call-update) | async-done | bytes 3276816 | tf_op jit(solution)/shard_map/all_gather | solution.py:179
  146.6 2.8 multiply_reduce_fusion.22
  149.5 44.6 %all-gather.9.cloned.1.call-done = bf16[1,1280,1280]{2,1,0:T(8,128)(2,1)} async-done(((bf16[1,80,1280]{2,1,0:T(8,128)(2,1)}), bf16[1,1280,1280]{2,1,0:T(8,128)(2,1)}) %all-gather.9.cloned.1.call-update) | async-done | bytes 3276816 | tf_op jit(solution)/shard_map/all_gather | solution.py:180
  194.1 2.5 fusion.40
  196.6 44.8 %all-gather.11.cloned.1.call-done = bf16[1,1280,1280]{2,1,0:T(8,128)(2,1)} async-done(((bf16[1,80,1280]{2,1,0:T(8,128)(2,1)}), bf16[1,1280,1280]{2,1,0:T(8,128)(2,1)}) %all-gather.11.cloned.1.call-update) | async-done | bytes 3276816 | tf_op jit(solution)/shard_map/all_gather | solution.py:181
  241.5 2.6 fusion.96
  246.4 7.7 collective-permute-done
  254.4 6.7 fusion.243
  277.8 1.9 fusion.108
  279.8 1.9 copy.151
  283.1 1.6 multiply_reduce_fusion.2
  287.2 7.5 multiply_reduce_fusion.11
  294.8 2.1 add_convert_fusion.2
  297.5 2.8 fusion.245
  301.2 1.9 copy.149
  303.1 1.9 copy.147
  305.0 2.0 slice.87
  306.9 2.2 copy.148
  313.4 1.9 multiply_reduce_fusion.18
  318.2 2.2 fusion.102
  324.0 2.1 fusion.111
  326.1 1.9 copy.155
  329.5 1.6 multiply_reduce_fusion.1
  333.5 7.5 multiply_reduce_fusion.9
  343.9 3.8 convolution_multiply_fusion.8
  347.7 3.1 collective-permute-done.4
  354.7 1.9 fusion.114
  363.7 8.3 multiply_reduce_fusion.7
  376.4 3.8 fusion.1
  381.3 2.6 convolution_multiply_fusion.2
  385.3 5.0 fusion.5
  391.4 2.1 convolution_multiply_fusion.4
  394.6 3.8 fusion.3
  399.5 9.6 %fusion.144 = f32[1280,3840]{1,0:T(8,128)} fusion(bf16[128,1280]{0,1:T(8,128)(2,1)S(1)} %bitcast.396, bf16[128,1280]{0,1:T(8,128)(2,1)} %bitcast.398, bf16[128,1280]{0,1:T(8,128)(2,1)} %bitcast.404, bf16[128,1280]{1,0:T(8,128)(2,1)S(1)} %copy-done.45, pred[]{:T(512)S(6)} %eq.5, f32[128]{0:T(128)S(1)} %add_rsqrt_fusion.5, f32[1280]{0:T(1024)S(1)} %get-tuple-element.25, ...), kind=kOutput, calls=%fused_computation.196 | convolution fusion | flops 1262223360 | bytes 21308928 | tf_op jit(solution)/shard_map/dot_general | solution.py:28
  409.1 8.3 fusion.143
  417.4 22.6 %multiply_add_fusion = f32[1280,3840]{1,0:T(8,128)} fusion(f32[1280,3840]{1,0:T(8,128)} %fusion.143, f32[1280,3840]{1,0:T(8,128)} %fusion.144, f32[]{:T(128)S(6)} %convert_element_type.426, f32[]{:T(128)S(6)} %convert_element_type.425, f32[]{:T(128)S(6)} %convert_element_type.424, bf16[128,1280]{0,1:T(8,128)(2,1)S(1)} %bitcast.392, ...), kind=kOutput, calls=%fused_computation | convolution fusion | flops 1285980160 | bytes 60620812 | tf_op jit(solution)/shard_map/dot_general | solution.py:28
  441.2 3.6 fusion.90
  447.2 5.2 collective-permute-done.2
  457.3 30.5 %psum.7 = f32[80]{0:T(128)S(1)} all-reduce(f32[80]{0:T(128)S(1)} %multiply_add_fusion.1), channel_id=1, replica_groups=mesh['section'=2,'fsdp'=16] {'fsdp'}, use_global_device_ids=true, to_apply=%region_35.36 | all-reduce | flops 80 | bytes 640 | tf_op jit(solution)/shard_map/psum | solution.py:252
  490.6 29.3 %reduce-scatter.10.cloned.1.call-done = f32[80,1280]{1,0:T(8,128)} async-done(((f32[1280,1280]{1,0:T(8,128)}), f32[80,1280]{1,0:T(8,128)}) %reduce-scatter.10.cloned.1.call-update) | async-done | bytes 409616 | tf_op jit(solution)/shard_map/reduce_scatter | solution.py:246
  519.9 90.5 %reduce-scatter.14.cloned.1.call-done = f32[80,1280]{1,0:T(8,128)} async-done(((f32[1280,1280]{1,0:T(8,128)}), f32[80,1280]{1,0:T(8,128)}) %reduce-scatter.14.cloned.1.call-update) | async-done | bytes 409616 | tf_op jit(solution)/shard_map/reduce_scatter | solution.py:248
  610.4 91.0 %reduce-scatter.12.cloned.1.call-done = f32[80,1280]{1,0:T(8,128)} async-done(((f32[1280,1280]{1,0:T(8,128)}), f32[80,1280]{1,0:T(8,128)}) %reduce-scatter.12.cloned.1.call-update) | async-done | bytes 409616 | tf_op jit(solution)/shard_map/reduce_scatter | solution.py:247
  701.4 204.4 %reduce-scatter.8.cloned.1.call-done = f32[80,3840]{1,0:T(8,128)} async-done(((f32[1280,3840]{1,0:T(8,128)}), f32[80,3840]{1,0:T(8,128)}) %reduce-scatter.8.cloned.1.call-update) | async-done | bytes 1228816 | tf_op jit(solution)/shard_map/reduce_scatter | solution.py:245
  (402 shorter events, 89.5 us)
Async XLA Ops:
  7.2 33.9 %copy-start.116 = (s32[2]{0:T(128)S(1)}, s32[2]{0:T(128)}, u32[]{:S(2)}) copy-start(s32[2]{0:T(128)} %param.11) | copy-start | bytes 28
  7.2 39.9 %copy-start.4 = (bf16[2,128,1280]{2,1,0:T(8,128)(2,1)S(1)}, bf16[2,128,1280]{2,1,0:T(8,128)(2,1)}, u32[]{:S(2)}) copy-start(bf16[2,128,1280]{2,1,0:T(8,128)(2,1)} %param.9) | copy-start | bytes 1966084
  7.2 40.0 %copy-start.121 = (f32[1,80]{1,0:T(1,128)S(1)}, f32[1,80]{1,0:T(1,128)}, u32[]{:S(2)}) copy-start(f32[1,80]{1,0:T(1,128)} %param.17) | copy-start | bytes 964
  7.2 92.5 %all-gather.5.cloned.1.call-start = ((), (), s32[]{:S(2)}) async-start(), calls=%async_computation.5 | async-start | bytes 10444800 | tf_op jit(solution)/shard_map/all_gather | solution.py:178
  9.6 137.0 %all-gather.7.cloned.1.call-start = ((), (), s32[]{:S(2)}) async-start(), calls=%async_computation.6 | async-start | bytes 3481600 | tf_op jit(solution)/shard_map/all_gather | solution.py:179
  11.4 182.7 %all-gather.9.cloned.1.call-start = ((), (), s32[]{:S(2)}) async-start(), calls=%async_computation.7 | async-start | bytes 3481600 | tf_op jit(solution)/shard_map/all_gather | solution.py:180
  12.1 229.3 %all-gather.11.cloned.1.call-start = ((), (), s32[]{:S(2)}) async-start(), calls=%async_computation.8 | async-start | bytes 3481600 | tf_op jit(solution)/shard_map/all_gather | solution.py:181
  12.9 475.4 %reduce-scatter.16.cloned.1.call-start = ((), (), s32[]{:S(2)}) async-start(), calls=%async_computation.13 | async-start | bytes 696320
  149.3 94.8 %copy-start.34 = (f32[128,1280]{1,0:T(8,128)}, f32[128,1280]{1,0:T(8,128)S(1)}, u32[]{:S(2)}) copy-start(f32[128,1280]{1,0:T(8,128)S(1)} %get-tuple-element.74) | copy-start | bytes 1966084
  149.5 92.0 %copy-start.55 = (bf16[128,1280]{1,0:T(8,128)(2,1)}, bf16[128,1280]{1,0:T(8,128)(2,1)S(1)}, u32[]{:S(2)}) copy-start(bf16[128,1280]{1,0:T(8,128)(2,1)S(1)} %multiply_convert_fusion.15) | copy-start | bytes 983044
  196.6 57.6 %copy-start.76 = (f32[128,1280]{1,0:T(8,128)}, f32[128,1280]{1,0:T(8,128)S(1)}, u32[]{:S(2)}) copy-start(f32[128,1280]{1,0:T(8,128)S(1)} %fusion.40) | copy-start | bytes 1966084
  244.1 9.9 %collective-permute-start = (bf16[128,1280]{1,0:T(8,128)(2,1)S(1)}, bf16[128,1280]{1,0:T(8,128)(2,1)S(1)}, u32[]{:S(2)}, u32[]{:S(2)}) collective-permute-start(bf16[128,1280]{1,0:T(8,128)(2,1)S(1)} %fusion.96), channel_id=1, source_target_pairs={{0,16},{16,0},{1,17},{17,1},{2,18},{18,2},{3,19},{19,3},{4,20},{20... | collective-permute-start | bytes 983048 | tf_op jit(solution)/shard_map/ppermute | solution.py:18
  272.2 15.0 %collective-permute-start.1 = (bf16[128,1280]{1,0:T(8,128)(2,1)}, bf16[128,1280]{1,0:T(8,128)(2,1)}, u32[]{:S(2)}, u32[]{:S(2)}) collective-permute-start(bf16[128,1280]{1,0:T(8,128)(2,1)} %fusion.93), channel_id=1, source_target_pairs={{0,16},{16,0},{1,17},{17,1},{2,18},{18,2},{3,19},{19,3},{4,20},{20... | collective-permute-start | bytes 983048 | tf_op jit(solution)/shard_map/ppermute | solution.py:18
  285.3 9.5 %copy-start.91 = (bf16[16,80,128]{2,1,0:T(8,128)(2,1)}, bf16[16,80,128]{2,1,0:T(8,128)(2,1)S(1)}, u32[]{:S(2)}) copy-start(bf16[16,80,128]{2,1,0:T(8,128)(2,1)S(1)} %convolution_convert_fusion.4) | copy-start | bytes 983044
  286.0 8.8 copy-start.93
  287.2 7.6 copy-start.98
  287.2 10.3 %slice-start = ((s8[9830400]{0:T(1024)(128)(4,1)}), s8[4194304]{0:T(1024)(128)(4,1)S(1)}, s32[]{:S(2)}) async-start(s8[9830400]{0:T(1024)(128)(4,1)} %bitcast.349), calls=%async_computation.14 | async-start | bytes 8388608
  287.2 7.6 copy-start.29
  287.2 10.3 %slice-start.1 = ((s8[9830400]{0:T(1024)(128)(4,1)}), s8[4194304]{0:T(1024)(128)(4,1)S(1)}, s32[]{:S(2)}) async-start(s8[9830400]{0:T(1024)(128)(4,1)} %bitcast.349), calls=%async_computation.15 | async-start | bytes 8388608
  287.2 10.3 %slice-start.2 = ((s8[9830400]{0:T(1024)(128)(4,1)}), s8[1441792]{0:T(1024)(128)(4,1)S(1)}, s32[]{:S(2)}) async-start(s8[9830400]{0:T(1024)(128)(4,1)} %bitcast.349), calls=%async_computation.16 | async-start | bytes 2883584
  296.9 19.9 %collective-permute-start.3 = (bf16[128,1280]{1,0:T(8,128)(2,1)}, bf16[128,1280]{1,0:T(8,128)(2,1)}, u32[]{:S(2)}, u32[]{:S(2)}) collective-permute-start(bf16[128,1280]{1,0:T(8,128)(2,1)} %get-tuple-element.47), channel_id=1, source_target_pairs={{0,16},{16,0},{1,17},{17,1},{2,18},{18,2},{3,19},{19,3},{4,20},{20... | collective-permute-start | bytes 983048 | tf_op jit(solution)/shard_map/ppermute | solution.py:18
  331.6 9.4 %copy-start.94 = (bf16[16,80,128]{2,1,0:T(8,128)(2,1)}, bf16[16,80,128]{2,1,0:T(8,128)(2,1)S(1)}, u32[]{:S(2)}) copy-start(bf16[16,80,128]{2,1,0:T(8,128)(2,1)S(1)} %convolution_convert_fusion.2) | copy-start | bytes 983044
  332.3 8.7 copy-start.96
  333.5 7.5 copy-start.100
  333.5 7.5 copy-start.32
  333.5 10.4 %copy-start.30 = (f32[128,1280]{1,0:T(8,128)S(1)}, f32[128,1280]{1,0:T(8,128)}, u32[]{:S(2)}) copy-start(f32[128,1280]{1,0:T(8,128)} %copy-done.28) | copy-start | bytes 1966084
  333.5 10.3 %copy-start.107 = (bf16[16,80,128]{2,1,0:T(8,128)(2,1)S(1)}, bf16[16,80,128]{2,1,0:T(8,128)(2,1)}, u32[]{:S(2)}) copy-start(bf16[16,80,128]{2,1,0:T(8,128)(2,1)} %get-tuple-element.52) | copy-start | bytes 983044
  342.3 8.6 collective-permute-start.4
  362.1 9.9 %copy-start.89 = (bf16[16,80,128]{2,1,0:T(8,128)(2,1)}, bf16[16,80,128]{2,1,0:T(8,128)(2,1)S(1)}, u32[]{:S(2)}) copy-start(bf16[16,80,128]{2,1,0:T(8,128)(2,1)S(1)} %convolution_convert_fusion.1) | copy-start | bytes 983044
  363.6 8.4 copy-start.85
  363.6 9.6 %copy-start.27 = (f32[128,1280]{1,0:T(8,128)S(1)}, f32[128,1280]{1,0:T(8,128)}, u32[]{:S(2)}) copy-start(f32[128,1280]{1,0:T(8,128)} %copy-done.26) | copy-start | bytes 1966084
  363.7 9.6 %copy-start.106 = (bf16[16,80,128]{2,1,0:T(8,128)(2,1)S(1)}, bf16[16,80,128]{2,1,0:T(8,128)(2,1)}, u32[]{:S(2)}) copy-start(bf16[16,80,128]{2,1,0:T(8,128)(2,1)} %get-tuple-element.51) | copy-start | bytes 983044
  373.2 146.7 %reduce-scatter.10.cloned.1.call-start = ((), (), s32[]{:S(2)}) async-start(), calls=%async_computation.10 | async-start | bytes 6963200 | tf_op jit(solution)/shard_map/reduce_scatter | solution.py:246
  380.2 230.2 %reduce-scatter.14.cloned.1.call-start = ((), (), s32[]{:S(2)}) async-start(), calls=%async_computation.12 | async-start | bytes 6963200 | tf_op jit(solution)/shard_map/reduce_scatter | solution.py:248
  390.4 311.0 %reduce-scatter.12.cloned.1.call-start = ((), (), s32[]{:S(2)}) async-start(), calls=%async_computation.11 | async-start | bytes 6963200 | tf_op jit(solution)/shard_map/reduce_scatter | solution.py:247
  398.4 10.7 %copy-start.47 = (bf16[128,1280]{1,0:T(8,128)(2,1)S(1)}, bf16[128,1280]{1,0:T(8,128)(2,1)}, u32[]{:S(2)}) copy-start(bf16[128,1280]{1,0:T(8,128)(2,1)} %copy-done.46) | copy-start | bytes 983044
  398.4 507.3 %reduce-scatter.8.cloned.1.call-start = ((), (), s32[]{:S(2)}) async-start(), calls=%async_computation.9 | async-start | bytes 20889600 | tf_op jit(solution)/shard_map/reduce_scatter | solution.py:245
  399.5 9.6 %copy-start.95 = (bf16[16,80,128]{2,1,0:T(8,128)(2,1)S(1)}, bf16[16,80,128]{2,1,0:T(8,128)(2,1)}, u32[]{:S(2)}) copy-start(bf16[16,80,128]{2,1,0:T(8,128)(2,1)} %copy-done.94) | copy-start | bytes 983044
  399.5 9.6 %copy-start.97 = (bf16[16,80,128]{2,1,0:T(8,128)(2,1)S(1)}, bf16[16,80,128]{2,1,0:T(8,128)(2,1)}, u32[]{:S(2)}) copy-start(bf16[16,80,128]{2,1,0:T(8,128)(2,1)} %copy-done.96) | copy-start | bytes 983044
  399.5 9.6 %copy-start.101 = (bf16[128,16,80]{0,2,1:T(8,128)(2,1)S(1)}, bf16[128,16,80]{0,2,1:T(8,128)(2,1)}, u32[]{:S(2)}) copy-start(bf16[128,16,80]{0,2,1:T(8,128)(2,1)} %copy-done.100) | copy-start | bytes 983044
  409.1 8.3 copy-start.86
  409.1 8.3 copy-start.88
  409.1 8.3 copy-start.90
  444.7 43.0 %copy-start.84 = (bf16[128,1280]{1,0:T(8,128)(2,1)S(1)}, bf16[128,1280]{1,0:T(8,128)(2,1)}, u32[]{:S(2)}) copy-start(bf16[128,1280]{1,0:T(8,128)(2,1)} %copy-done.82) | copy-start | bytes 983044
  444.7 43.0 %copy-start.109 = (bf16[128,1280]{1,0:T(8,128)(2,1)S(1)}, bf16[128,1280]{1,0:T(8,128)(2,1)}, u32[]{:S(2)}) copy-start(bf16[128,1280]{1,0:T(8,128)(2,1)} %copy-done.108) | copy-start | bytes 983044
  444.8 43.0 %copy-start.122 = (f32[1,80]{1,0:T(1,128)S(1)}, f32[1,80]{1,0:T(1,128)}, u32[]{:S(2)}) copy-start(f32[1,80]{1,0:T(1,128)} %param.17) | copy-start | bytes 964
  444.8 7.7 collective-permute-start.2
  455.7 34.1 %collective-permute-start.5 = (bf16[128,1280]{1,0:T(8,128)(2,1)S(1)}, bf16[128,1280]{1,0:T(8,128)(2,1)S(1)}, u32[]{:S(2)}, u32[]{:S(2)}) collective-permute-start(bf16[128,1280]{1,0:T(8,128)(2,1)S(1)} %add_convert_fusion), channel_id=1, source_target_pairs={{0,16},{16,0},{1,17},{17,1},{2,18},{18,2},{3,19},{19,3},{4,20},{20... | collective-permute-start | bytes 983048 | tf_op jit(solution)/shard_map/ppermute | solution.py:18
  (95 other events, 257.8 us)
Sparse Core Ops, SparseCore 0:
  10.9 88.7 all-gather.4
  102.6 43.9 all-gather.6
  149.4 44.6 all-gather.8
  196.8 44.6 all-gather.10
  373.3 55.0 reduce-scatter.15
  433.4 86.4 reduce-scatter.9
  524.4 85.9 reduce-scatter.13
  615.4 85.8 reduce-scatter.11
  706.1 199.5 reduce-scatter.7
where the time goes:
time: 923 us; the launch traced here: 913 us
  waiting for transfers between devices  607 us (66%)
  matrix products  155 us (17%)
  blocking collectives  58 us (6%)
  local copies, waits for them, and re-layouts  41.1 us (4%)
  other arithmetic  26.6 us (3%)
  between operations  16.2 us (2%)
    reduce_scatter x1, waiting for transfers between devices, shards(): lax.psum_scatter(grad_totals[0], 'fsdp', scatter_dimension=0, tiled=True)  204 us
    reduce_scatter x1, waiting for transfers between devices, shards(): lax.psum_scatter(grad_totals[2], 'fsdp', scatter_dimension=0, tiled=True)  91 us
    reduce_scatter x1, waiting for transfers between devices, shards(): lax.psum_scatter(grad_totals[3], 'fsdp', scatter_dimension=0, tiled=True)  90.5 us
    dot_general x12, matrix products, contract_rows(): lax.dot_general(left, right, (((0,), (0,)), ((), ())), preferred_element_...  65 us
    all_gather x1, waiting for transfers between devices, gather_weights(): lax.all_gather(qkv_weight.astype(jnp.bfloat16), 'fsdp', axis=1, tiled=True)  52 us
    all_gather x1, waiting for transfers between devices, gather_weights(): lax.all_gather(down_weight.astype(jnp.bfloat16), 'fsdp', axis=1, tiled=True)  44.8 us
    all_gather x1, waiting for transfers between devices, gather_weights(): lax.all_gather(up_weight.astype(jnp.bfloat16), 'fsdp', axis=1, tiled=True)  44.6 us
    dot_general x12, matrix products, contract_cols(): lax.dot_general(left, right, (((1,), (1,)), ((), ())), preferred_element_...  38 us
  transfers between devices with their start and end apart: 15, of which 11 were waited for; matrix products, arithmetic and copies ran while one was open for 15% of the time, Pallas kernels for 0%

commit v1 on v0

--- a/solution.py
+++ b/solution.py
@@ -3,6 +3,8 @@
 import jax
 import jax.numpy as jnp
 from jax import lax
+from jax.experimental import pallas as pl
+from jax.experimental.pallas import tpu as pltpu
 from jax.sharding import PartitionSpec as P
 
 H = 16
@@ -12,6 +14,366 @@
 NORM_EPS = 1e-06
 NEG_FILL = -1e30
 LOG_BASE = 1.442695041
+
+
+MESH_ID = pl.DeviceIdType.MESH
+BF16 = jnp.bfloat16
+F32 = jnp.float32
+NZ = 4
+FIRST = 0
+
+
+def place():
+    s, f = lax.axis_index("section"), lax.axis_index("fsdp")
+    return s, f // 4, (f // 2) % 2, f % 2
+
+
+def device(s, z, x, c):
+    return (s, z * 4 + x * 2 + c)
+
+
+def piece_rows(z, x, c, n):
+    return pl.ds(pl.multiple_of((z * 4 + x * 2 + c) * n, 16), n)
+
+
+def inside(z):
+    return (z >= 0) & (z < NZ)
+
+
+def neighbour_barrier(s, z, x, c):
+    barrier = pltpu.get_barrier_semaphore()
+
+    def tell(target):
+        pl.semaphore_signal(barrier, inc=1, device_id=target, device_id_type=MESH_ID)
+
+    tell(device(s, z, x, 1 - c))
+    tell(device(s, z, 1 - x, c))
+    pl.when(z > 0)(lambda: tell(device(s, z - 1, x, c)))
+    pl.when(z < NZ - 1)(lambda: tell(device(s, z + 1, x, c)))
+    pl.semaphore_wait(barrier, 2 + (z > 0).astype(jnp.int32) + (z < NZ - 1).astype(jnp.int32))
+
+
+def gather_engine(s, z, x, c, n, held, send_sem, recv_sem, core_send, core_recv):
+    sent = []
+
+    def copy(p, zz, xx, target, sem_s, sem_r, cc=c):
+        rows = piece_rows(zz, xx, cc, n)
+        return pltpu.make_async_remote_copy(
+            held.at[p, rows], held.at[p, rows], sem_s, sem_r, device_id=target, device_id_type=MESH_ID
+        )
+
+    def ship(p, zz, xx, way, cond=None):
+        i = zz * 2 + xx
+        target = (
+            device(s, jnp.minimum(z + 1, NZ - 1), x, c),
+            device(s, jnp.maximum(z - 1, 0), x, c),
+            device(s, z, 1 - x, c),
+            device(s, z, x, 1 - c),
+        )[way]
+        if way < 3:
+            cp = copy(p, zz, xx, target, send_sem.at[p, i, way], recv_sem.at[p, i])
+        else:
+            cp = copy(p, zz, xx, target, core_send.at[p, i], core_recv.at[p, i])
+        if cond is None:
+            cp.start()
+        else:
+            pl.when(cond)(cp.start)
+        sent.append((cp, cond))
+
+    def arrived(p, zz, xx):
+        copy(p, zz, xx, device(s, z, 1 - x, c), send_sem.at[p, 0, 0], recv_sem.at[p, zz * 2 + xx]).wait_recv()
+
+    def own(p):
+        for way, cond in ((0, z < NZ - 1), (1, z > 0), (2, None), (3, None)):
+            ship(p, z, x, way, cond)
+
+    def relay(p, cols):
+        for d in range(1, NZ):
+            for sign, way in ((-1, 0), (1, 1)):
+                zz = z + sign * d
+                here = inside(zz)
+                zc = jnp.clip(zz, 0, NZ - 1)
+                for xx in cols:
+                    pl.when(here)(lambda xx=xx: arrived(p, zc, xx))
+                    ship(p, zc, xx, way, here & inside(z - sign))
+                    if len(cols) == 1:
+                        ship(p, zc, xx, 2, here)
+                    ship(p, zc, xx, 3, here)
+
+    def across_first(p):
+        arrived(p, z, 1 - x)
+        ship(p, z, 1 - x, 0, z < NZ - 1)
+        ship(p, z, 1 - x, 1, z > 0)
+        ship(p, z, 1 - x, 3)
+
+    def across(p):
+        for d in range(NZ):
+            for sign in (-1, 1) if d else (1,):
+                zz = z + sign * d
+                here = inside(zz)
+                zc = jnp.clip(zz, 0, NZ - 1)
+                pl.when(here)(lambda: arrived(p, zc, 1 - x))
+                ship(p, zc, 1 - x, 3, here)
+
+    def finish(p):
+        for zz in range(NZ):
+            for xx in range(2):
+                copy(p, zz, xx, device(s, z, x, 1 - c), core_send.at[p, 0], core_recv.at[p, zz * 2 + xx], 1 - c).wait_recv()
+
+    def drain():
+        for cp, cond in sent:
+            if cond is None:
+                cp.wait_send()
+            else:
+                pl.when(cond)(cp.wait_send)
+
+    return own, relay, across_first, across, finish, drain
+
+
+def gather_kernel(n, wq, wo, wu, wd, held, send_sem, recv_sem, core_send, core_recv):
+    s, z, x, c = place()
+    width = wo.shape[-1]
+    mine = piece_rows(z, x, c, n)
+    for k in range(3):
+        held[k, mine] = wq[:, k * width : (k + 1) * width].astype(BF16)
+    for k, ref in enumerate((wo, wu, wd)):
+        held[3 + k, mine] = ref[...].astype(BF16)
+    neighbour_barrier(s, z, x, c)
+    own, relay, across_first, across, finish, drain = gather_engine(
+        s, z, x, c, n, held, send_sem, recv_sem, core_send, core_recv
+    )
+    own(0)
+    for p in range(6):
+        if p + 1 < 6:
+            own(p + 1)
+        if p == FIRST:
+            across_first(p)
+            relay(p, (x, 1 - x))
+        else:
+            relay(p, (x,))
+        if p > 0 and p - 1 != FIRST:
+            across(p - 1)
+    if FIRST != 5:
+        across(5)
+    for p in range(6):
+        finish(p)
+    drain()
+
+
+def gather_pieces(wq, wo, wu, wd):
+    n, width = wo.shape
+    dma = pltpu.SemaphoreType.DMA
+    return pl.pallas_call(
+        lambda *refs: gather_kernel(n, *refs),
+        out_shape=jax.ShapeDtypeStruct((6, n * 16, width), BF16),
+        in_specs=[pl.BlockSpec(memory_space=pltpu.VMEM)] * 4,
+        out_specs=pl.BlockSpec(memory_space=pltpu.VMEM),
+        scratch_shapes=[dma((6, 8, 3)), dma((6, 8)), dma((6, 8)), dma((6, 8))],
+        compiler_params=pltpu.CompilerParams(collective_id=1, has_side_effects=True, vmem_limit_bytes=40 << 20),
+        name="gather_weights",
+    )(wq, wo, wu, wd)
+
+
+def add_block(dst, src):
+    n = dst.shape[0]
+
+    @pl.loop(0, n // 16)
+    def _(k):
+        r = pl.ds(pl.multiple_of(k * 16, 16), 16)
+        dst[r] = (dst[r].astype(F32) + src[r].astype(F32)).astype(BF16)
+
+
+def scatter_engine(s, z, x, c, n, part, got_core, got_x, got_z, got_zz, out_store, sems):
+    core_s, core_r, x_s, x_r, z_s, z_r = sems
+    sent = []
+
+    def begin(cp, cond=None):
+        if cond is None:
+            cp.start()
+        else:
+            pl.when(cond)(cp.start)
+        sent.append((cp, cond))
+
+    def remote(src, dst, a, b, target):
+        return pltpu.make_async_remote_copy(src, dst, a, b, device_id=target, device_id_type=MESH_ID)
+
+    other = device(s, z, x, 1 - c)
+    side = device(s, z, 1 - x, c)
+
+    def core_copy(p, i):
+        rows = piece_rows(i // 2, i % 2, 1 - c, n)
+        return remote(part.at[p, rows], got_core.at[p, i], core_s.at[p, i], core_r.at[p, i], other)
+
+    def core_send(p):
+        for i in range(8):
+            begin(core_copy(p, i))
+
+    def core_add(p):
+        for i in range(8):
+            core_copy(p, i).wait_recv()
+            add_block(part.at[p, piece_rows(i // 2, i % 2, c, n)], got_core.at[p, i])
+
+    def walk(fn):
+        for d in range(NZ - 1, 0, -1):
+            for sign in (1, -1):
+                zz = z + sign * d
+                fn(jnp.clip(zz, 0, NZ - 1), inside(zz), sign)
+
+    def x_copy(p, zz):
+        return remote(
+            part.at[p, piece_rows(zz, 1 - x, c, n)], got_x.at[p, zz], x_s.at[p, zz], x_r.at[p, zz], side
+        )
+
+    def x_send(p):
+        walk(lambda zz, here, sign: begin(x_copy(p, zz), here))
+        begin(x_copy(p, z))
+
+    def x_add(p, zz):
+        x_copy(p, zz).wait_recv()
+        add_block(part.at[p, piece_rows(zz, x, c, n)], got_x.at[p, zz])
+
+    def z_copy(p, zz, xx, sign, slot, buf):
+        target = device(s, jnp.clip(z + sign, 0, NZ - 1), x, c)
+        return remote(
+            part.at[p, piece_rows(zz, xx, c, n)], buf(slot, xx), z_s.at[p, xx, zz], z_r.at[p, xx, slot], target
+        )
+
+    def buffer(p):
+        if p == FIRST:
+            return lambda slot, xx: got_zz.at[xx, slot]
+        return lambda slot, xx: got_z.at[p, slot]
+
+    def slot_there(zz, sign):
+        return jnp.where((sign < 0) & (z + sign == zz), NZ, zz)
+
+    def z_chain(p, cols, before=None):
+        buf = buffer(p)
+
+        def step(zz, here, sign):
+            def go():
+                if before is not None:
+                    before(zz)
+                for xx in cols:
+                    def take(xx=xx):
+                        z_copy(p, zz, xx, sign, zz, buf).wait_recv()
+                        add_block(part.at[p, piece_rows(zz, xx, c, n)], buf(zz, xx))
+
+                    pl.when(inside(z - sign))(take)
+                    z_copy(p, zz, xx, sign, slot_there(zz, sign), buf).start()
+
+            pl.when(here)(go)
+            for xx in cols:
+                sent.append((z_copy(p, zz, xx, sign, slot_there(zz, sign), buf), here))
+
+        walk(step)
+
+    def z_last(p, xx):
+        buf = buffer(p)
+        mine = part.at[p, piece_rows(z, xx, c, n)]
+
+        def take(slot):
+            z_copy(p, z, xx, 1, slot, buf).wait_recv()
+            add_block(mine, buf(slot, xx))
+
+        pl.when(z > 0)(lambda: take(z))
+        pl.when(z < NZ - 1)(lambda: take(NZ))
+
+    def total(p, pieces):
+        @pl.loop(0, n // 16)
+        def _(k):
+            r = pl.ds(pl.multiple_of(k * 16, 16), 16)
+            value = part[p, piece_rows(z, x, c, n)] if False else part.at[p, piece_rows(z, x, c, n)][r].astype(F32)
+            out_store(p, r, value)
+
+    def serve(p):
+        if p == FIRST:
+            z_chain(p, (x, 1 - x))
+            z_last(p, 1 - x)
+            begin(x_copy(p, z))
+            z_last(p, x)
+            x_add(p, z)
+        else:
+            z_chain(p, (x,), before=lambda zz: x_add(p, zz))
+            x_add(p, z)
+            z_last(p, x)
+        total(p, None)
+
+    def drain():
+        for cp, cond in sent:
+            if cond is None:
+                cp.wait_send()
+            else:
+                pl.when(cond)(cp.wait_send)
+
+    return core_send, core_add, x_send, serve, drain
+
+
+def scatter_kernel(n, grads, dq, do, du, dd, part, got_core, got_x, got_z, got_zz, load_sem, *sems):
+    s, z, x, c = place()
+    width = do.shape[-1]
+    loads = [pltpu.make_async_copy(grads.at[p], part.at[p], load_sem.at[p]) for p in range(6)]
+    for ld in loads:
+        ld.start()
+
+    def out_store(p, r, value):
+        if p < 3:
+            dq[r, p * width : (p + 1) * width] = value
+        else:
+            (do, du, dd)[p - 3][r] = value
+
+    neighbour_barrier(s, z, x, c)
+    core_send, core_add, x_send, serve, drain = scatter_engine(
+        s, z, x, c, n, part, got_core, got_x, got_z, got_zz, out_store, sems
+    )
+    order = [FIRST] + [p for p in range(6) if p != FIRST]
+    for k in range(2):
+        loads[order[k]].wait()
+        core_send(order[k])
+    for k, p in enumerate(order):
+        if k + 2 < 6:
+            loads[order[k + 2]].wait()
+            core_send(order[k + 2])
+        core_add(p)
+        if p != FIRST:
+            x_send(p)
+        if k > 0:
+            serve(order[k - 1])
+    serve(order[5])
+    drain()
+
+
+def scatter_pieces(grads):
+    rows, width = grads.shape[1:]
+    n = rows // 16
+    dma = pltpu.SemaphoreType.DMA
+    block = (n, width)
+    return pl.pallas_call(
+        lambda *refs: scatter_kernel(n, *refs),
+        out_shape=(
+            jax.ShapeDtypeStruct((n, 3 * width), F32),
+            jax.ShapeDtypeStruct(block, F32),
+            jax.ShapeDtypeStruct(block, F32),
+            jax.ShapeDtypeStruct(block, F32),
+        ),
+        in_specs=[pl.BlockSpec(memory_space=pl.ANY)],
+        out_specs=(pl.BlockSpec(memory_space=pltpu.VMEM),) * 4,
+        scratch_shapes=[
+            pltpu.VMEM((6, rows, width), BF16),
+            pltpu.VMEM((6, 8) + block, BF16),
+            pltpu.VMEM((6, 4) + block, BF16),
+            pltpu.VMEM((6, 5) + block, BF16),
+            pltpu.VMEM((2, 5) + block, BF16),
+            dma((6,)),
+            dma((6, 8)),
+            dma((6, 8)),
+            dma((6, 4)),
+            dma((6, 4)),
+            dma((6, 2, 4)),
+            dma((6, 2, 5)),
+        ],
+        compiler_params=pltpu.CompilerParams(collective_id=2, has_side_effects=True, vmem_limit_bytes=56 << 20),
+        name="scatter_gradients",
+    )(grads)
 
 
 def swapped(value, axis, bit):
@@ -167,6 +529,7 @@
     norm_gains,
     query_gain,
 ):
+    near = lax.axis_size("fsdp") == 16
     section_index = lax.axis_index("section")
     micro_count, slot_rows, width = tokens.shape
     half_width = width // 2
@@ -186,7 +549,12 @@
     def handoff(value):
         return swapped(value, "section", 0)
 
-    weights = gather_weights()
+    gains = lax.all_gather(norm_gains.astype(jnp.bfloat16), "fsdp", axis=1, tiled=True)[0]
+    if near:
+        held = gather_pieces(qkv_weight[0], out_weight[0], up_weight[0], down_weight[0])
+        weights = (jnp.concatenate([held[0], held[1], held[2]], -1), held[3], held[4], held[5], gains)
+    else:
+        weights = gather_weights()
     received = jnp.zeros((slot_rows, width), jnp.bfloat16)
     kept = []
     result_parts = []
@@ -205,7 +573,6 @@
                 lax.dynamic_slice_in_dim(finished, section_index * half_width, half_width, 1)
             )
     output = jnp.stack(result_parts)
-    weights = gather_weights()
     row_ids = lax.iota(jnp.int32, slot_rows)
     grad_received = jnp.zeros((slot_rows, width), jnp.bfloat16)
     grad_parts = []
@@ -241,7 +608,15 @@
         else:
             grad_totals = tuple((total + piece for total, piece in zip(grad_totals, weight_grads)))
     d_tokens = jnp.stack(grad_parts)
-    scattered = (
+    if near:
+        d_qkv = grad_totals[0]
+        parts = [d_qkv[:, k * width : (k + 1) * width] for k in range(3)] + list(grad_totals[1:4])
+        scattered = scatter_pieces(jnp.stack([item.astype(BF16) for item in parts]))
+        scattered = scattered + (
+            lax.psum_scatter(grad_totals[4], "fsdp", scatter_dimension=0, tiled=True),
+        )
+    else:
+        scattered = (
         lax.psum_scatter(grad_totals[0], "fsdp", scatter_dimension=0, tiled=True),
         lax.psum_scatter(grad_totals[1], "fsdp", scatter_dimension=0, tiled=True),
         lax.psum_scatter(grad_totals[2], "fsdp", scatter_dimension=0, tiled=True),

time: 923 us -> 591 us (0.64)
  waiting for transfers between devices: 607 us -> 13.1 us
  Pallas kernels: 0 us -> 260 us
  local copies, waits for them, and re-layouts: 41.1 us -> 53.8 us
  matrix products: 155 us -> 165 us
    reduce_scatter x4 -> x0, waiting for transfers between devices: 415 us -> none  [the longest x1 204 us: shards(): lax.psum_scatter(grad_totals[0], 'fsdp', scatter_dimension=0, tiled=True)]
    pallas_call x0 -> x2, Pallas kernels: none -> 260 us  [the longest x1 132 us: gather_pieces(): pl.pallas_call(lambda *refs: gather_kernel(n, *refs), out_shape=jax.Shape...]
    all_gather x4 -> x0, waiting for transfers between devices: 176 us -> none  [the longest x1 52 us: gather_weights(): lax.all_gather(qkv_weight.astype(jnp.bfloat16), 'fsdp', axis=1, tiled=True)]
    unnamed x258 -> x235, local copies, waits for them, and re-layouts: 17.9 us -> 27.7 us
  transfers between devices with their start and end apart: 15 -> 7, of which waited for: 11 -> 3; matrix products, arithmetic and copies ran while one was open for 15% -> 17% of each run, Pallas kernels for 0% -> 22%
where the time goes in v1:
time: 591 us; the launch traced here: 583 us
  Pallas kernels  260 us (44%)
  matrix products  165 us (28%)
  local copies, waits for them, and re-layouts  53.8 us (9%)
  blocking collectives  50 us (8%)
  other arithmetic  17.4 us (3%)
  between operations  16.5 us (3%)
  waiting for transfers between devices  13.1 us (2%)
  starting transfers between devices  6.74 us (1%)
    pallas_call x1, Pallas kernels, gather_pieces(): pl.pallas_call(lambda *refs: gather_kernel(n, *refs), out_shape=jax.Shape...  132 us
    pallas_call x1, Pallas kernels, scatter_pieces(): pl.pallas_call(lambda *refs: scatter_kernel(n, *refs), out_shape=(jax.Sha...  128 us
    dot_general x12, matrix products, contract_rows(): lax.dot_general(left, right, (((0,), (0,)), ((), ())), preferred_element_...  71.1 us
    dot_general x12, matrix products, contract_cols(): lax.dot_general(left, right, (((1,), (1,)), ((), ())), preferred_element_...  31.6 us
    psum x1, blocking collectives, shards(): scale_sum = lax.psum(scale_total, 'fsdp')  29.5 us
    unnamed x235, local copies, waits for them, and re-layouts  27.7 us
    all_gather x1, blocking collectives, shards(): lax.all_gather(norm_gains.astype(jnp.bfloat16), 'fsdp', axis=1, tiled=True)  20.5 us
    dot_general x3, matrix products, layer_forward(): proj = jnp.dot(normed, qkv_w, preferred_element_type=jnp.float32)  15.6 us
  transfers between devices with their start and end apart: 7, of which 3 were waited for; matrix products, arithmetic and copies ran while one was open for 17% of the time, Pallas kernels for 22%

profile of v1, /device:TPU:0, one launch (start us, length us, event | category | flops | bytes accessed | tf_op | source)
XLA Modules:
  0.0 582.6 jit_solution(3760129320024217827)
XLA Ops:
  11.5 132.4 %gather_weights.1 = bf16[6,1280,1280]{2,1,0:T(8,128)(2,1)} custom-call(f32[80,3840]{1,0:T(8,128)S(1)} %bitcast.356, f32[80,1280]{1,0:T(8,128)S(1)} %bitcast.357, f32[80,1280]{1,0:T(8,128)S(1)} %bitcast.358, f32[80,1280]{1,0:T(8,128)S(1)} %bitcast.359), custom_call_target="tpu_custom_call" | custom-call | tf_op jit(solution)/shard_map/gather_weights/pallas_call | solution.py:166
  144.0 7.1 %slice_bitcast_fusion.5 = (bf16[1280,1280]{1,0:T(8,128)(2,1)}, bf16[1280,1280]{1,0:T(8,128)(2,1)}, bf16[1280,1280]{1,0:T(8,128)(2,1)}) fusion(bf16[6,1280,1280]{2,1,0:T(8,128)(2,1)} %gather_weights.1), kind=kLoop, calls=%fused_computation.70 | loop fusion | bytes 19660800 | tf_op jit(solution)/shard_map/squeeze | solution.py:555
  151.2 20.5 %all_gather.3 = bf16[1,1280,2]{2,0,1:T(2,128)(2,1)S(1)} all-gather(bf16[1,80,2]{2,0,1:T(2,128)(2,1)S(1)} %copy.137), channel_id=1, replica_groups=mesh['section'=2,'fsdp'=16] {'fsdp'}, dimensions={1}, use_global_device_ids=true | all-gather | bytes 5440 | tf_op jit(solution)/shard_map/all_gather | solution.py:552
  172.3 6.3 %fusion.256 = (bf16[128,3840]{1,0:T(8,128)(2,1)S(1)}, f32[128,3840]{1,0:T(8,128)}) fusion(bf16[1280,1280]{1,0:T(8,128)(2,1)} %get-tuple-element.50, bf16[1280,1280]{1,0:T(8,128)(2,1)} %get-tuple-element.51, bf16[1280,1280]{1,0:T(8,128)(2,1)} %get-tuple-element.49, f32[1280]{0:T(1024)S(1)} %get-tuple-element.33, f32[128]{0:T(128)S(1)} %add_rsqrt_fusion.5, ...), kind=kOutput, calls=%fused_computation.372 | convolution fusion | flops 1289093120 | bytes 13115905 | tf_op jit(solution)/shard_map/dot_general | solution.py:412
  183.0 2.8 multiply_reduce_fusion.22
  186.0 2.7 fusion.40
  189.6 2.6 fusion.96
  199.5 2.7 collective-permute-done
  202.6 6.5 %fusion.258 = (bf16[128,3840]{1,0:T(8,128)(2,1)S(1)}, f32[128,3840]{1,0:T(8,128)}) fusion(bf16[128,1280]{1,0:T(8,128)(2,1)S(1)} %multiply_convert_fusion.13, bf16[1280,1280]{1,0:T(8,128)(2,1)} %get-tuple-element.50, bf16[1280,1280]{1,0:T(8,128)(2,1)} %get-tuple-element.51, bf16[1280,1280]{1,0:T(8,128)(2,1)} %get-tuple-element.49), kind=kOutput, calls=%fused_computation.374 | convolution fusion | flops 1288273920 | bytes 13107200 | tf_op jit(solution)/shard_map/dot_general | solution.py:412
  210.8 2.0 slice.123
  218.0 2.8 multiply_reduce_fusion.20
  221.0 3.0 fusion.38
  223.9 3.6 fusion.93
  227.5 3.2 fusion.99
  230.7 3.4 multiply_reduce_fusion.10
  234.4 3.4 fusion.108
  245.5 8.7 %fusion.164 = f32[1280,3840]{1,0:T(8,128)} fusion(bf16[128,1280]{0,1:T(8,128)(2,1)S(1)} %bitcast.410, bf16[128,1280]{0,1:T(8,128)(2,1)S(1)} %bitcast.412, bf16[128,1280]{0,1:T(8,128)(2,1)S(1)} %bitcast.418, bf16[128,1280]{1,0:T(8,128)(2,1)S(1)} %copy-done.29, pred[]{:T(512)S(6)} %eq.5, f32[1280]{0:T(1024)S(1)} %get-tuple-element.33, ...), kind=kOutput, calls=%fused_computation.222 | convolution fusion | flops 1262223360 | bytes 21308928 | tf_op jit(solution)/shard_map/dot_general | solution.py:390
  254.3 4.7 convolution_multiply_fusion.2
  259.0 1.6 copy-done.54
  260.6 3.6 multiply_reduce_fusion.11
  265.9 2.8 fusion.260
  270.3 2.0 slice.126
  275.6 2.5 broadcast_select_fusion.1
  278.1 2.8 multiply_reduce_fusion.18
  281.1 2.8 fusion.36
  284.0 3.6 fusion.90
  289.7 3.7 convolution_multiply_fusion.8
  293.5 10.2 %collective-permute-done.3 = bf16[128,1280]{1,0:T(8,128)(2,1)S(1)} collective-permute-done((bf16[128,1280]{1,0:T(8,128)(2,1)S(1)}, bf16[128,1280]{1,0:T(8,128)(2,1)S(1)}, u32[]{:S(2)}, u32[]{:S(2)}) %collective-permute-start.3) | collective-permute-done | bytes 327712 | tf_op jit(solution)/shard_map/ppermute | solution.py:380
  315.0 8.3 %fusion.162 = f32[1280,3840]{1,0:T(8,128)} fusion(bf16[128,1280]{0,1:T(8,128)(2,1)S(1)} %bitcast.414, bf16[128,1280]{0,1:T(8,128)(2,1)S(1)} %bitcast.416, bf16[128,1280]{0,1:T(8,128)(2,1)S(1)} %bitcast.420, bf16[128,1280]{1,0:T(8,128)(2,1)S(1)} %copy-done.32, pred[]{:T(512)S(6)} %eq.5, f32[1280]{0:T(1024)S(1)} %get-tuple-element.33, ...), kind=kOutput, calls=%fused_computation.220 | convolution fusion | flops 1262223360 | bytes 21308928 | tf_op jit(solution)/shard_map/dot_general | solution.py:390
  323.4 6.2 %multiply_reduce_fusion.9 = (f32[1280]{0:T(1024)S(1)}, f32[128]{0:T(128)S(1)}, f32[128,1280]{1,0:T(8,128)S(1)}) fusion(f32[128]{0:T(128)S(1)} %copy-done.93, bf16[128,1280]{1,0:T(8,128)(2,1)S(1)} %copy-done.49, bf16[2,128,1280]{2,1,0:T(8,128)(2,1)S(1)} %copy-done.5, pred[]{:T(512)S(6)} %eq.5, f32[1280]{0:T(1024)S(1)} %get-tuple-element.33, ...), kind=kOutput, calls=%fused_computation.179 | convolution fusion | flops 1292696192 | bytes 12464128 | tf_op jit(solution)/shard_map/dot_general | solution.py:396
  332.9 4.9 convolution_multiply_fusion.4
  341.9 1.9 fusion.114
  343.8 1.9 copy.159
  347.7 1.7 convolution_convert_fusion
  351.6 3.5 multiply_reduce_fusion.7
  357.2 3.7 convolution_multiply_fusion.3
  360.9 15.2 %add_convert_fusion = bf16[1280,3840]{1,0:T(8,128)(2,1)S(1)} fusion(f32[1280,3840]{1,0:T(8,128)} %fusion.162, f32[1280,3840]{1,0:T(8,128)} %fusion.164, f32[]{:T(128)S(6)} %convert_element_type.409, f32[]{:T(128)S(6)} %convert_element_type.408, f32[]{:T(128)S(6)} %convert_element_type.407, bf16[128,1280]{0,1:T(8,128)(2,1)S(1)} %bitcast.407, ...), kind=kOutput, calls=%fused_computation | convolution fusion | flops 1290895360 | bytes 50790412 | tf_op jit(solution)/shard_map/dot_general | solution.py:390
  376.9 6.6 %copy-done.4 = bf16[6,1280,1280]{2,1,0:T(8,128)(2,1)} copy-done((bf16[6,1280,1280]{2,1,0:T(8,128)(2,1)}, bf16[6,1280,1280]{2,1,0:T(8,128)(2,1)S(1)}, u32[]{:S(2)}) %copy-start.4) | copy-done | bytes 19660824
  383.5 3.8 convolution_multiply_fusion.6
  388.4 29.5 %psum.7 = f32[80]{0:T(128)S(1)} all-reduce(f32[80]{0:T(128)S(1)} %multiply_add_fusion), channel_id=1, replica_groups=mesh['section'=2,'fsdp'=16] {'fsdp'}, use_global_device_ids=true, to_apply=%region_31.32 | all-reduce | flops 80 | bytes 640 | tf_op jit(solution)/shard_map/psum | solution.py:627
  418.0 7.6 %fusion.10 = bf16[6,1280,1280]{2,1,0:T(8,128)(2,1)} fusion(bf16[6,1280,1280]{2,1,0:T(8,128)(2,1)} %copy-done.4, f32[1280,1280]{1,0:T(8,128)} %convolution_multiply_fusion.6, f32[1280,1280]{1,0:T(8,128)} %convolution_multiply_fusion.8, bf16[128,1280]{0,1:T(8,128)(2,1)S(1)} %bitcast.428, f32[]{:T(128)S(6)} %convert_element_type.408, f32[128,1280]{1,0:T(8,128)S(1)} %copy-done.8), kind=kOutput, calls=%fused_computation.21 | convolution fusion | flops 426147840 | bytes 17367044 | tf_op jit(solution)/shard_map/dot_general | solution.py:390
  425.7 5.8 %fusion.12 = bf16[6,1280,1280]{2,1,0:T(8,128)(2,1)} fusion(bf16[6,1280,1280]{2,1,0:T(8,128)(2,1)} %fusion.10, f32[1280,1280]{1,0:T(8,128)} %convolution_multiply_fusion.3, f32[1280,1280]{1,0:T(8,128)S(1)} %bitcast.365, bf16[128,1280]{1,0:T(8,128)(2,1)S(1)} %copy-done.73, f32[]{:T(128)S(6)} %convert_element_type.407, bf16[128,1280]{1,0:T(8,128)(2,1)S(1)} %copy-done.35, ...), kind=kOutput, calls=%fused_computation.23 | convolution fusion | flops 426147840 | bytes 17367044 | tf_op jit(solution)/shard_map/dot_general | solution.py:390
  433.1 3.1 fusion.14.refs_0_
  436.7 127.7 %scatter_gradients.1 = (f32[80,3840]{1,0:T(8,128)}, f32[80,1280]{1,0:T(8,128)}, f32[80,1280]{1,0:T(8,128)}, f32[80,1280]{1,0:T(8,128)}) custom-call(bf16[6,1280,1280]{2,1,0:T(8,128)(2,1)} %fusion.14.refs_0_), custom_call_target="tpu_custom_call" | custom-call | tf_op jit(solution)/shard_map/scatter_gradients/pallas_call | solution.py:350
  567.7 2.4 copy.186
  570.1 1.8 copy.187
  571.9 1.8 copy.188
  573.6 1.8 copy.189
  (356 shorter events, 73.0 us)
Async XLA Ops:
  7.2 557.3 %reduce-scatter.4.cloned.1.call-start = ((), (), s32[]{:S(2)}) async-start(), calls=%async_computation.1 | async-start | bytes 696320
  144.0 28.2 %copy-start.5 = (bf16[2,128,1280]{2,1,0:T(8,128)(2,1)S(1)}, bf16[2,128,1280]{2,1,0:T(8,128)(2,1)}, u32[]{:S(2)}) copy-start(bf16[2,128,1280]{2,1,0:T(8,128)(2,1)} %param.9) | copy-start | bytes 1966084
  172.3 8.0 %copy-start.95 = (f32[1,80]{1,0:T(1,128)S(1)}, f32[1,80]{1,0:T(1,128)}, u32[]{:S(2)}) copy-start(f32[1,80]{1,0:T(1,128)} %param.17) | copy-start | bytes 964
  172.3 8.3 %copy-start.89 = (s32[2]{0:T(128)S(1)}, s32[2]{0:T(128)}, u32[]{:S(2)}) copy-start(s32[2]{0:T(128)} %param.11) | copy-start | bytes 28
  185.8 44.9 %copy-start.20 = (f32[128,1280]{1,0:T(8,128)}, f32[128,1280]{1,0:T(8,128)S(1)}, u32[]{:S(2)}) copy-start(f32[128,1280]{1,0:T(8,128)S(1)} %get-tuple-element.85) | copy-start | bytes 1966084
  186.0 16.4 %copy-start.33 = (bf16[128,1280]{1,0:T(8,128)(2,1)}, bf16[128,1280]{1,0:T(8,128)(2,1)S(1)}, u32[]{:S(2)}) copy-start(bf16[128,1280]{1,0:T(8,128)(2,1)S(1)} %multiply_convert_fusion.15) | copy-start | bytes 983044
  192.2 10.0 %collective-permute-start = (bf16[128,1280]{1,0:T(8,128)(2,1)S(1)}, bf16[128,1280]{1,0:T(8,128)(2,1)S(1)}, u32[]{:S(2)}, u32[]{:S(2)}) collective-permute-start(bf16[128,1280]{1,0:T(8,128)(2,1)S(1)} %fusion.96), channel_id=1, source_target_pairs={{0,16},{16,0},{1,17},{17,1},{2,18},{18,2},{3,19},{19,3},{4,20},{20... | collective-permute-start | bytes 983048 | tf_op jit(solution)/shard_map/ppermute | solution.py:380
  202.2 62.5 %copy-start.26 = (bf16[128,1280]{1,0:T(8,128)(2,1)}, bf16[128,1280]{1,0:T(8,128)(2,1)S(1)}, u32[]{:S(2)}) copy-start(bf16[128,1280]{1,0:T(8,128)(2,1)S(1)} %collective-permute-done) | copy-start | bytes 983044
  220.8 9.9 %copy-start.22 = (f32[128,1280]{1,0:T(8,128)}, f32[128,1280]{1,0:T(8,128)S(1)}, u32[]{:S(2)}) copy-start(f32[128,1280]{1,0:T(8,128)S(1)} %get-tuple-element.91) | copy-start | bytes 1966084
  220.9 9.7 %copy-start.36 = (bf16[128,1280]{1,0:T(8,128)(2,1)}, bf16[128,1280]{1,0:T(8,128)(2,1)S(1)}, u32[]{:S(2)}) copy-start(bf16[128,1280]{1,0:T(8,128)(2,1)S(1)} %multiply_convert_fusion.11) | copy-start | bytes 983044
  234.4 30.3 %copy-start.9 = (f32[128,1280]{1,0:T(8,128)}, f32[128,1280]{1,0:T(8,128)S(1)}, u32[]{:S(2)}) copy-start(f32[128,1280]{1,0:T(8,128)S(1)} %fusion.147) | copy-start | bytes 1966084
  243.9 15.0 %collective-permute-start.1 = (bf16[128,1280]{1,0:T(8,128)(2,1)S(1)}, bf16[128,1280]{1,0:T(8,128)(2,1)S(1)}, u32[]{:S(2)}, u32[]{:S(2)}) collective-permute-start(bf16[128,1280]{1,0:T(8,128)(2,1)S(1)} %copy-done.87), channel_id=1, source_target_pairs={{0,16},{16,0},{1,17},{17,1},{2,18},{18,2},{3,19},{19,3},{4,20},{20... | collective-permute-start | bytes 983048 | tf_op jit(solution)/shard_map/ppermute | solution.py:380
  245.5 8.7 %copy-start.43 = (bf16[2,128,1280]{2,1,0:T(8,128)(2,1)S(1)}, bf16[2,128,1280]{2,1,0:T(8,128)(2,1)}, u32[]{:S(2)}) copy-start(bf16[2,128,1280]{2,1,0:T(8,128)(2,1)} %param.10) | copy-start | bytes 1966084
  245.5 8.7 %copy-start.63 = (f32[128,1280]{1,0:T(8,128)S(1)}, f32[128,1280]{1,0:T(8,128)}, u32[]{:S(2)}) copy-start(f32[128,1280]{1,0:T(8,128)} %copy-done.62) | copy-start | bytes 1966084
  245.5 8.7 %copy-start.82 = (f32[128,1280]{1,0:T(8,128)S(1)}, f32[128,1280]{1,0:T(8,128)}, u32[]{:S(2)}) copy-start(f32[128,1280]{1,0:T(8,128)} %copy-done.80) | copy-start | bytes 1966084
  273.6 7.3 %copy-start.18 = (f32[128,1280]{0,1:T(8,128)}, f32[128,1280]{0,1:T(8,128)S(1)}, u32[]{:S(2)}) copy-start(f32[128,1280]{0,1:T(8,128)S(1)} %copy.148) | copy-start | bytes 1966084
  275.6 28.1 %slice-start = ((s8[19660800]{0:T(1024)(128)(4,1)}), s8[4194304]{0:T(1024)(128)(4,1)S(1)}, s32[]{:S(2)}) async-start(s8[19660800]{0:T(1024)(128)(4,1)} %bitcast.360), calls=%async_computation.2 | async-start | bytes 8388608
  278.1 25.6 %slice-start.1 = ((s8[19660800]{0:T(1024)(128)(4,1)}), s8[4194304]{0:T(1024)(128)(4,1)S(1)}, s32[]{:S(2)}) async-start(s8[19660800]{0:T(1024)(128)(4,1)} %bitcast.360), calls=%async_computation.3 | async-start | bytes 8388608
  280.9 24.1 %copy-start.24 = (f32[128,1280]{1,0:T(8,128)}, f32[128,1280]{1,0:T(8,128)S(1)}, u32[]{:S(2)}) copy-start(f32[128,1280]{1,0:T(8,128)S(1)} %get-tuple-element.103) | copy-start | bytes 1966084
  281.0 8.6 %copy-start.88 = (bf16[128,1280]{1,0:T(8,128)(2,1)S(1)}, bf16[128,1280]{1,0:T(8,128)(2,1)}, u32[]{:S(2)}) copy-start(bf16[128,1280]{1,0:T(8,128)(2,1)} %fusion.93) | copy-start | bytes 983044
  281.1 8.6 %copy-start.10 = (f32[128,1280]{1,0:T(8,128)S(1)}, f32[128,1280]{1,0:T(8,128)}, u32[]{:S(2)}) copy-start(f32[128,1280]{1,0:T(8,128)} %copy-done.9) | copy-start | bytes 1966084
  281.1 22.6 %slice-start.2 = ((s8[19660800]{0:T(1024)(128)(4,1)}), s8[4194304]{0:T(1024)(128)(4,1)S(1)}, s32[]{:S(2)}) async-start(s8[19660800]{0:T(1024)(128)(4,1)} %bitcast.360), calls=%async_computation.4 | async-start | bytes 8388608
  284.0 19.7 %copy-start.39 = (f32[128,1280]{1,0:T(8,128)}, f32[128,1280]{1,0:T(8,128)S(1)}, u32[]{:S(2)}) copy-start(f32[128,1280]{1,0:T(8,128)S(1)} %fusion.36) | copy-start | bytes 1966084
  284.0 19.8 %slice-start.3 = ((s8[19660800]{0:T(1024)(128)(4,1)}), s8[4194304]{0:T(1024)(128)(4,1)S(1)}, s32[]{:S(2)}) async-start(s8[19660800]{0:T(1024)(128)(4,1)} %bitcast.360), calls=%async_computation.5 | async-start | bytes 8388608
  287.6 42.9 %collective-permute-start.2 = (bf16[128,1280]{1,0:T(8,128)(2,1)}, bf16[128,1280]{1,0:T(8,128)(2,1)}, u32[]{:S(2)}, u32[]{:S(2)}) collective-permute-start(bf16[128,1280]{1,0:T(8,128)(2,1)} %fusion.90), channel_id=1, source_target_pairs={{0,16},{16,0},{1,17},{17,1},{2,18},{18,2},{3,19},{19,3},{4,20},{20... | collective-permute-start | bytes 983048 | tf_op jit(solution)/shard_map/ppermute | solution.py:380
  288.1 15.6 %collective-permute-start.3 = (bf16[128,1280]{1,0:T(8,128)(2,1)S(1)}, bf16[128,1280]{1,0:T(8,128)(2,1)S(1)}, u32[]{:S(2)}, u32[]{:S(2)}) collective-permute-start(bf16[128,1280]{1,0:T(8,128)(2,1)S(1)} %copy-done.85), channel_id=1, source_target_pairs={{0,16},{16,0},{1,17},{17,1},{2,18},{18,2},{3,19},{19,3},{4,20},{20... | collective-permute-start | bytes 983048 | tf_op jit(solution)/shard_map/ppermute | solution.py:380
  289.7 14.1 %copy-start.44 = (bf16[2,128,1280]{2,1,0:T(8,128)(2,1)S(1)}, bf16[2,128,1280]{2,1,0:T(8,128)(2,1)}, u32[]{:S(2)}) copy-start(bf16[2,128,1280]{2,1,0:T(8,128)(2,1)} %param.10) | copy-start | bytes 1966084
  289.7 14.1 %copy-start.83 = (f32[128,1280]{1,0:T(8,128)S(1)}, f32[128,1280]{1,0:T(8,128)}, u32[]{:S(2)}) copy-start(f32[128,1280]{1,0:T(8,128)} %copy-done.80) | copy-start | bytes 1966084
  289.7 14.0 %slice-start.4 = ((s8[19660800]{0:T(1024)(128)(4,1)}), s8[2883584]{0:T(1024)(128)(4,1)S(1)}, s32[]{:S(2)}) async-start(s8[19660800]{0:T(1024)(128)(4,1)} %bitcast.360), calls=%async_computation.6 | async-start | bytes 5767168
  293.5 11.6 %copy-start.21 = (f32[128,1280]{1,0:T(8,128)S(1)}, f32[128,1280]{1,0:T(8,128)}, u32[]{:S(2)}) copy-start(f32[128,1280]{1,0:T(8,128)} %copy-done.20) | copy-start | bytes 1966084
  315.0 8.3 %copy-start.49 = (bf16[128,1280]{1,0:T(8,128)(2,1)S(1)}, bf16[128,1280]{1,0:T(8,128)(2,1)}, u32[]{:S(2)}) copy-start(bf16[128,1280]{1,0:T(8,128)(2,1)} %copy-done.47) | copy-start | bytes 983044
  315.0 8.3 %copy-start.93 = (f32[128]{0:T(128)S(1)}, f32[128]{0:T(128)}, u32[]{:S(2)}) copy-start(f32[128]{0:T(128)} %get-tuple-element.67) | copy-start | bytes 1540
  323.3 9.5 %copy-start.34 = (bf16[128,1280]{1,0:T(8,128)(2,1)S(1)}, bf16[128,1280]{1,0:T(8,128)(2,1)}, u32[]{:S(2)}) copy-start(bf16[128,1280]{1,0:T(8,128)(2,1)} %copy-done.33) | copy-start | bytes 983044
  323.3 14.6 %slice-start.5 = ((s8[19660800]{0:T(1024)(128)(4,1)}), s8[4194304]{0:T(1024)(128)(4,1)S(1)}, s32[]{:S(2)}) async-start(s8[19660800]{0:T(1024)(128)(4,1)} %bitcast.362), calls=%async_computation.7 | async-start | bytes 8388608
  323.3 14.6 %slice-start.6 = ((s8[19660800]{0:T(1024)(128)(4,1)}), s8[4194304]{0:T(1024)(128)(4,1)S(1)}, s32[]{:S(2)}) async-start(s8[19660800]{0:T(1024)(128)(4,1)} %bitcast.362), calls=%async_computation.8 | async-start | bytes 8388608
  323.4 14.6 %slice-start.7 = ((s8[19660800]{0:T(1024)(128)(4,1)}), s8[4194304]{0:T(1024)(128)(4,1)S(1)}, s32[]{:S(2)}) async-start(s8[19660800]{0:T(1024)(128)(4,1)} %bitcast.362), calls=%async_computation.9 | async-start | bytes 8388608
  323.4 14.6 %slice-start.8 = ((s8[19660800]{0:T(1024)(128)(4,1)}), s8[2883584]{0:T(1024)(128)(4,1)S(1)}, s32[]{:S(2)}) async-start(s8[19660800]{0:T(1024)(128)(4,1)} %bitcast.362), calls=%async_computation.10 | async-start | bytes 5767168
  329.9 7.9 %copy-start.78 = (bf16[128,1280]{1,0:T(8,128)(2,1)}, bf16[128,1280]{1,0:T(8,128)(2,1)S(1)}, u32[]{:S(2)}) copy-start(bf16[128,1280]{1,0:T(8,128)(2,1)S(1)} %add_convert_fusion.2) | copy-start | bytes 983044
  329.9 8.0 %collective-permute-start.4 = (bf16[128,1280]{1,0:T(8,128)(2,1)S(1)}, bf16[128,1280]{1,0:T(8,128)(2,1)S(1)}, u32[]{:S(2)}, u32[]{:S(2)}) collective-permute-start(bf16[128,1280]{1,0:T(8,128)(2,1)S(1)} %add_convert_fusion.2), channel_id=1, source_target_pairs={{0,16},{16,0},{1,17},{17,1},{2,18},{18,2},{3,19},{19,3},{4,20},{20... | collective-permute-start | bytes 983048 | tf_op jit(solution)/shard_map/ppermute | solution.py:380
  356.2 209.7 %collective-permute-start.5 = (bf16[128,1280]{1,0:T(8,128)(2,1)}, bf16[128,1280]{1,0:T(8,128)(2,1)}, u32[]{:S(2)}, u32[]{:S(2)}) collective-permute-start(bf16[128,1280]{1,0:T(8,128)(2,1)} %add_convert_fusion.1), channel_id=1, source_target_pairs={{0,16},{16,0},{1,17},{17,1},{2,18},{18,2},{3,19},{19,3},{4,20},{20... | collective-permute-start | bytes 983048 | tf_op jit(solution)/shard_map/ppermute | solution.py:380
  383.4 34.5 %copy-start.8 = (f32[128,1280]{1,0:T(8,128)S(1)}, f32[128,1280]{1,0:T(8,128)}, u32[]{:S(2)}) copy-start(f32[128,1280]{1,0:T(8,128)} %copy-done.6) | copy-start | bytes 1966084
  383.4 34.5 %copy-start.86 = (bf16[16,80,128]{2,1,0:T(8,128)(2,1)S(1)}, bf16[16,80,128]{2,1,0:T(8,128)(2,1)}, u32[]{:S(2)}) copy-start(bf16[16,80,128]{2,1,0:T(8,128)(2,1)} %get-tuple-element.61) | copy-start | bytes 983044
  383.4 42.2 %slice-start.10 = ((s8[6553600]{0:T(1024)(128)(4,1)}), s8[2359296]{0:T(1024)(128)(4,1)S(1)}, s32[]{:S(2)}) async-start(s8[6553600]{0:T(1024)(128)(4,1)} %bitcast.364), calls=%async_computation.12 | async-start | bytes 4718592
  417.9 7.7 %slice-start.11 = ((s8[6553600]{0:T(1024)(128)(4,1)}), s8[4194304]{0:T(1024)(128)(4,1)S(1)}, s32[]{:S(2)}) async-start(s8[6553600]{0:T(1024)(128)(4,1)} %bitcast.364), calls=%async_computation.13 | async-start | bytes 8388608
  417.9 7.7 %copy-start.35 = (bf16[128,1280]{1,0:T(8,128)(2,1)S(1)}, bf16[128,1280]{1,0:T(8,128)(2,1)}, u32[]{:S(2)}) copy-start(bf16[128,1280]{1,0:T(8,128)(2,1)} %copy-done.33) | copy-start | bytes 983044
  418.0 7.7 %copy-start.38 = (bf16[128,1280]{1,0:T(8,128)(2,1)S(1)}, bf16[128,1280]{1,0:T(8,128)(2,1)}, u32[]{:S(2)}) copy-start(bf16[128,1280]{1,0:T(8,128)(2,1)} %copy-done.36) | copy-start | bytes 983044
  418.0 7.7 %copy-start.73 = (bf16[128,1280]{1,0:T(8,128)(2,1)S(1)}, bf16[128,1280]{1,0:T(8,128)(2,1)}, u32[]{:S(2)}) copy-start(bf16[128,1280]{1,0:T(8,128)(2,1)} %copy-done.72) | copy-start | bytes 983044
  418.0 15.0 %slice-start.12 = ((s8[6553600]{0:T(1024)(128)(4,1)}), s8[4194304]{0:T(1024)(128)(4,1)S(1)}, s32[]{:S(2)}) async-start(s8[6553600]{0:T(1024)(128)(4,1)} %bitcast.381), calls=%async_computation.14 | async-start | bytes 8388608
  (72 other events, 312.3 us)
Sparse Core Ops, SparseCore 0:
  388.5 52.9 reduce-scatter.3

commit v2 on v0

--- a/solution.py
+++ b/solution.py
@@ -3,6 +3,8 @@
 import jax
 import jax.numpy as jnp
 from jax import lax
+from jax.experimental import pallas as pl
+from jax.experimental.pallas import tpu as pltpu
 from jax.sharding import PartitionSpec as P
 
 H = 16
@@ -12,6 +14,786 @@
 NORM_EPS = 1e-06
 NEG_FILL = -1e30
 LOG_BASE = 1.442695041
+
+
+MESH_ID = pl.DeviceIdType.MESH
+BF16 = jnp.bfloat16
+F32 = jnp.float32
+NZ = 4
+TILE = 256
+PIECES = 6
+GAINS = 6
+FIRST_IN = 0
+FIRST_OUT = 5
+
+
+def place():
+    s, f = lax.axis_index("section"), lax.axis_index("fsdp")
+    return s, f // 4, (f // 2) % 2, f % 2
+
+
+def device(s, z, x, c):
+    return (s, z * 4 + x * 2 + c)
+
+
+def inside(z):
+    return (z >= 0) & (z < NZ)
+
+
+def clipped(z):
+    return jnp.clip(z, 0, NZ - 1)
+
+
+def neighbour_barrier(s, z, x, c):
+    barrier = pltpu.get_barrier_semaphore()
+
+    def tell(target):
+        pl.semaphore_signal(barrier, inc=1, device_id=target, device_id_type=MESH_ID)
+
+    tell(device(s, z, x, 1 - c))
+    tell(device(s, z, 1 - x, c))
+    tell(device(1 - s, z, x, c))
+    tell(device(s, (z + 2) % NZ, x, c))
+    pl.when(z > 0)(lambda: tell(device(s, z - 1, x, c)))
+    pl.when(z < NZ - 1)(lambda: tell(device(s, z + 1, x, c)))
+    pl.semaphore_wait(barrier, 4 + (z > 0).astype(jnp.int32) + (z < NZ - 1).astype(jnp.int32))
+
+
+def remote(src, dst, send_sem, recv_sem, target):
+    return pltpu.make_async_remote_copy(
+        src, dst, send_sem, recv_sem, device_id=target, device_id_type=MESH_ID
+    )
+
+
+class Gather:
+    def __init__(self, where, view, sems):
+        self.where, self.view = where, view
+        self.send_sem, self.recv_sem, self.core_send, self.core_recv = sems
+
+    def ship(self, p, zz, xx, way, cond, wait):
+        s, z, x, c = self.where
+        i = zz * 2 + xx
+        block = self.view(p, zz, xx, c)
+        if way < 3:
+            target = (
+                device(s, clipped(z + 1), x, c),
+                device(s, clipped(z - 1), x, c),
+                device(s, z, 1 - x, c),
+            )[way]
+            cp = remote(block, block, self.send_sem.at[p, i, way], self.recv_sem.at[p, i], target)
+        else:
+            cp = remote(block, block, self.core_send.at[p, i], self.core_recv.at[p, i], device(s, z, x, 1 - c))
+        act = cp.wait_send if wait else cp.start
+        if cond is None:
+            act()
+        else:
+            pl.when(cond)(act)
+
+    def arrived(self, p, zz, xx):
+        s, z, x, c = self.where
+        block = self.view(p, zz, xx, c)
+        i = zz * 2 + xx
+        remote(block, block, self.send_sem.at[p, i, 0], self.recv_sem.at[p, i], device(s, z, 1 - x, c)).wait_recv()
+
+    def own(self, p, wait=False):
+        s, z, x, c = self.where
+        for way, cond in ((0, z < NZ - 1), (1, z > 0), (2, None), (3, None)):
+            self.ship(p, z, x, way, cond, wait)
+
+    def relay(self, p, wait=False):
+        s, z, x, c = self.where
+        cols = (x, 1 - x) if p == FIRST_IN else (x,)
+        if p == FIRST_IN:
+            if not wait:
+                self.arrived(p, z, 1 - x)
+            self.ship(p, z, 1 - x, 0, z < NZ - 1, wait)
+            self.ship(p, z, 1 - x, 1, z > 0, wait)
+            self.ship(p, z, 1 - x, 3, None, wait)
+        for d in range(1, NZ):
+            for sign, way in ((-1, 0), (1, 1)):
+                zz = clipped(z + sign * d)
+                here = inside(z + sign * d)
+                for xx in cols:
+                    if not wait:
+                        pl.when(here)(lambda zz=zz, xx=xx: self.arrived(p, zz, xx))
+                    self.ship(p, zz, xx, way, here & inside(z - sign), wait)
+                    if p != FIRST_IN:
+                        self.ship(p, zz, xx, 2, here, wait)
+                    self.ship(p, zz, xx, 3, here, wait)
+
+    def across(self, p, wait=False):
+        s, z, x, c = self.where
+        if p == FIRST_IN:
+            return
+        for d in range(NZ):
+            for sign in (-1, 1) if d else (1,):
+                zz = clipped(z + sign * d)
+                here = inside(z + sign * d)
+                if not wait:
+                    pl.when(here)(lambda zz=zz: self.arrived(p, zz, 1 - x))
+                self.ship(p, zz, 1 - x, 3, here, wait)
+
+    def finish(self, p):
+        s, z, x, c = self.where
+        for zz in range(NZ):
+            for xx in range(2):
+                block = self.view(p, zz, xx, 1 - c)
+                i = zz * 2 + xx
+                remote(block, block, self.core_send.at[p, i], self.core_recv.at[p, i], device(s, z, x, 1 - c)).wait_recv()
+
+    def drain(self, p):
+        self.own(p, True)
+        self.relay(p, True)
+        self.across(p, True)
+
+
+def add_block(dst, src):
+    @pl.loop(0, dst.shape[0] // 16)
+    def _(k):
+        r = pl.ds(pl.multiple_of(k * 16, 16), 16)
+        dst[r] = (dst[r].astype(F32) + src[r].astype(F32)).astype(BF16)
+
+
+class Scatter:
+    def __init__(self, where, view, bufs, sems, store):
+        self.where, self.view, self.store = where, view, store
+        self.got_core, self.got_x, self.got_z, self.got_zz = bufs
+        self.core_s, self.core_r, self.x_s, self.x_r, self.z_s, self.z_r = sems
+
+    def core_copy(self, p, i):
+        s, z, x, c = self.where
+        return remote(
+            self.view(p, i // 2, i % 2, 1 - c),
+            self.got_core.at[p, i],
+            self.core_s.at[p, i],
+            self.core_r.at[p, i],
+            device(s, z, x, 1 - c),
+        )
+
+    def core_send(self, p):
+        for i in range(2 * NZ):
+            self.core_copy(p, i).start()
+
+    def core_add(self, p):
+        c = self.where[3]
+
+        @pl.loop(0, 2 * NZ)
+        def _(i):
+            self.core_copy(p, i).wait_recv()
+            add_block(self.view(p, i // 2, i % 2, c), self.got_core.at[p, i])
+
+    def x_copy(self, p, zz):
+        s, z, x, c = self.where
+        return remote(
+            self.view(p, zz, 1 - x, c),
+            self.got_x.at[p, zz],
+            self.x_s.at[p, zz],
+            self.x_r.at[p, zz],
+            device(s, z, 1 - x, c),
+        )
+
+    def steps(self):
+        z = self.where[1]
+        for d in range(NZ - 1, 0, -1):
+            for sign in (1, -1):
+                yield d, clipped(z + sign * d), inside(z + sign * d), sign
+
+    def x_send(self, p):
+        for _, zz, here, _ in self.steps():
+            pl.when(here)(lambda zz=zz: self.x_copy(p, zz).start())
+        self.x_copy(p, self.where[1]).start()
+
+    def x_add(self, p, zz):
+        s, z, x, c = self.where
+        self.x_copy(p, zz).wait_recv()
+        add_block(self.view(p, zz, x, c), self.got_x.at[p, zz])
+
+    def slot(self, p, k, xx):
+        return self.got_zz.at[xx, k] if p == FIRST_OUT else self.got_z.at[p, k]
+
+    def z_copy(self, p, zz, xx, sign, k):
+        s, z, x, c = self.where
+        return remote(
+            self.view(p, zz, xx, c),
+            self.slot(p, k, xx),
+            self.z_s.at[p, xx, zz],
+            self.z_r.at[p, xx, k],
+            device(s, clipped(z + sign), x, c),
+        )
+
+    def z_out(self, p, zz, xx, sign):
+        k = jnp.where((sign < 0) & (self.where[1] + sign == zz), NZ, zz)
+        return self.z_copy(p, zz, xx, sign, k)
+
+    def cols(self, p):
+        x = self.where[2]
+        return (x, 1 - x) if p == FIRST_OUT else (x,)
+
+    def z_take(self, p, zz, xx, k):
+        self.z_copy(p, zz, xx, 1, k).wait_recv()
+        add_block(self.view(p, zz, xx, self.where[3]), self.slot(p, k, xx))
+
+    def z_step(self, p, distance):
+        z = self.where[1]
+        for d, zz, here, sign in self.steps():
+            if d != distance:
+                continue
+
+            @pl.when(here)
+            def _(zz=zz, sign=sign):
+                if p != FIRST_OUT:
+                    self.x_add(p, zz)
+                for xx in self.cols(p):
+                    pl.when(inside(z - sign))(lambda xx=xx: self.z_take(p, zz, xx, zz))
+                    self.z_out(p, zz, xx, sign).start()
+
+    def z_last(self, p, xx):
+        z = self.where[1]
+        pl.when(z > 0)(lambda: self.z_take(p, z, xx, z))
+        pl.when(z < NZ - 1)(lambda: self.z_take(p, z, xx, NZ))
+
+    def close(self, p):
+        s, z, x, c = self.where
+        if p == FIRST_OUT:
+            self.z_last(p, 1 - x)
+            self.x_copy(p, z).start()
+            self.z_last(p, x)
+            self.x_add(p, z)
+        else:
+            self.x_add(p, z)
+            self.z_last(p, x)
+        self.store(p, self.view(p, z, x, c))
+
+    def serve(self, p):
+        for d in range(NZ - 1, 0, -1):
+            self.z_step(p, d)
+        self.close(p)
+
+    def drain(self, p):
+        for i in range(2 * NZ):
+            self.core_copy(p, i).wait_send()
+        for _, zz, here, sign in self.steps():
+            if p != FIRST_OUT:
+                pl.when(here)(lambda zz=zz: self.x_copy(p, zz).wait_send())
+            for xx in self.cols(p):
+                pl.when(here)(lambda zz=zz, xx=xx, sign=sign: self.z_out(p, zz, xx, sign).wait_send())
+        self.x_copy(p, self.where[1]).wait_send()
+
+
+def head_windows():
+    for k in range(8):
+        start = HD * k // 128 * 128
+        offset = HD * k - start
+        span = 128 if offset + HD <= 128 else 256
+        yield k, start, offset, span
+
+
+def layers_kernel(
+    n,
+    tokens,
+    cotangent,
+    lengths,
+    gain_block,
+    scale,
+    wq,
+    wo,
+    wu,
+    wd,
+    out_half,
+    token_half,
+    d_q,
+    d_o,
+    d_u,
+    d_d,
+    small_out,
+    held,
+    gain_all,
+    gain_rows,
+    hb,
+    a1,
+    qf,
+    qb,
+    kb,
+    vb,
+    prob,
+    ob,
+    mid,
+    a2,
+    up,
+    hid,
+    grad,
+    dup,
+    dmid,
+    low,
+    give,
+    sums,
+    swap,
+    got_core,
+    got_x,
+    got_z,
+    got_zz,
+    *sems,
+):
+    where = s, z, x, c = place()
+    dob = dup
+    rows, width = hb.shape
+    slots = cotangent.shape[1]
+    half = width // 2
+    group = 8 * HD
+    g_sems, r_sems = sems[:4], sems[4:10]
+    swap_s, swap_r, hand_s, hand_r, back_s, back_r, end_s, end_r = sems[10:]
+    across_y = device(1 - s, z, x, c)
+
+    def weight_view(p, zz, xx, cc):
+        return held.at[p, pl.ds(pl.multiple_of((zz * 4 + xx * 2 + cc) * n, 16), n)]
+
+    def view(p, zz, xx, cc):
+        if p == GAINS:
+            return gain_all.at[zz * 4 + xx * 2 + cc]
+        return weight_view(p, zz, xx, cc)
+
+    def store(p, block):
+        @pl.loop(0, n // 16)
+        def _(k):
+            r = pl.ds(pl.multiple_of(k * 16, 16), 16)
+            value = block[r].astype(F32)
+            if p < 3:
+                d_q[r, p * width : (p + 1) * width] = value
+            else:
+                (d_o, d_u, d_d)[p - 3][r] = value
+
+    gather = Gather(where, view, g_sems)
+    scatter = Scatter(where, weight_view, (got_core, got_x, got_z, got_zz), r_sems, store)
+
+
+    def row_loop(fn):
+        @pl.loop(0, rows // 32)
+        def _(k):
+            fn(pl.ds(pl.multiple_of(k * 32, 32), 32))
+
+    def project(p, a, emit):
+        @pl.loop(0, width // TILE)
+        def _(k):
+            lanes = pl.ds(pl.multiple_of(k * TILE, TILE), TILE)
+            emit(lanes, jnp.dot(a[...], held[p, :, lanes], preferred_element_type=F32))
+
+    def project_back(pieces, emit):
+        @pl.loop(0, width // TILE)
+        def _(k):
+            lanes = pl.ds(pl.multiple_of(k * TILE, TILE), TILE)
+            total = None
+            for p, a in pieces:
+                term = contract_cols(a[...], held[p, lanes, :])
+                total = term if total is None else total + term
+            emit(lanes, total)
+
+    def weight_grad(p, a, g):
+        @pl.loop(0, width // TILE)
+        def _(k):
+            lanes = pl.ds(pl.multiple_of(k * TILE, TILE), TILE)
+            flipped = a[:, lanes].T
+            for j in range(width // TILE):
+                cols = slice(j * TILE, (j + 1) * TILE)
+                held[p, lanes, cols] = jnp.dot(flipped, g[:, cols], preferred_element_type=F32).astype(BF16)
+
+    def recip_of(value):
+        return lax.rsqrt(jnp.mean(value * value, -1, keepdims=True) + NORM_EPS)
+
+    def norm(src, row, dst):
+        def part(r):
+            value = src[r].astype(F32)
+            dst[r] = (value * recip_of(value) * gain_rows[row : row + 1]).astype(BF16)
+
+        row_loop(part)
+
+    def put(ref):
+        def emit(lanes, value):
+            ref[:, lanes] = value.astype(ref.dtype)
+
+        return emit
+
+    def emit_query(lanes, value):
+        qf[:, lanes] = value
+        qb[:, lanes] = (value * scale[0:1, lanes]).astype(BF16)
+
+    def emit_up(lanes, value):
+        up[:, lanes] = value
+        hid[:, lanes] = (value / (1.0 + jnp.exp(-value))).astype(BF16)
+
+    def emit_mid(lanes, value):
+        mid[:, lanes] = hb[:, lanes].astype(F32) + value
+
+    def emit_out(lanes, value):
+        give[:, lanes] = (mid[:, lanes] + value).astype(BF16)
+
+    def lane_mask(offset, span):
+        lane = lax.broadcasted_iota(jnp.int32, (1, span), 1)
+        return ((lane >= offset) & (lane < offset + HD)).astype(F32).astype(BF16)
+
+    def attention(body):
+        @pl.loop(0, rows // slots * 2)
+        def _(it):
+            seq, g = it // 2, it % 2
+            r = pl.ds(pl.multiple_of(seq * slots, slots), slots)
+
+            def window(ref, start, span):
+                return ref[r, pl.ds(pl.multiple_of(g * group + start, 128), span)]
+
+            body(it, seq, r, g, window)
+
+    def spread(total, start, span, value):
+        for j in range(span // 128):
+            k = start // 128 + j
+            term = value[:, j * 128 : (j + 1) * 128]
+            total[k] = term if total[k] is None else total[k] + term
+
+    def attend(it, seq, r, g, window):
+        allowed = causal_allowed(slots, lengths[seq])
+        total = [None] * (group // 128)
+        for k, start, offset, span in head_windows():
+            only = lane_mask(offset, span)
+            scores = contract_cols(window(qb, start, span) * only, window(kb, start, span))
+            scores = jnp.where(allowed, scores, NEG_FILL)
+            expd = jnp.exp(scores - jnp.max(scores, -1, keepdims=True))
+            probs = expd / jnp.sum(expd, -1, keepdims=True)
+            prob[it, k] = probs
+            value = jnp.dot(probs.astype(BF16), window(vb, start, span) * only, preferred_element_type=F32)
+            spread(total, start, span, value)
+        for k, value in enumerate(total):
+            ob[r, pl.ds(pl.multiple_of(g * group + k * 128, 128), 128)] = value.astype(BF16)
+
+    def attend_back(it, seq, r, g, window):
+        count = group // 128
+        t_q, t_k, t_v = [None] * count, [None] * count, [None] * count
+        for k, start, offset, span in head_windows():
+            only = lane_mask(offset, span)
+            d_o_part = window(dob, start, span) * only
+            probs = prob[it, k]
+            d_probs = contract_cols(d_o_part, window(vb, start, span))
+            spread(t_v, start, span, contract_rows(probs.astype(BF16), d_o_part))
+            d_scores = probs * (d_probs - jnp.sum(probs * d_probs, -1, keepdims=True))
+            d_scores = d_scores.astype(BF16)
+            spread(t_q, start, span, jnp.dot(d_scores, window(kb, start, span) * only, preferred_element_type=F32))
+            spread(t_k, start, span, contract_rows(d_scores, window(qb, start, span) * only))
+        for k in range(count):
+            lanes = pl.ds(pl.multiple_of(g * group + k * 128, 128), 128)
+            products = t_q[k] * qf[r, lanes]
+            sums[2, :, lanes] += jnp.sum(products.reshape(slots // 8, 8, 128), 0)
+            qb[r, lanes] = (t_q[k] * scale[0:1, lanes]).astype(BF16)
+            kb[r, lanes] = t_k[k].astype(BF16)
+            vb[r, lanes] = t_v[k].astype(BF16)
+
+    def emit_dup(lanes, value):
+        u = up[:, lanes]
+        sig = 1.0 / (1.0 + jnp.exp(-u))
+        dup[:, lanes] = (value * sig * (1.0 + u * (1.0 - sig))).astype(BF16)
+
+    def norm_grad(row, src, base, emit):
+        def part(r):
+            value, d_normed = src[r].astype(F32), up[r]
+            recip = recip_of(value)
+            sums[row] += jnp.sum((d_normed * value * recip).reshape(4, 8, width), 0)
+            emit(r, base[r].astype(F32) + norm_back(value, recip, d_normed * gain_rows[row : row + 1]))
+
+        row_loop(part)
+
+    def emit_dmid(r, value):
+        dmid[r] = value
+        low[r] = value.astype(BF16)
+
+    def emit_give(r, value):
+        give[r] = value.astype(BF16)
+
+    def spread_gains():
+        gain_rows[...] = jnp.zeros_like(gain_rows)
+        for f in range(4 * NZ):
+            start = min(n * f // 128 * 128, width - 256)
+            block = jnp.concatenate([gain_all[f], jnp.zeros((8, 128), F32)], -1)
+            block = pltpu.roll(block, n * f - start, 1) if n * f > start else block
+            gain_rows[:, start : start + 256] += block
+
+    def forward_stage(p):
+        if p == 0:
+            spread_gains()
+            norm(hb, 0, a1)
+            project(0, a1, emit_query)
+        elif p == 1:
+            project(1, a1, put(kb))
+        elif p == 2:
+            project(2, a1, put(vb))
+            attention(attend)
+        elif p == 3:
+            project(3, ob, emit_mid)
+            norm(mid, 1, a2)
+        elif p == 4:
+            project(4, a2, emit_up)
+        else:
+            project(5, hid, emit_out)
+
+
+    def hand(k):
+        r = pl.ds(k * slots, slots)
+        return remote(give.at[r], hb.at[r], hand_s.at[k], hand_r.at[k], across_y)
+
+    def back(k):
+        r = pl.ds(k * slots, slots)
+        return remote(give.at[r], grad.at[r], back_s.at[k], back_r.at[k], across_y)
+
+    def end(which):
+        dst, col = ((out_half, 0), (token_half, half))[which]
+        return remote(give.at[:, col : col + half], dst, end_s.at[which], end_r.at[which], across_y)
+
+
+    mine = pl.ds(pl.multiple_of((z * 4 + x * 2 + c) * n, 16), n)
+    for k in range(3):
+        held[k, mine] = wq[:, k * width : (k + 1) * width].astype(BF16)
+    for k, ref in enumerate((wo, wu, wd)):
+        held[3 + k, mine] = ref[...].astype(BF16)
+    gain_all[z * 4 + x * 2 + c] = gain_block[...]
+    sums[...] = jnp.zeros_like(sums)
+    neighbour_barrier(s, z, x, c)
+
+    @pl.when(s == 0)
+    def _():
+        for k in range(rows // slots):
+            hb[k * slots : (k + 1) * slots] = tokens[k]
+
+    order_in = [GAINS] + list(range(PIECES))
+
+    @pl.loop(0, 2)
+    def _(phase):
+        @pl.when(phase == 0)
+        def _():
+            gather.own(order_in[0])
+            gather.own(order_in[1])
+
+        @pl.when((phase == 1) & (s == 1))
+        def _():
+            for k in range(rows // slots):
+                hand(k).wait_recv()
+
+        count = len(order_in)
+        for t in range(count + 2):
+
+            @pl.when(phase == 0)
+            def _():
+                if t + 2 < count:
+                    gather.own(order_in[t + 2])
+                if t < count:
+                    gather.relay(order_in[t])
+                if 0 <= t - 1 < count:
+                    gather.across(order_in[t - 1])
+                if 0 <= t - 2:
+                    gather.finish(order_in[t - 2])
+
+            if t - 2 >= 1:
+                pl.when(phase == s)(lambda: forward_stage(order_in[t - 2]))
+
+        @pl.when((phase == 0) & (s == 0))
+        def _():
+            for k in range(rows // slots):
+                hand(k).start()
+
+    for p in order_in:
+        gather.drain(p)
+
+    @pl.when(s == 0)
+    def _():
+        for k in range(rows // slots):
+            hand(k).wait_send()
+            back(k).wait_recv()
+
+    @pl.when(s == 1)
+    def _():
+        end(0).start()
+        out_half[...] = give[:, half:]
+        for k in range(rows // slots):
+            row = lax.broadcasted_iota(jnp.int32, (slots, 1), 0)
+            live = (row < lengths[k]).astype(F32)
+            grad[k * slots : (k + 1) * slots] = (cotangent[k].astype(F32) * live).astype(BF16)
+
+    project_back([(5, grad)], emit_dup)
+    weight_grad(5, hid, grad)
+    scatter.core_send(5)
+    project_back([(4, dup)], put(up))
+    weight_grad(4, a2, dup)
+    scatter.core_send(4)
+    scatter.core_add(5)
+    scatter.z_step(5, 3)
+    norm_grad(1, mid, grad, emit_dmid)
+    project_back([(3, low)], put(dob))
+    weight_grad(3, ob, low)
+    scatter.core_send(3)
+    scatter.core_add(4)
+    scatter.x_send(4)
+    attention(attend_back)
+    project_back([(0, qb), (1, kb), (2, vb)], put(up))
+
+    @pl.when(s == 1)
+    def _():
+        end(0).wait_send()
+
+    norm_grad(0, hb, dmid, emit_give)
+
+    @pl.when(s == 1)
+    def _():
+        for k in range(rows // slots):
+            back(k).start()
+
+    @pl.when(s == 0)
+    def _():
+        end(1).start()
+        token_half[...] = give[:, :half]
+
+    scatter.core_add(3)
+    scatter.x_send(3)
+    for p, ref in enumerate((qb, kb, vb)):
+        weight_grad(p, a1, ref)
+        scatter.core_send(p)
+
+    totals = [jnp.sum(sums[k], 0, keepdims=True) for k in range(3)]
+    swap[0, 0] = jnp.concatenate(totals + [jnp.zeros((5, width), F32)], 0)
+    partners = (
+        device(s, z, x, 1 - c),
+        device(s, z, 1 - x, c),
+        device(s, z + 1 - 2 * (z % 2), x, c),
+        device(s, (z + 2) % NZ, x, c),
+    )
+
+    def exchange(k):
+        return remote(swap.at[k, 0], swap.at[k, 1], swap_s.at[k], swap_r.at[k], partners[k])
+
+    exchange(0).start()
+    for d in (2, 1):
+        scatter.z_step(5, d)
+    scatter.close(5)
+    order_out = [4, 3, 0, 1, 2]
+    for k, p in enumerate(order_out):
+        if k + 2 < len(order_out):
+            scatter.core_add(order_out[k + 2])
+            scatter.x_send(order_out[k + 2])
+        if k < 4:
+            exchange(k).wait_recv()
+            if k < 3:
+                swap[k + 1, 0] = swap[k, 0] + swap[k, 1]
+                exchange(k + 1).start()
+            else:
+                small_out[...] = swap[k, 0] + swap[k, 1]
+        scatter.serve(p)
+    for p in range(PIECES):
+        scatter.drain(p)
+    for k in range(4):
+        exchange(k).wait_send()
+
+    @pl.when(s == 0)
+    def _():
+        end(1).wait_send()
+        end(0).wait_recv()
+
+    @pl.when(s == 1)
+    def _():
+        for k in range(rows // slots):
+            back(k).wait_send()
+        end(1).wait_recv()
+
+
+def near_shards(
+    tokens, cotangent, lengths, qkv_weight, out_weight, up_weight, down_weight, norm_gains, query_gain
+):
+    n, width = out_weight.shape
+    count, slots, _ = tokens.shape
+    rows = count * slots
+    factor = LOG_BASE / math.sqrt(HD)
+    scale = jnp.tile(jax.nn.softplus(query_gain) * factor, (8, H))
+    gains = norm_gains.astype(BF16).astype(F32).T
+    gain_block = jnp.pad(gains, ((0, 6), (0, 128 - n)))
+    dma = pltpu.SemaphoreType.DMA
+    whole = pl.BlockSpec(memory_space=pltpu.VMEM)
+    block = (n, width)
+    low_rows = pltpu.VMEM((rows, width), BF16)
+    wide_rows = pltpu.VMEM((rows, width), F32)
+    scratch = dict(
+        held=pltpu.VMEM((PIECES, 4 * NZ * n, width), BF16),
+        gain_all=pltpu.VMEM((4 * NZ, 8, 128), F32),
+        gain_rows=pltpu.VMEM((8, width), F32),
+        hb=low_rows,
+        a1=low_rows,
+        qf=wide_rows,
+        qb=low_rows,
+        kb=low_rows,
+        vb=low_rows,
+        prob=pltpu.VMEM((2 * count, 8, slots, slots), F32),
+        ob=low_rows,
+        mid=wide_rows,
+        a2=low_rows,
+        up=wide_rows,
+        hid=low_rows,
+        grad=low_rows,
+        dup=low_rows,
+        dmid=wide_rows,
+        low=low_rows,
+        give=low_rows,
+        sums=pltpu.VMEM((3, 8, width), F32),
+        swap=pltpu.VMEM((4, 2, 8, width), F32),
+        got_core=pltpu.VMEM((PIECES, 2 * NZ) + block, BF16),
+        got_x=pltpu.VMEM((PIECES, NZ) + block, BF16),
+        got_z=pltpu.VMEM((PIECES - 1, NZ + 1) + block, BF16),
+        got_zz=pltpu.VMEM((2, NZ + 1) + block, BF16),
+    )
+    semaphores = [
+        dma((PIECES + 1, 2 * NZ, 3)),
+        dma((PIECES + 1, 2 * NZ)),
+        dma((PIECES + 1, 2 * NZ)),
+        dma((PIECES + 1, 2 * NZ)),
+        dma((PIECES, 2 * NZ)),
+        dma((PIECES, 2 * NZ)),
+        dma((PIECES, NZ)),
+        dma((PIECES, NZ)),
+        dma((PIECES, 2, NZ)),
+        dma((PIECES, 2, NZ + 1)),
+        dma((4,)),
+        dma((4,)),
+        dma((count,)),
+        dma((count,)),
+        dma((count,)),
+        dma((count,)),
+        dma((2,)),
+        dma((2,)),
+    ]
+    half = jax.ShapeDtypeStruct((rows, width // 2), BF16)
+    out, d_tokens, d_q, d_o, d_u, d_d, small = pl.pallas_call(
+        lambda *refs: layers_kernel(n, *refs),
+        out_shape=(
+            half,
+            half,
+            jax.ShapeDtypeStruct((n, 3 * width), F32),
+            jax.ShapeDtypeStruct(block, F32),
+            jax.ShapeDtypeStruct(block, F32),
+            jax.ShapeDtypeStruct(block, F32),
+            jax.ShapeDtypeStruct((8, width), F32),
+        ),
+        in_specs=[whole, whole, pl.BlockSpec(memory_space=pltpu.SMEM)] + [whole] * 6,
+        out_specs=(whole,) * 7,
+        scratch_shapes=list(scratch.values()) + semaphores,
+        compiler_params=pltpu.CompilerParams(
+            collective_id=1, has_side_effects=True, vmem_limit_bytes=63 << 20
+        ),
+        name="two_layers",
+    )(tokens, cotangent, lengths, gain_block, scale, qkv_weight, out_weight, up_weight, down_weight)
+    own = lax.dynamic_slice_in_dim(small[:2], lax.axis_index("fsdp") * n, n, 1).T
+    d_scale = jnp.sum(small[2].reshape(H, HD), 0)
+    d_query_gain = (d_scale * jax.nn.sigmoid(query_gain[0]) * factor)[None]
+    shape = (count, slots, width // 2)
+    return (
+        out.reshape(shape),
+        d_tokens.reshape(shape),
+        d_q[None],
+        d_o[None],
+        d_u[None],
+        d_d[None],
+        own[None],
+        d_query_gain,
+    )
 
 
 def swapped(value, axis, bit):
@@ -167,6 +949,18 @@
     norm_gains,
     query_gain,
 ):
+    if lax.axis_size("fsdp") == 4 * NZ:
+        return near_shards(
+            tokens,
+            cotangent,
+            lengths,
+            qkv_weight[0],
+            out_weight[0],
+            up_weight[0],
+            down_weight[0],
+            norm_gains[0],
+            query_gain,
+        )
     section_index = lax.axis_index("section")
     micro_count, slot_rows, width = tokens.shape
     half_width = width // 2

time: 923 us -> 369 us (0.40); the launches traced: 913 us -> 368 us
  waiting for transfers between devices: 607 us -> 0 us
  Pallas kernels: 0 us -> 355 us
  matrix products: 155 us -> 0 us
  blocking collectives: 58 us -> 0 us
  local copies, waits for them, and re-layouts: 41.1 us -> 10.1 us
  other arithmetic: 26.6 us -> 2.51 us
  between operations: 16.2 us -> 0.67 us
    reduce_scatter x4 -> x0, waiting for transfers between devices: 415 us -> none  [the longest x1 204 us: shards(): lax.psum_scatter(grad_totals[0], 'fsdp', scatter_dimension=0, tiled=True)]
    pallas_call x0 -> x1, Pallas kernels: none -> 355 us  [near_shards(): pl.pallas_call(lambda *refs: layers_kernel(n, *refs), out_shape=(half, ha...]
    all_gather x4 -> x0, waiting for transfers between devices: 176 us -> none  [the longest x1 52 us: gather_weights(): lax.all_gather(qkv_weight.astype(jnp.bfloat16), 'fsdp', axis=1, tiled=True)]
    dot_general x57 -> x0, matrix products: 155 us -> none  [the longest x12 65 us: contract_rows(): lax.dot_general(left, right, (((0,), (0,)), ((), ())), preferred_element_...]
    psum x1 -> x0, blocking collectives: 30.5 us -> none  [shards(): scale_sum = lax.psum(scale_total, 'fsdp')]
    all_gather x1 -> x0, blocking collectives: 27.6 us -> none  [gather_weights(): lax.all_gather(norm_gains.astype(jnp.bfloat16), 'fsdp', axis=1, tiled=True)]
    ppermute x6 -> x0, waiting for transfers between devices: 16 us -> none  [swapped(): lax.ppermute(value, axis, [(i, i ^ 1 << bit) for i in range(lax.axis_size...]
    slice x15 -> x2, local copies, waits for them, and re-layouts: 17 us -> 1.68 us  [the longest x1 0.9 us: near_shards(): d_scale = jnp.sum(small[2].reshape(H, HD), 0)]
  transfers between devices with their start and end apart: 15 -> 0, of which waited for: 11 -> 0; matrix products, arithmetic and copies ran while one was open for 15% -> 0% of each run, Pallas kernels for 0% -> 0%
where the time goes in v2:
time: 369 us; the launch traced here: 368 us
  Pallas kernels  355 us (96%)
  local copies, waits for them, and re-layouts  10.1 us (3%)
    pallas_call x1, Pallas kernels, near_shards(): pl.pallas_call(lambda *refs: layers_kernel(n, *refs), out_shape=(half, ha...  355 us

profile of v2, /device:TPU:0, one launch (start us, length us, event | category | flops | bytes accessed | tf_op | source)
XLA Modules:
  0.0 368.3 jit_solution(4806687697207819142)
XLA Ops:
  0.6 0.7 convert_bitcast_fusion
  1.3 0.7 fusion.1
  2.0 0.6 pad_convert_fusion.refs_3_
  2.6 0.1 tile.15
  2.7 0.6 tile.16.refs_4_
  3.3 0.0 copy-start.4
  3.3 355.1 %two_layers.1 = (bf16[256,640]{1,0:T(8,128)(2,1)}, bf16[256,640]{1,0:T(8,128)(2,1)}, f32[80,3840]{1,0:T(8,128)}, f32[80,1280]{1,0:T(8,128)}, f32[80,1280]{1,0:T(...) custom-call(bf16[2,128,1280]{2,1,0:T(8,128)(2,1)} %refs_0_.1, bf16[2,128,1280]{2,1,0:T(8,128)(2,1)} %refs_1_.1, s32[2]{0:T(128)} %refs_2_.1, ...), custom_call_target="tpu_custom_call" | custom-call | tf_op jit(solution)/shard_map/two_layers/pallas_call | solution.py:764
  358.4 0.0 copy-start
  358.4 0.9 slice_reduce_fusion
  359.3 0.8 slice.6
  360.1 0.6 dynamic-slice_bitcast_fusion
  360.7 0.1 reshape_squeeze.3
  360.8 0.0 copy-done.4
  360.8 0.5 fusion.2
  361.4 1.7 copy.23
  363.1 1.7 copy.24
  364.8 0.0 copy-done
  364.8 0.0 copy-start.3
  364.8 0.0 copy-start.2
  364.8 1.0 copy.25
  365.8 0.2 copy-done.3
  366.1 0.0 copy-start.1
  366.1 0.8 copy.26
  366.8 0.0 copy-done.2
  366.8 0.8 copy.27
  367.6 0.0 copy-done.1
  367.6 0.8 copy.28
  (2 shorter events, 0.0 us)
Async XLA Ops:
  3.3 357.5 %copy-start.4 = (f32[1,80]{1,0:T(1,128)S(1)}, f32[1,80]{1,0:T(1,128)}, u32[]{:S(2)}) copy-start(f32[1,80]{1,0:T(1,128)} %param.17) | copy-start | bytes 964
  358.4 6.4 %copy-start = (f32[80,3840]{1,0:T(8,128)S(1)}, f32[80,3840]{1,0:T(8,128)}, u32[]{:S(2)}) copy-start(f32[80,3840]{1,0:T(8,128)} %get-tuple-element.17) | copy-start | bytes 3686404
  364.8 1.3 copy-start.3
  364.8 2.0 copy-start.2
  366.1 1.5 copy-start.1

commit v3 on v2

--- a/solution.py
+++ b/solution.py
@@ -23,8 +23,8 @@
 TILE = 256
 PIECES = 6
 GAINS = 6
-FIRST_IN = 0
-FIRST_OUT = 5
+FIRST_IN = 5
+FIRST_OUT = 4
 
 
 def place():
@@ -63,6 +63,255 @@
     return pltpu.make_async_remote_copy(
         src, dst, send_sem, recv_sem, device_id=target, device_id_type=MESH_ID
     )
+
+
+GATHER_STEPS = (
+    ("own", 5),
+    ("own", 6),
+    ("own", 1),
+    ("own", 0),
+    ("relay", 0, 1, (-1,)),
+    ("relay", 1, 1, (1,)),
+    ("relay", 6, 1, (-1,)),
+    ("relay", 6, 1, (1,)),
+    ("relay", 6, 2, (-1,)),
+    ("relay", 6, 2, (1,)),
+    ("own", 2),
+    ("relay", 0, 1, (1,)),
+    ("relay", 0, 2, (-1,)),
+    ("relay", 6, 3, (1,)),
+    ("relay", 6, 3, (-1,)),
+    ("across", 6, 0),
+    ("relay", 1, 1, (-1,)),
+    ("relay", 2, 1, (1,)),
+    ("relay", 1, 2, (1,)),
+    ("relay", 1, 2, (-1,)),
+    ("across", 6, 1),
+    ("relay", 0, 2, (1,)),
+    ("relay", 0, 3, (1,)),
+    ("across", 6, 2),
+    ("relay", 1, 3, (-1,)),
+    ("relay", 1, 3, (1,)),
+    ("across", 1, 0),
+    ("across", 6, 3),
+    ("relay", 0, 3, (-1,)),
+    ("across", 0, 0),
+    ("across", 0, 1),
+    ("turn", 5),
+    ("across", 1, 1),
+    ("relay", 2, 1, (-1,)),
+    ("relay", 2, 2, (-1,)),
+    ("relay", 5, 1, (-1,)),
+    ("relay", 2, 2, (1,)),
+    ("own", 3),
+    ("relay", 2, 3, (-1,)),
+    ("relay", 2, 3, (1,)),
+    ("across", 0, 2),
+    ("across", 0, 3),
+    ("relay", 3, 1, (1,)),
+    ("finish", 6),
+    ("finish", 0),
+    ("relay", 3, 1, (-1,)),
+    ("across", 2, 0),
+    ("across", 2, 1),
+    ("across", 2, 2),
+    ("across", 1, 2),
+    ("across", 1, 3),
+    ("relay", 3, 2, (-1,)),
+    ("relay", 3, 2, (1,)),
+    ("across", 2, 3),
+    ("relay", 5, 1, (1,)),
+    ("own", 4),
+    ("finish", 1),
+    ("relay", 4, 1, (-1,)),
+    ("relay", 4, 1, (1,)),
+    ("relay", 3, 3, (-1,)),
+    ("finish", 2),
+    ("relay", 3, 3, (1,)),
+    ("relay", 4, 2, (1,)),
+    ("relay", 5, 2, (1,)),
+    ("across", 3, 0),
+    ("across", 3, 1),
+    ("relay", 4, 2, (-1,)),
+    ("across", 3, 2),
+    ("relay", 5, 2, (-1,)),
+    ("across", 3, 3),
+    ("relay", 4, 3, (1,)),
+    ("relay", 4, 3, (-1,)),
+    ("across", 4, 0),
+    ("finish", 3),
+    ("across", 4, 1),
+    ("across", 4, 2),
+    ("across", 4, 3),
+    ("relay", 5, 3, (1,)),
+    ("relay", 5, 3, (-1,)),
+    ("finish", 4),
+    ("finish", 5),
+)
+BACKWARD_STEPS = (
+    (
+        ("hidden",),
+        ("weight", 5),
+        ("core_send", 5),
+        ("normed_two",),
+        ("weight", 4),
+        ("core_send", 4),
+        ("core_add", 5),
+        ("x_send", 5),
+        ("core_add", 4),
+        ("z_step", 4, 3, (1,)),
+        ("z_step", 4, 3, (-1,)),
+        ("middle",),
+        ("attended",),
+        ("heads", 0),
+        ("z_step", 4, 2, (1,)),
+        ("weight", 3),
+        ("core_send", 3),
+        ("z_step", 4, 2, (-1,)),
+        ("heads", 1),
+        ("core_add", 3),
+        ("x_send", 3),
+        ("z_step", 5, 3, (1,)),
+        ("z_step", 4, 1, (1,)),
+        ("normed",),
+        ("weight", 2),
+        ("z_step", 5, 3, (-1,)),
+        ("z_step", 4, 1, (-1,)),
+        ("z_step", 5, 2, (-1,)),
+        ("z_step", 3, 3, (-1,)),
+        ("weight", 0),
+        ("core_send", 0),
+        ("weight", 1),
+        ("core_add", 0),
+        ("x_send", 0),
+        ("input",),
+        ("core_send", 1),
+        ("core_add", 1),
+        ("x_send", 1),
+        ("z_step", 3, 3, (1,)),
+        ("z_step", 0, 3, (-1,)),
+        ("z_step", 0, 2, (-1,)),
+        ("z_step", 3, 2, (-1,)),
+        ("small", 0),
+        ("small", 1),
+        ("z_step", 5, 1, (-1,)),
+        ("z_step", 5, 2, (1,)),
+        ("z_step", 5, 1, (1,)),
+        ("z_step", 0, 1, (-1,)),
+        ("core_send", 2),
+        ("core_add", 2),
+        ("x_send", 2),
+        ("z_step", 3, 2, (1,)),
+        ("z_step", 3, 1, (1,)),
+        ("z_step", 0, 3, (1,)),
+        ("z_step", 0, 2, (1,)),
+        ("z_step", 0, 1, (1,)),
+        ("z_step", 1, 3, (-1,)),
+        ("z_step", 3, 1, (-1,)),
+        ("z_step", 1, 3, (1,)),
+        ("z_step", 1, 2, (-1,)),
+        ("z_step", 2, 3, (-1,)),
+        ("small", 2),
+        ("turn", 4),
+        ("z_step", 1, 1, (-1,)),
+        ("close", 5),
+        ("z_step", 2, 2, (-1,)),
+        ("z_step", 1, 2, (1,)),
+        ("z_step", 1, 1, (1,)),
+        ("close", 3),
+        ("z_step", 2, 3, (1,)),
+        ("z_step", 2, 2, (1,)),
+        ("small", 3),
+        ("small", 4),
+        ("close", 0),
+        ("z_step", 2, 1, (1,)),
+        ("z_step", 2, 1, (-1,)),
+        ("close", 4),
+        ("close", 1),
+        ("close", 2),
+    ),
+    (
+        ("hidden",),
+        ("normed_two",),
+        ("middle",),
+        ("attended",),
+        ("heads", 0),
+        ("heads", 1),
+        ("normed",),
+        ("input",),
+        ("weight", 5),
+        ("core_send", 5),
+        ("weight", 4),
+        ("core_send", 4),
+        ("core_add", 5),
+        ("x_send", 5),
+        ("core_add", 4),
+        ("z_step", 4, 3, (1,)),
+        ("z_step", 4, 3, (-1,)),
+        ("z_step", 4, 2, (1,)),
+        ("weight", 3),
+        ("core_send", 3),
+        ("z_step", 4, 2, (-1,)),
+        ("core_add", 3),
+        ("x_send", 3),
+        ("z_step", 5, 3, (1,)),
+        ("z_step", 4, 1, (1,)),
+        ("weight", 2),
+        ("z_step", 5, 3, (-1,)),
+        ("z_step", 4, 1, (-1,)),
+        ("z_step", 5, 2, (-1,)),
+        ("z_step", 3, 3, (-1,)),
+        ("weight", 0),
+        ("core_send", 0),
+        ("weight", 1),
+        ("core_add", 0),
+        ("x_send", 0),
+        ("core_send", 1),
+        ("core_add", 1),
+        ("x_send", 1),
+        ("z_step", 3, 3, (1,)),
+        ("z_step", 0, 3, (-1,)),
+        ("z_step", 0, 2, (-1,)),
+        ("z_step", 3, 2, (-1,)),
+        ("small", 0),
+        ("small", 1),
+        ("z_step", 5, 1, (-1,)),
+        ("z_step", 5, 2, (1,)),
+        ("z_step", 5, 1, (1,)),
+        ("z_step", 0, 1, (-1,)),
+        ("core_send", 2),
+        ("core_add", 2),
+        ("x_send", 2),
+        ("z_step", 3, 2, (1,)),
+        ("z_step", 3, 1, (1,)),
+        ("z_step", 0, 3, (1,)),
+        ("z_step", 0, 2, (1,)),
+        ("z_step", 0, 1, (1,)),
+        ("z_step", 1, 3, (-1,)),
+        ("z_step", 3, 1, (-1,)),
+        ("z_step", 1, 3, (1,)),
+        ("z_step", 1, 2, (-1,)),
+        ("z_step", 2, 3, (-1,)),
+        ("small", 2),
+        ("turn", 4),
+        ("z_step", 1, 1, (-1,)),
+        ("close", 5),
+        ("z_step", 2, 2, (-1,)),
+        ("z_step", 1, 2, (1,)),
+        ("z_step", 1, 1, (1,)),
+        ("close", 3),
+        ("z_step", 2, 3, (1,)),
+        ("z_step", 2, 2, (1,)),
+        ("small", 3),
+        ("small", 4),
+        ("close", 0),
+        ("z_step", 2, 1, (1,)),
+        ("z_step", 2, 1, (-1,)),
+        ("close", 4),
+        ("close", 1),
+        ("close", 2),
+    ),
+)
 
 
 class Gather:
@@ -100,38 +349,36 @@
         for way, cond in ((0, z < NZ - 1), (1, z > 0), (2, None), (3, None)):
             self.ship(p, z, x, way, cond, wait)
 
-    def relay(self, p, wait=False):
+    def turn(self, p, wait=False):
         s, z, x, c = self.where
-        cols = (x, 1 - x) if p == FIRST_IN else (x,)
-        if p == FIRST_IN:
+        if not wait:
+            self.arrived(p, z, 1 - x)
+        self.ship(p, z, 1 - x, 0, z < NZ - 1, wait)
+        self.ship(p, z, 1 - x, 1, z > 0, wait)
+        self.ship(p, z, 1 - x, 3, None, wait)
+
+    def relay(self, p, d, signs=(-1, 1), wait=False):
+        s, z, x, c = self.where
+        for sign in signs:
+            way = 0 if sign < 0 else 1
+            zz = clipped(z + sign * d)
+            here = inside(z + sign * d)
+            for xx in (x, 1 - x) if p == FIRST_IN else (x,):
+                if not wait:
+                    pl.when(here)(lambda zz=zz, xx=xx: self.arrived(p, zz, xx))
+                self.ship(p, zz, xx, way, here & inside(z - sign), wait)
+                if p != FIRST_IN:
+                    self.ship(p, zz, xx, 2, here, wait)
+                self.ship(p, zz, xx, 3, here, wait)
+
+    def across(self, p, d, wait=False):
+        s, z, x, c = self.where
+        for sign in (-1, 1) if d else (1,):
+            zz = clipped(z + sign * d)
+            here = inside(z + sign * d)
             if not wait:
-                self.arrived(p, z, 1 - x)
-            self.ship(p, z, 1 - x, 0, z < NZ - 1, wait)
-            self.ship(p, z, 1 - x, 1, z > 0, wait)
-            self.ship(p, z, 1 - x, 3, None, wait)
-        for d in range(1, NZ):
-            for sign, way in ((-1, 0), (1, 1)):
-                zz = clipped(z + sign * d)
-                here = inside(z + sign * d)
-                for xx in cols:
-                    if not wait:
-                        pl.when(here)(lambda zz=zz, xx=xx: self.arrived(p, zz, xx))
-                    self.ship(p, zz, xx, way, here & inside(z - sign), wait)
-                    if p != FIRST_IN:
-                        self.ship(p, zz, xx, 2, here, wait)
-                    self.ship(p, zz, xx, 3, here, wait)
-
-    def across(self, p, wait=False):
-        s, z, x, c = self.where
-        if p == FIRST_IN:
-            return
-        for d in range(NZ):
-            for sign in (-1, 1) if d else (1,):
-                zz = clipped(z + sign * d)
-                here = inside(z + sign * d)
-                if not wait:
-                    pl.when(here)(lambda zz=zz: self.arrived(p, zz, 1 - x))
-                self.ship(p, zz, 1 - x, 3, here, wait)
+                pl.when(here)(lambda zz=zz: self.arrived(p, zz, 1 - x))
+            self.ship(p, zz, 1 - x, 3, here, wait)
 
     def finish(self, p):
         s, z, x, c = self.where
@@ -143,15 +390,17 @@
 
     def drain(self, p):
         self.own(p, True)
-        self.relay(p, True)
-        self.across(p, True)
+        if p == FIRST_IN:
+            self.turn(p, True)
+        for d in range(NZ):
+            if d:
+                self.relay(p, d, wait=True)
+            if p != FIRST_IN:
+                self.across(p, d, True)
 
 
 def add_block(dst, src):
-    @pl.loop(0, dst.shape[0] // 16)
-    def _(k):
-        r = pl.ds(pl.multiple_of(k * 16, 16), 16)
-        dst[r] = (dst[r].astype(F32) + src[r].astype(F32)).astype(BF16)
+    dst[...] = (dst[...].astype(F32) + src[...].astype(F32)).astype(BF16)
 
 
 class Scatter:
@@ -182,11 +431,14 @@
             self.core_copy(p, i).wait_recv()
             add_block(self.view(p, i // 2, i % 2, c), self.got_core.at[p, i])
 
+    def x_slot(self, p, zz):
+        return self.got_x.at[(PIECES - 1) * NZ if p == FIRST_OUT else (p - (p > FIRST_OUT)) * NZ + zz]
+
     def x_copy(self, p, zz):
         s, z, x, c = self.where
         return remote(
             self.view(p, zz, 1 - x, c),
-            self.got_x.at[p, zz],
+            self.x_slot(p, zz),
             self.x_s.at[p, zz],
             self.x_r.at[p, zz],
             device(s, z, 1 - x, c),
@@ -206,10 +458,10 @@
     def x_add(self, p, zz):
         s, z, x, c = self.where
         self.x_copy(p, zz).wait_recv()
-        add_block(self.view(p, zz, x, c), self.got_x.at[p, zz])
+        add_block(self.view(p, zz, x, c), self.x_slot(p, zz))
 
     def slot(self, p, k, xx):
-        return self.got_zz.at[xx, k] if p == FIRST_OUT else self.got_z.at[p, k]
+        return self.got_zz.at[xx, k] if p == FIRST_OUT else self.got_z.at[p - (p > FIRST_OUT), k]
 
     def z_copy(self, p, zz, xx, sign, k):
         s, z, x, c = self.where
@@ -233,10 +485,10 @@
         self.z_copy(p, zz, xx, 1, k).wait_recv()
         add_block(self.view(p, zz, xx, self.where[3]), self.slot(p, k, xx))
 
-    def z_step(self, p, distance):
+    def z_step(self, p, distance, signs=(1, -1)):
         z = self.where[1]
         for d, zz, here, sign in self.steps():
-            if d != distance:
+            if d != distance or sign not in signs:
                 continue
 
             @pl.when(here)
@@ -252,22 +504,20 @@
         pl.when(z > 0)(lambda: self.z_take(p, z, xx, z))
         pl.when(z < NZ - 1)(lambda: self.z_take(p, z, xx, NZ))
 
+    def turn(self, p):
+        s, z, x, c = self.where
+        self.z_last(p, 1 - x)
+        self.x_copy(p, z).start()
+
     def close(self, p):
         s, z, x, c = self.where
         if p == FIRST_OUT:
-            self.z_last(p, 1 - x)
-            self.x_copy(p, z).start()
             self.z_last(p, x)
             self.x_add(p, z)
         else:
             self.x_add(p, z)
             self.z_last(p, x)
         self.store(p, self.view(p, z, x, c))
-
-    def serve(self, p):
-        for d in range(NZ - 1, 0, -1):
-            self.z_step(p, d)
-        self.close(p)
 
     def drain(self, p):
         for i in range(2 * NZ):
@@ -325,6 +575,7 @@
     dup,
     dmid,
     low,
+    dob,
     give,
     sums,
     swap,
@@ -335,13 +586,12 @@
     *sems,
 ):
     where = s, z, x, c = place()
-    dob = dup
     rows, width = hb.shape
     slots = cotangent.shape[1]
     half = width // 2
     group = 8 * HD
     g_sems, r_sems = sems[:4], sems[4:10]
-    swap_s, swap_r, hand_s, hand_r, back_s, back_r, end_s, end_r = sems[10:]
+    swap_s, swap_r, hand_s, hand_r, back_s, back_r, end_s, end_r, load_sem = sems[10:]
     across_y = device(1 - s, z, x, c)
 
     def weight_view(p, zz, xx, cc):
@@ -353,14 +603,11 @@
         return weight_view(p, zz, xx, cc)
 
     def store(p, block):
-        @pl.loop(0, n // 16)
-        def _(k):
-            r = pl.ds(pl.multiple_of(k * 16, 16), 16)
-            value = block[r].astype(F32)
-            if p < 3:
-                d_q[r, p * width : (p + 1) * width] = value
-            else:
-                (d_o, d_u, d_d)[p - 3][r] = value
+        value = block[...].astype(F32)
+        if p < 3:
+            d_q[:, p * width : (p + 1) * width] = value
+        else:
+            (d_o, d_u, d_d)[p - 3][...] = value
 
     gather = Gather(where, view, g_sems)
     scatter = Scatter(where, weight_view, (got_core, got_x, got_z, got_zz), r_sems, store)
@@ -371,30 +618,22 @@
         def _(k):
             fn(pl.ds(pl.multiple_of(k * 32, 32), 32))
 
+    def tiles(emit, value):
+        for k in range(width // TILE):
+            emit(slice(k * TILE, (k + 1) * TILE), value[:, k * TILE : (k + 1) * TILE])
+
     def project(p, a, emit):
-        @pl.loop(0, width // TILE)
-        def _(k):
-            lanes = pl.ds(pl.multiple_of(k * TILE, TILE), TILE)
-            emit(lanes, jnp.dot(a[...], held[p, :, lanes], preferred_element_type=F32))
+        tiles(emit, jnp.dot(a[...], held[p], preferred_element_type=F32))
 
     def project_back(pieces, emit):
-        @pl.loop(0, width // TILE)
-        def _(k):
-            lanes = pl.ds(pl.multiple_of(k * TILE, TILE), TILE)
-            total = None
-            for p, a in pieces:
-                term = contract_cols(a[...], held[p, lanes, :])
-                total = term if total is None else total + term
-            emit(lanes, total)
+        total = None
+        for p, a in pieces:
+            term = contract_cols(a[...], held[p])
+            total = term if total is None else total + term
+        tiles(emit, total)
 
     def weight_grad(p, a, g):
-        @pl.loop(0, width // TILE)
-        def _(k):
-            lanes = pl.ds(pl.multiple_of(k * TILE, TILE), TILE)
-            flipped = a[:, lanes].T
-            for j in range(width // TILE):
-                cols = slice(j * TILE, (j + 1) * TILE)
-                held[p, lanes, cols] = jnp.dot(flipped, g[:, cols], preferred_element_type=F32).astype(BF16)
+        held[p] = contract_rows(a[...], g[...]).astype(BF16)
 
     def recip_of(value):
         return lax.rsqrt(jnp.mean(value * value, -1, keepdims=True) + NORM_EPS)
@@ -430,8 +669,8 @@
         lane = lax.broadcasted_iota(jnp.int32, (1, span), 1)
         return ((lane >= offset) & (lane < offset + HD)).astype(F32).astype(BF16)
 
-    def attention(body):
-        @pl.loop(0, rows // slots * 2)
+    def attention(body, first, last):
+        @pl.loop(2 * first, 2 * last)
         def _(it):
             seq, g = it // 2, it % 2
             r = pl.ds(pl.multiple_of(seq * slots, slots), slots)
@@ -521,7 +760,7 @@
             project(1, a1, put(kb))
         elif p == 2:
             project(2, a1, put(vb))
-            attention(attend)
+            attention(attend, 0, rows // slots)
         elif p == 3:
             project(3, ob, emit_mid)
             norm(mid, 1, a2)
@@ -551,50 +790,52 @@
         held[3 + k, mine] = ref[...].astype(BF16)
     gain_all[z * 4 + x * 2 + c] = gain_block[...]
     sums[...] = jnp.zeros_like(sums)
+    def load(k, wait=False):
+        r = pl.ds(k * slots, slots)
+
+        def first():
+            cp = pltpu.make_async_copy(tokens.at[k], hb.at[r], load_sem.at[k])
+            cp.wait() if wait else cp.start()
+
+        def second():
+            cp = pltpu.make_async_copy(cotangent.at[k], grad.at[r], load_sem.at[k])
+            cp.wait() if wait else cp.start()
+
+        pl.when(s == 0)(first)
+        pl.when(s == 1)(second)
+
+    for k in range(rows // slots):
+        load(k)
     neighbour_barrier(s, z, x, c)
-
-    @pl.when(s == 0)
-    def _():
-        for k in range(rows // slots):
-            hb[k * slots : (k + 1) * slots] = tokens[k]
-
-    order_in = [GAINS] + list(range(PIECES))
+    for k in range(rows // slots):
+        load(k, True)
+
+    def gather_steps(steps):
+        for step in steps:
+            getattr(gather, step[0])(*step[1:])
 
     @pl.loop(0, 2)
     def _(phase):
-        @pl.when(phase == 0)
-        def _():
-            gather.own(order_in[0])
-            gather.own(order_in[1])
-
         @pl.when((phase == 1) & (s == 1))
         def _():
             for k in range(rows // slots):
                 hand(k).wait_recv()
 
-        count = len(order_in)
-        for t in range(count + 2):
-
-            @pl.when(phase == 0)
-            def _():
-                if t + 2 < count:
-                    gather.own(order_in[t + 2])
-                if t < count:
-                    gather.relay(order_in[t])
-                if 0 <= t - 1 < count:
-                    gather.across(order_in[t - 1])
-                if 0 <= t - 2:
-                    gather.finish(order_in[t - 2])
-
-            if t - 2 >= 1:
-                pl.when(phase == s)(lambda: forward_stage(order_in[t - 2]))
+        run = []
+        for step in GATHER_STEPS:
+            run.append(step)
+            if step[0] == "finish":
+                now, run = run, []
+                pl.when(phase == 0)(lambda: gather_steps(now))
+                if step[1] != GAINS:
+                    pl.when(phase == s)(lambda: forward_stage(step[1]))
 
         @pl.when((phase == 0) & (s == 0))
         def _():
             for k in range(rows // slots):
                 hand(k).start()
 
-    for p in order_in:
+    for p in range(PIECES + 1):
         gather.drain(p)
 
     @pl.when(s == 0)
@@ -610,76 +851,66 @@
         for k in range(rows // slots):
             row = lax.broadcasted_iota(jnp.int32, (slots, 1), 0)
             live = (row < lengths[k]).astype(F32)
-            grad[k * slots : (k + 1) * slots] = (cotangent[k].astype(F32) * live).astype(BF16)
-
-    project_back([(5, grad)], emit_dup)
-    weight_grad(5, hid, grad)
-    scatter.core_send(5)
-    project_back([(4, dup)], put(up))
-    weight_grad(4, a2, dup)
-    scatter.core_send(4)
-    scatter.core_add(5)
-    scatter.z_step(5, 3)
-    norm_grad(1, mid, grad, emit_dmid)
-    project_back([(3, low)], put(dob))
-    weight_grad(3, ob, low)
-    scatter.core_send(3)
-    scatter.core_add(4)
-    scatter.x_send(4)
-    attention(attend_back)
-    project_back([(0, qb), (1, kb), (2, vb)], put(up))
-
-    @pl.when(s == 1)
-    def _():
-        end(0).wait_send()
-
-    norm_grad(0, hb, dmid, emit_give)
-
-    @pl.when(s == 1)
-    def _():
-        for k in range(rows // slots):
-            back(k).start()
-
-    @pl.when(s == 0)
-    def _():
-        end(1).start()
-        token_half[...] = give[:, :half]
-
-    scatter.core_add(3)
-    scatter.x_send(3)
-    for p, ref in enumerate((qb, kb, vb)):
-        weight_grad(p, a1, ref)
-        scatter.core_send(p)
-
-    totals = [jnp.sum(sums[k], 0, keepdims=True) for k in range(3)]
-    swap[0, 0] = jnp.concatenate(totals + [jnp.zeros((5, width), F32)], 0)
-    partners = (
-        device(s, z, x, 1 - c),
-        device(s, z, 1 - x, c),
-        device(s, z + 1 - 2 * (z % 2), x, c),
-        device(s, (z + 2) % NZ, x, c),
+            part = pl.ds(k * slots, slots)
+            grad[part] = (grad[part].astype(F32) * live).astype(BF16)
+
+    grads = ((a1, qb), (a1, kb), (a1, vb), (ob, low), (a2, dup), (hid, grad))
+
+    def exchange(k):
+        partner = (
+            device(s, z, x, 1 - c),
+            device(s, z, 1 - x, c),
+            device(s, z + 1 - 2 * (z % 2), x, c),
+            device(s, (z + 2) % NZ, x, c),
+        )[k]
+        return remote(swap.at[k, 0], swap.at[k, 1], swap_s.at[k], swap_r.at[k], partner)
+
+    def small(k):
+        if k == 0:
+            totals = [jnp.sum(sums[i], 0, keepdims=True) for i in range(3)]
+            swap[0, 0] = jnp.concatenate(totals + [jnp.zeros((5, width), F32)], 0)
+            exchange(0).start()
+            return
+        exchange(k - 1).wait_recv()
+        value = swap[k - 1, 0] + swap[k - 1, 1]
+        if k < 4:
+            swap[k, 0] = value
+            exchange(k).start()
+        else:
+            small_out[...] = value
+
+    def finish_input(section):
+        if section == 1:
+            end(0).wait_send()
+        norm_grad(0, hb, dmid, emit_give)
+        if section == 1:
+            for k in range(rows // slots):
+                back(k).start()
+        else:
+            end(1).start()
+            token_half[...] = give[:, :half]
+
+    compute = dict(
+        hidden=lambda section: project_back([(5, grad)], emit_dup),
+        normed_two=lambda section: project_back([(4, dup)], put(up)),
+        middle=lambda section: norm_grad(1, mid, grad, emit_dmid),
+        attended=lambda section: project_back([(3, low)], put(dob)),
+        heads=lambda section, k: attention(attend_back, k, k + 1),
+        normed=lambda section: project_back([(0, qb), (1, kb), (2, vb)], put(up)),
+        input=finish_input,
+        weight=lambda section, p: weight_grad(p, *grads[p]),
+        small=lambda section, k: small(k),
     )
 
-    def exchange(k):
-        return remote(swap.at[k, 0], swap.at[k, 1], swap_s.at[k], swap_r.at[k], partners[k])
-
-    exchange(0).start()
-    for d in (2, 1):
-        scatter.z_step(5, d)
-    scatter.close(5)
-    order_out = [4, 3, 0, 1, 2]
-    for k, p in enumerate(order_out):
-        if k + 2 < len(order_out):
-            scatter.core_add(order_out[k + 2])
-            scatter.x_send(order_out[k + 2])
-        if k < 4:
-            exchange(k).wait_recv()
-            if k < 3:
-                swap[k + 1, 0] = swap[k, 0] + swap[k, 1]
-                exchange(k + 1).start()
+    def backward(section):
+        for step in BACKWARD_STEPS[section]:
+            if step[0] in compute:
+                compute[step[0]](section, *step[1:])
             else:
-                small_out[...] = swap[k, 0] + swap[k, 1]
-        scatter.serve(p)
+                getattr(scatter, step[0])(*step[1:])
+
+    pl.when(s == 0)(lambda: backward(0))
+    pl.when(s == 1)(lambda: backward(1))
     for p in range(PIECES):
         scatter.drain(p)
     for k in range(4):
@@ -732,11 +963,12 @@
         dup=low_rows,
         dmid=wide_rows,
         low=low_rows,
+        dob=low_rows,
         give=low_rows,
         sums=pltpu.VMEM((3, 8, width), F32),
         swap=pltpu.VMEM((4, 2, 8, width), F32),
         got_core=pltpu.VMEM((PIECES, 2 * NZ) + block, BF16),
-        got_x=pltpu.VMEM((PIECES, NZ) + block, BF16),
+        got_x=pltpu.VMEM(((PIECES - 1) * NZ + 1,) + block, BF16),
         got_z=pltpu.VMEM((PIECES - 1, NZ + 1) + block, BF16),
         got_zz=pltpu.VMEM((2, NZ + 1) + block, BF16),
     )
@@ -759,6 +991,7 @@
         dma((count,)),
         dma((2,)),
         dma((2,)),
+        dma((count,)),
     ]
     half = jax.ShapeDtypeStruct((rows, width // 2), BF16)
     out, d_tokens, d_q, d_o, d_u, d_d, small = pl.pallas_call(
@@ -772,7 +1005,7 @@
             jax.ShapeDtypeStruct(block, F32),
             jax.ShapeDtypeStruct((8, width), F32),
         ),
-        in_specs=[whole, whole, pl.BlockSpec(memory_space=pltpu.SMEM)] + [whole] * 6,
+        in_specs=[pl.BlockSpec(memory_space=pl.ANY)] * 2 + [pl.BlockSpec(memory_space=pltpu.SMEM)] + [whole] * 6,
         out_specs=(whole,) * 7,
         scratch_shapes=list(scratch.values()) + semaphores,
         compiler_params=pltpu.CompilerParams(

time: 369 us -> 324 us (0.88)
  the two profiles are of different devices: /device:TPU:0 before, /device:TPU:17 now
where the time goes in v3:
time: 324 us; the launch traced here: 318 us
  Pallas kernels  304 us (94%)
  local copies, waits for them, and re-layouts  10.1 us (3%)
    pallas_call x1, Pallas kernels, near_shards(): pl.pallas_call(lambda *refs: layers_kernel(n, *refs), out_shape=(half, ha...  304 us
    unnamed x16, local copies, waits for them, and re-layouts  6.98 us

profile of v3, /device:TPU:17, one launch (start us, length us, event | category | flops | bytes accessed | tf_op | source)
XLA Modules:
  0.0 317.7 jit_solution(191060712395967947)
XLA Ops:
  0.6 0.7 convert_bitcast_fusion
  1.3 0.7 fusion.1
  2.0 0.6 pad_convert_fusion.refs_3_
  2.6 0.1 tile.15
  2.7 0.6 tile.16.refs_4_
  3.3 0.0 copy-start.4
  3.3 304.0 %two_layers.1 = (bf16[256,640]{1,0:T(8,128)(2,1)}, bf16[256,640]{1,0:T(8,128)(2,1)}, f32[80,3840]{1,0:T(8,128)}, f32[80,1280]{1,0:T(8,128)}, f32[80,1280]{1,0:T(...) custom-call(bf16[2,128,1280]{2,1,0:T(8,128)(2,1)} %refs_0_.1, bf16[2,128,1280]{2,1,0:T(8,128)(2,1)} %refs_1_.1, s32[2]{0:T(128)} %refs_2_.1, ...), custom_call_target="tpu_custom_call" | custom-call | tf_op jit(solution)/shard_map/two_layers/pallas_call | solution.py:997
  307.3 0.0 copy-start
  307.3 0.9 slice_reduce_fusion
  308.2 0.8 slice.6
  309.0 0.6 dynamic-slice_bitcast_fusion
  309.6 0.1 reshape_squeeze.3
  309.7 0.0 copy-done.4
  309.7 0.5 fusion.2
  310.2 1.7 copy.23
  312.0 1.7 copy.24
  313.7 0.0 copy-done
  313.7 0.0 copy-start.3
  313.7 0.0 copy-start.2
  313.7 1.0 copy.25
  314.7 0.2 copy-done.3
  315.0 0.0 copy-start.1
  315.0 0.8 copy.26
  315.7 0.0 copy-done.2
  315.7 0.8 copy.27
  316.5 0.0 copy-done.1
  316.5 0.8 copy.28
  (2 shorter events, 0.0 us)
Async XLA Ops:
  3.3 306.4 %copy-start.4 = (f32[1,80]{1,0:T(1,128)S(1)}, f32[1,80]{1,0:T(1,128)}, u32[]{:S(2)}) copy-start(f32[1,80]{1,0:T(1,128)} %param.17) | copy-start | bytes 964
  307.3 6.4 %copy-start = (f32[80,3840]{1,0:T(8,128)S(1)}, f32[80,3840]{1,0:T(8,128)}, u32[]{:S(2)}) copy-start(f32[80,3840]{1,0:T(8,128)} %get-tuple-element.17) | copy-start | bytes 3686404
  313.7 1.3 copy-start.3
  313.7 2.0 copy-start.2
  315.0 1.5 copy-start.1

commit v4 on v3

--- a/solution.py
+++ b/solution.py
@@ -23,8 +23,12 @@
 TILE = 256
 PIECES = 6
 GAINS = 6
-FIRST_IN = 5
-FIRST_OUT = 4
+LENT = 7
+LENT_IN = 5
+TURN_IN = (4, 5)
+LENT_OUT = 5
+LENT_SUM = 6
+TURN_OUT = (4, 4)
 
 
 def place():
@@ -66,257 +70,330 @@
 
 
 GATHER_STEPS = (
-    ("own", 5),
-    ("own", 6),
-    ("own", 1),
-    ("own", 0),
-    ("relay", 0, 1, (-1,)),
-    ("relay", 1, 1, (1,)),
-    ("relay", 6, 1, (-1,)),
-    ("relay", 6, 1, (1,)),
-    ("relay", 6, 2, (-1,)),
-    ("relay", 6, 2, (1,)),
-    ("own", 2),
-    ("relay", 0, 1, (1,)),
-    ("relay", 0, 2, (-1,)),
-    ("relay", 6, 3, (1,)),
-    ("relay", 6, 3, (-1,)),
-    ("across", 6, 0),
-    ("relay", 1, 1, (-1,)),
-    ("relay", 2, 1, (1,)),
-    ("relay", 1, 2, (1,)),
-    ("relay", 1, 2, (-1,)),
-    ("across", 6, 1),
-    ("relay", 0, 2, (1,)),
-    ("relay", 0, 3, (1,)),
-    ("across", 6, 2),
-    ("relay", 1, 3, (-1,)),
-    ("relay", 1, 3, (1,)),
-    ("across", 1, 0),
-    ("across", 6, 3),
-    ("relay", 0, 3, (-1,)),
-    ("across", 0, 0),
-    ("across", 0, 1),
-    ("turn", 5),
-    ("across", 1, 1),
-    ("relay", 2, 1, (-1,)),
-    ("relay", 2, 2, (-1,)),
-    ("relay", 5, 1, (-1,)),
-    ("relay", 2, 2, (1,)),
-    ("own", 3),
-    ("relay", 2, 3, (-1,)),
-    ("relay", 2, 3, (1,)),
-    ("across", 0, 2),
-    ("across", 0, 3),
-    ("relay", 3, 1, (1,)),
-    ("finish", 6),
-    ("finish", 0),
-    ("relay", 3, 1, (-1,)),
-    ("across", 2, 0),
-    ("across", 2, 1),
-    ("across", 2, 2),
-    ("across", 1, 2),
-    ("across", 1, 3),
-    ("relay", 3, 2, (-1,)),
-    ("relay", 3, 2, (1,)),
-    ("across", 2, 3),
-    ("relay", 5, 1, (1,)),
-    ("own", 4),
-    ("finish", 1),
-    ("relay", 4, 1, (-1,)),
-    ("relay", 4, 1, (1,)),
-    ("relay", 3, 3, (-1,)),
-    ("finish", 2),
-    ("relay", 3, 3, (1,)),
-    ("relay", 4, 2, (1,)),
-    ("relay", 5, 2, (1,)),
-    ("across", 3, 0),
-    ("across", 3, 1),
-    ("relay", 4, 2, (-1,)),
-    ("across", 3, 2),
-    ("relay", 5, 2, (-1,)),
-    ("across", 3, 3),
-    ("relay", 4, 3, (1,)),
-    ("relay", 4, 3, (-1,)),
-    ("across", 4, 0),
-    ("finish", 3),
-    ("across", 4, 1),
-    ("across", 4, 2),
-    ("across", 4, 3),
-    ("relay", 5, 3, (1,)),
-    ("relay", 5, 3, (-1,)),
-    ("finish", 4),
-    ("finish", 5),
+    (
+        ("own", 0),
+        ("own", 2),
+        ("own", 6),
+        ("own", 4),
+        ("own", 5),
+        ("relay", 2, 1, (-1,)),
+        ("own", 1),
+        ("relay", 0, 1, (-1,)),
+        ("relay", 0, 1, (1,)),
+        ("relay", 0, 2, (-1,)),
+        ("relay", 6, 1, (1,)),
+        ("relay", 6, 1, (-1,)),
+        ("relay", 2, 1, (1,)),
+        ("relay", 6, 2, (1,)),
+        ("relay", 1, 1, (-1,)),
+        ("relay", 0, 2, (1,)),
+        ("relay", 0, 3, (-1,)),
+        ("relay", 6, 2, (-1,)),
+        ("relay", 6, 3, (-1,)),
+        ("relay", 1, 1, (1,)),
+        ("relay", 1, 2, (-1,)),
+        ("turn", 4),
+        ("relay", 1, 2, (1,)),
+        ("relay", 1, 3, (-1,)),
+        ("relay", 0, 3, (1,)),
+        ("across", 0, 0),
+        ("relay", 6, 3, (1,)),
+        ("across", 6, 0),
+        ("across", 6, 1),
+        ("relay", 2, 2, (-1,)),
+        ("relay", 2, 2, (1,)),
+        ("relay", 2, 3, (-1,)),
+        ("across", 6, 2),
+        ("across", 0, 1),
+        ("across", 6, 3),
+        ("own", 3),
+        ("relay", 2, 3, (1,)),
+        ("relay", 4, 1, (1,)),
+        ("relay", 3, 1, (-1,)),
+        ("home", 5, 0),
+        ("home", 5, 1),
+        ("relay", 1, 3, (1,)),
+        ("across", 1, 0),
+        ("across", 2, 0),
+        ("home", 5, 2),
+        ("across", 1, 1),
+        ("relay", 4, 1, (-1,)),
+        ("relay", 4, 2, (1,)),
+        ("across", 1, 2),
+        ("across", 2, 1),
+        ("finish", 6),
+        ("home", 5, 3),
+        ("across", 2, 2),
+        ("across", 2, 3),
+        ("across", 1, 3),
+        ("relay", 4, 2, (-1,)),
+        ("across", 0, 2),
+        ("across", 0, 3),
+        ("finish", 0),
+        ("stage", 0),
+        ("relay", 3, 1, (1,)),
+        ("finish", 5),
+        ("relay", 3, 2, (-1,)),
+        ("finish", 1),
+        ("stage", 1),
+        ("finish", 2),
+        ("relay", 4, 3, (-1,)),
+        ("relay", 4, 3, (1,)),
+        ("finish", 4),
+        ("relay", 3, 2, (1,)),
+        ("relay", 3, 3, (-1,)),
+        ("relay", 3, 3, (1,)),
+        ("across", 3, 0),
+        ("stage", 2),
+        ("across", 3, 1),
+        ("across", 3, 2),
+        ("across", 3, 3),
+        ("finish", 3),
+        ("stage", 3),
+        ("stage", 4),
+        ("stage", 5),
+    ),
+    (
+        ("own", 5),
+        ("own", 0),
+        ("own", 7),
+        ("relay", 0, 1, (-1,)),
+        ("relay", 7, 1, (-1,)),
+        ("own", 6),
+        ("own", 2),
+        ("relay", 7, 1, (1,)),
+        ("relay", 6, 1, (-1,)),
+        ("relay", 7, 2, (-1,)),
+        ("relay", 6, 1, (1,)),
+        ("relay", 7, 2, (1,)),
+        ("relay", 6, 2, (-1,)),
+        ("relay", 7, 3, (-1,)),
+        ("relay", 0, 1, (1,)),
+        ("relay", 0, 2, (1,)),
+        ("turn", 5),
+        ("relay", 5, 1, (-1,)),
+        ("relay", 6, 2, (1,)),
+        ("own", 4),
+        ("relay", 7, 3, (1,)),
+        ("across", 7, 0),
+        ("own", 3),
+        ("own", 1),
+        ("across", 7, 1),
+        ("across", 7, 2),
+        ("across", 7, 3),
+        ("relay", 2, 1, (-1,)),
+        ("relay", 1, 1, (1,)),
+        ("relay", 6, 3, (1,)),
+        ("relay", 0, 2, (-1,)),
+        ("relay", 0, 3, (1,)),
+        ("relay", 1, 1, (-1,)),
+        ("relay", 0, 3, (-1,)),
+        ("relay", 2, 1, (1,)),
+        ("relay", 2, 2, (1,)),
+        ("relay", 4, 1, (1,)),
+        ("relay", 6, 3, (-1,)),
+        ("across", 6, 0),
+        ("across", 0, 0),
+        ("relay", 1, 2, (1,)),
+        ("across", 6, 1),
+        ("relay", 1, 2, (-1,)),
+        ("relay", 1, 3, (1,)),
+        ("relay", 2, 2, (-1,)),
+        ("relay", 2, 3, (1,)),
+        ("relay", 1, 3, (-1,)),
+        ("across", 6, 2),
+        ("relay", 3, 1, (1,)),
+        ("across", 0, 1),
+        ("across", 0, 2),
+        ("across", 0, 3),
+        ("relay", 3, 1, (-1,)),
+        ("relay", 5, 1, (1,)),
+        ("relay", 3, 2, (-1,)),
+        ("across", 1, 0),
+        ("relay", 2, 3, (-1,)),
+        ("relay", 3, 2, (1,)),
+        ("relay", 3, 3, (-1,)),
+        ("across", 1, 1),
+        ("across", 1, 2),
+        ("across", 2, 0),
+        ("across", 2, 1),
+        ("across", 2, 2),
+        ("across", 2, 3),
+        ("across", 1, 3),
+        ("relay", 5, 2, (-1,)),
+        ("relay", 4, 1, (-1,)),
+        ("relay", 5, 2, (1,)),
+        ("finish", 2),
+        ("relay", 4, 2, (-1,)),
+        ("finish", 1),
+        ("relay", 3, 3, (1,)),
+        ("finish", 0),
+        ("across", 3, 0),
+        ("across", 3, 1),
+        ("relay", 5, 3, (1,)),
+        ("across", 6, 3),
+        ("relay", 5, 3, (-1,)),
+        ("relay", 4, 2, (1,)),
+        ("finish", 5),
+        ("finish", 6),
+        ("across", 3, 2),
+        ("across", 3, 3),
+        ("finish", 3),
+        ("relay", 4, 3, (1,)),
+        ("relay", 4, 3, (-1,)),
+        ("across", 4, 0),
+        ("across", 4, 1),
+        ("hand",),
+        ("stage", 0),
+        ("stage", 1),
+        ("stage", 2),
+        ("across", 4, 2),
+        ("across", 4, 3),
+        ("stage", 3),
+        ("finish", 4),
+        ("stage", 4),
+        ("stage", 5),
+    ),
 )
 BACKWARD_STEPS = (
     (
         ("hidden",),
-        ("weight", 5),
-        ("core_send", 5),
         ("normed_two",),
         ("weight", 4),
         ("core_send", 4),
-        ("core_add", 5),
-        ("x_send", 5),
-        ("core_add", 4),
-        ("z_step", 4, 3, (1,)),
-        ("z_step", 4, 3, (-1,)),
         ("middle",),
         ("attended",),
-        ("heads", 0),
-        ("z_step", 4, 2, (1,)),
         ("weight", 3),
         ("core_send", 3),
-        ("z_step", 4, 2, (-1,)),
+        ("core_add", 4),
+        ("z_step", 4, 0),
+        ("core_add", 3),
+        ("weight", 5),
+        ("core_send", 5),
+        ("x_send", 3),
         ("heads", 1),
-        ("core_add", 3),
-        ("x_send", 3),
-        ("z_step", 5, 3, (1,)),
-        ("z_step", 4, 1, (1,)),
+        ("z_step", 4, 1),
+        ("heads", 0),
         ("normed",),
-        ("weight", 2),
-        ("z_step", 5, 3, (-1,)),
-        ("z_step", 4, 1, (-1,)),
-        ("z_step", 5, 2, (-1,)),
-        ("z_step", 3, 3, (-1,)),
         ("weight", 0),
+        ("z_step", 3, 0),
         ("core_send", 0),
-        ("weight", 1),
         ("core_add", 0),
         ("x_send", 0),
+        ("z_step", 4, 2),
+        ("weight", 2),
+        ("weight", 1),
+        ("core_send", 1),
+        ("core_add", 5),
+        ("lend", 0),
+        ("lend", 1),
+        ("core_add", 1),
         ("input",),
-        ("core_send", 1),
-        ("core_add", 1),
-        ("x_send", 1),
-        ("z_step", 3, 3, (1,)),
-        ("z_step", 0, 3, (-1,)),
-        ("z_step", 0, 2, (-1,)),
-        ("z_step", 3, 2, (-1,)),
+        ("z_step", 0, 0),
         ("small", 0),
         ("small", 1),
-        ("z_step", 5, 1, (-1,)),
-        ("z_step", 5, 2, (1,)),
-        ("z_step", 5, 1, (1,)),
-        ("z_step", 0, 1, (-1,)),
+        ("x_send", 1),
+        ("z_step", 0, 1),
+        ("z_step", 0, 2),
         ("core_send", 2),
+        ("z_step", 1, 0),
+        ("z_step", 3, 1),
+        ("small", 2),
         ("core_add", 2),
         ("x_send", 2),
-        ("z_step", 3, 2, (1,)),
-        ("z_step", 3, 1, (1,)),
-        ("z_step", 0, 3, (1,)),
-        ("z_step", 0, 2, (1,)),
-        ("z_step", 0, 1, (1,)),
-        ("z_step", 1, 3, (-1,)),
-        ("z_step", 3, 1, (-1,)),
-        ("z_step", 1, 3, (1,)),
-        ("z_step", 1, 2, (-1,)),
-        ("z_step", 2, 3, (-1,)),
-        ("small", 2),
+        ("close", 0),
+        ("z_step", 1, 1),
+        ("z_step", 1, 2),
+        ("z_step", 2, 0),
+        ("close", 1),
+        ("z_step", 3, 2),
+        ("z_step", 2, 1),
         ("turn", 4),
-        ("z_step", 1, 1, (-1,)),
-        ("close", 5),
-        ("z_step", 2, 2, (-1,)),
-        ("z_step", 1, 2, (1,)),
-        ("z_step", 1, 1, (1,)),
-        ("close", 3),
-        ("z_step", 2, 3, (1,)),
-        ("z_step", 2, 2, (1,)),
+        ("z_step", 2, 2),
         ("small", 3),
         ("small", 4),
-        ("close", 0),
-        ("z_step", 2, 1, (1,)),
-        ("z_step", 2, 1, (-1,)),
+        ("close", 3),
         ("close", 4),
-        ("close", 1),
         ("close", 2),
+        ("home",),
     ),
     (
         ("hidden",),
         ("normed_two",),
         ("middle",),
         ("attended",),
+        ("weight", 5),
+        ("core_send", 5),
         ("heads", 0),
+        ("core_add", 5),
+        ("x_send", 5),
         ("heads", 1),
         ("normed",),
         ("input",),
-        ("weight", 5),
-        ("core_send", 5),
+        ("weight", 3),
+        ("core_send", 3),
+        ("z_step", 5, 0),
         ("weight", 4),
         ("core_send", 4),
-        ("core_add", 5),
-        ("x_send", 5),
-        ("core_add", 4),
-        ("z_step", 4, 3, (1,)),
-        ("z_step", 4, 3, (-1,)),
-        ("z_step", 4, 2, (1,)),
-        ("weight", 3),
-        ("core_send", 3),
-        ("z_step", 4, 2, (-1,)),
         ("core_add", 3),
         ("x_send", 3),
-        ("z_step", 5, 3, (1,)),
-        ("z_step", 4, 1, (1,)),
-        ("weight", 2),
-        ("z_step", 5, 3, (-1,)),
-        ("z_step", 4, 1, (-1,)),
-        ("z_step", 5, 2, (-1,)),
-        ("z_step", 3, 3, (-1,)),
         ("weight", 0),
         ("core_send", 0),
-        ("weight", 1),
+        ("core_add", 4),
+        ("z_step", 4, 0),
         ("core_add", 0),
         ("x_send", 0),
-        ("core_send", 1),
-        ("core_add", 1),
-        ("x_send", 1),
-        ("z_step", 3, 3, (1,)),
-        ("z_step", 0, 3, (-1,)),
-        ("z_step", 0, 2, (-1,)),
-        ("z_step", 3, 2, (-1,)),
-        ("small", 0),
-        ("small", 1),
-        ("z_step", 5, 1, (-1,)),
-        ("z_step", 5, 2, (1,)),
-        ("z_step", 5, 1, (1,)),
-        ("z_step", 0, 1, (-1,)),
+        ("weight", 2),
         ("core_send", 2),
+        ("z_step", 5, 1),
         ("core_add", 2),
         ("x_send", 2),
-        ("z_step", 3, 2, (1,)),
-        ("z_step", 3, 1, (1,)),
-        ("z_step", 0, 3, (1,)),
-        ("z_step", 0, 2, (1,)),
-        ("z_step", 0, 1, (1,)),
-        ("z_step", 1, 3, (-1,)),
-        ("z_step", 3, 1, (-1,)),
-        ("z_step", 1, 3, (1,)),
-        ("z_step", 1, 2, (-1,)),
-        ("z_step", 2, 3, (-1,)),
+        ("weight", 1),
+        ("z_step", 4, 1),
+        ("core_send", 1),
+        ("small", 0),
+        ("core_add", 1),
+        ("z_step", 3, 0),
+        ("z_step", 3, 1),
+        ("z_step", 4, 2),
+        ("small", 1),
+        ("z_step", 0, 0),
+        ("z_step", 5, 2),
+        ("z_step", 2, 0),
+        ("z_step", 2, 1),
+        ("z_step", 2, 2),
+        ("x_send", 1),
+        ("z_step", 0, 1),
+        ("x_send", 6, 0, 1),
         ("small", 2),
+        ("z_step", 0, 2),
+        ("close", 2),
+        ("z_step", 3, 2),
+        ("close", 0),
+        ("z_step", 1, 0),
+        ("x_send", 6, 1, 2),
+        ("x_send", 6, 2, 3),
+        ("z_step", 6, 0),
+        ("z_step", 6, 1),
+        ("z_step", 6, 2),
+        ("x_send", 6, 3, 4),
+        ("small", 3),
+        ("z_step", 1, 1),
+        ("close", 6),
+        ("z_step", 1, 2),
         ("turn", 4),
-        ("z_step", 1, 1, (-1,)),
+        ("small", 4),
+        ("close", 3),
         ("close", 5),
-        ("z_step", 2, 2, (-1,)),
-        ("z_step", 1, 2, (1,)),
-        ("z_step", 1, 1, (1,)),
-        ("close", 3),
-        ("z_step", 2, 3, (1,)),
-        ("z_step", 2, 2, (1,)),
-        ("small", 3),
-        ("small", 4),
-        ("close", 0),
-        ("z_step", 2, 1, (1,)),
-        ("z_step", 2, 1, (-1,)),
+        ("close", 1),
         ("close", 4),
-        ("close", 1),
-        ("close", 2),
     ),
 )
 
 
 class Gather:
-    def __init__(self, where, view, sems):
-        self.where, self.view = where, view
+    def __init__(self, where, section, view, sems):
+        self.where, self.section, self.view = where, section, view
         self.send_sem, self.recv_sem, self.core_send, self.core_recv = sems
 
     def ship(self, p, zz, xx, way, cond, wait):
@@ -330,8 +407,12 @@
                 device(s, z, 1 - x, c),
             )[way]
             cp = remote(block, block, self.send_sem.at[p, i, way], self.recv_sem.at[p, i], target)
+        elif way == 3:
+            cp = remote(block, block, self.core_send.at[p, i], self.core_recv.at[p, i], device(s, z, x, 1 - c))
         else:
-            cp = remote(block, block, self.core_send.at[p, i], self.core_recv.at[p, i], device(s, z, x, 1 - c))
+            q = LENT if self.section == 0 else LENT_IN
+            there = self.view(q, zz, xx, c)
+            cp = remote(block, there, self.send_sem.at[p, i, 3], self.recv_sem.at[q, i], device(1 - s, z, x, c))
         act = cp.wait_send if wait else cp.start
         if cond is None:
             act()
@@ -346,7 +427,14 @@
 
     def own(self, p, wait=False):
         s, z, x, c = self.where
-        for way, cond in ((0, z < NZ - 1), (1, z > 0), (2, None), (3, None)):
+        ways = ((0, z < NZ - 1), (1, z > 0), (2, None), (3, None))
+        if p == LENT:
+            ways = ways[:3]
+            if not wait:
+                self.arrived(p, z, x)
+        elif self.section == 0 and p == LENT_IN:
+            ways = ((4, None), (3, None))
+        for way, cond in ways:
             self.ship(p, z, x, way, cond, wait)
 
     def turn(self, p, wait=False):
@@ -359,17 +447,18 @@
 
     def relay(self, p, d, signs=(-1, 1), wait=False):
         s, z, x, c = self.where
+        turned = p == TURN_IN[self.section]
         for sign in signs:
             way = 0 if sign < 0 else 1
             zz = clipped(z + sign * d)
             here = inside(z + sign * d)
-            for xx in (x, 1 - x) if p == FIRST_IN else (x,):
+            for xx in (x, 1 - x) if turned else (x,):
                 if not wait:
                     pl.when(here)(lambda zz=zz, xx=xx: self.arrived(p, zz, xx))
                 self.ship(p, zz, xx, way, here & inside(z - sign), wait)
-                if p != FIRST_IN:
+                if not turned:
                     self.ship(p, zz, xx, 2, here, wait)
-                self.ship(p, zz, xx, 3, here, wait)
+                self.ship(p, zz, xx, 4 if p == LENT else 3, here, wait)
 
     def across(self, p, d, wait=False):
         s, z, x, c = self.where
@@ -378,7 +467,17 @@
             here = inside(z + sign * d)
             if not wait:
                 pl.when(here)(lambda zz=zz: self.arrived(p, zz, 1 - x))
-            self.ship(p, zz, 1 - x, 3, here, wait)
+            self.ship(p, zz, 1 - x, 4 if p == LENT else 3, here, wait)
+
+    def home(self, p, d, wait=False):
+        s, z, x, c = self.where
+        for sign in (-1, 1) if d else (1,):
+            zz = clipped(z + sign * d)
+            here = inside(z + sign * d)
+            for xx in (x, 1 - x) if d else (1 - x,):
+                if not wait:
+                    pl.when(here)(lambda zz=zz, xx=xx: self.arrived(p, zz, xx))
+                self.ship(p, zz, xx, 3, here, wait)
 
     def finish(self, p):
         s, z, x, c = self.where
@@ -388,26 +487,35 @@
                 i = zz * 2 + xx
                 remote(block, block, self.core_send.at[p, i], self.core_recv.at[p, i], device(s, z, x, 1 - c)).wait_recv()
 
-    def drain(self, p):
-        self.own(p, True)
-        if p == FIRST_IN:
-            self.turn(p, True)
-        for d in range(NZ):
-            if d:
-                self.relay(p, d, wait=True)
-            if p != FIRST_IN:
-                self.across(p, d, True)
-
-
-def add_block(dst, src):
-    dst[...] = (dst[...].astype(F32) + src[...].astype(F32)).astype(BF16)
+    def drain(self):
+        for step in GATHER_STEPS[self.section]:
+            if step[0] not in ("finish", "stage", "hand"):
+                getattr(self, step[0])(*step[1:], wait=True)
+
+
+def add_into(dst, terms):
+    total = dst[...].astype(F32)
+    for ref, cond in terms:
+        value = ref[...].astype(F32)
+        total = total + (value if cond is None else jnp.where(cond, value, 0.0))
+    return total
+
+
+def farthest_first(z, k):
+    orders = ((3, 2, 1, 0), (3, 0, 2, 1), (0, 3, 1, 2), (0, 1, 2, 3))
+    return jnp.where(
+        z == 0, orders[0][k], jnp.where(z == 1, orders[1][k], jnp.where(z == 2, orders[2][k], orders[3][k]))
+    )
 
 
 class Scatter:
-    def __init__(self, where, view, bufs, sems, store):
-        self.where, self.view, self.store = where, view, store
-        self.got_core, self.got_x, self.got_z, self.got_zz = bufs
-        self.core_s, self.core_r, self.x_s, self.x_r, self.z_s, self.z_r = sems
+    def __init__(self, where, section, view, bufs, sems, store):
+        self.where, self.section, self.view, self.store = where, section, view, store
+        self.got_core, self.got_x, self.got_z, self.got_zz, self.got_home = bufs
+        self.core_s, self.core_r, self.x_s, self.x_r, self.z_s, self.z_r, self.lend_s, self.lend_r, self.home_s, self.home_r = sems
+        self.turned = TURN_OUT[section]
+        left_out = (self.turned, LENT_OUT, LENT_SUM) if section == 0 else (self.turned,)
+        self.straight = [p for p in range(PIECES + 1) if p not in left_out]
 
     def core_copy(self, p, i):
         s, z, x, c = self.where
@@ -429,10 +537,11 @@
         @pl.loop(0, 2 * NZ)
         def _(i):
             self.core_copy(p, i).wait_recv()
-            add_block(self.view(p, i // 2, i % 2, c), self.got_core.at[p, i])
+            dst = self.view(p, i // 2, i % 2, c)
+            dst[...] = add_into(dst, [(self.got_core.at[p, i], None)]).astype(BF16)
 
     def x_slot(self, p, zz):
-        return self.got_x.at[(PIECES - 1) * NZ if p == FIRST_OUT else (p - (p > FIRST_OUT)) * NZ + zz]
+        return self.got_x.at[PIECES * NZ if p == self.turned else self.straight.index(p) * NZ + zz]
 
     def x_copy(self, p, zz):
         s, z, x, c = self.where
@@ -444,24 +553,45 @@
             device(s, z, 1 - x, c),
         )
 
-    def steps(self):
-        z = self.where[1]
-        for d in range(NZ - 1, 0, -1):
-            for sign in (1, -1):
-                yield d, clipped(z + sign * d), inside(z + sign * d), sign
-
-    def x_send(self, p):
-        for _, zz, here, _ in self.steps():
-            pl.when(here)(lambda zz=zz: self.x_copy(p, zz).start())
-        self.x_copy(p, self.where[1]).start()
-
-    def x_add(self, p, zz):
-        s, z, x, c = self.where
+    def lent_copy(self, zz, xx):
+        s, z, x, c = self.where
+        i = zz * 2 + xx
+        dst = self.view(LENT_SUM, zz, xx, c)
+        src = self.view(LENT_OUT, zz, xx, c) if self.section == 0 else dst
+        return remote(src, dst, self.lend_s.at[i], self.lend_r.at[i], device(1 - s, z, x, c))
+
+    def lend(self, side, wait=False):
+        s, z, x, c = self.where
+        xx = 1 - x if side == 0 else x
+
+        for i in range(NZ):
+            cp = self.lent_copy(farthest_first(z, i), xx)
+            cp.wait_send() if wait else cp.start()
+
+    def home_copy(self):
+        s, z, x, c = self.where
+        return remote(self.view(LENT_SUM, z, x, c), self.got_home, self.home_s.at[0], self.home_r.at[0], device(1 - s, z, x, c))
+
+    def home(self):
+        self.home_copy().wait_recv()
+        self.store(LENT_OUT, self.got_home[...].astype(F32))
+
+    def x_send(self, p, first=0, last=NZ):
+        s, z, x, c = self.where
+        for i in range(first, last):
+            zz = farthest_first(z, i)
+            if p == LENT_SUM:
+                self.lent_copy(zz, 1 - x).wait_recv()
+            self.x_copy(p, zz).start()
+
+    def x_wait(self, p, zz):
+        if p == LENT_SUM:
+            self.lent_copy(zz, self.where[2]).wait_recv()
         self.x_copy(p, zz).wait_recv()
-        add_block(self.view(p, zz, x, c), self.x_slot(p, zz))
+        return self.x_slot(p, zz), None
 
     def slot(self, p, k, xx):
-        return self.got_zz.at[xx, k] if p == FIRST_OUT else self.got_z.at[p - (p > FIRST_OUT), k]
+        return self.got_zz.at[xx, k] if p == self.turned else self.got_z.at[self.straight.index(p), k]
 
     def z_copy(self, p, zz, xx, sign, k):
         s, z, x, c = self.where
@@ -479,55 +609,64 @@
 
     def cols(self, p):
         x = self.where[2]
-        return (x, 1 - x) if p == FIRST_OUT else (x,)
-
-    def z_take(self, p, zz, xx, k):
-        self.z_copy(p, zz, xx, 1, k).wait_recv()
-        add_block(self.view(p, zz, xx, self.where[3]), self.slot(p, k, xx))
-
-    def z_step(self, p, distance, signs=(1, -1)):
-        z = self.where[1]
-        for d, zz, here, sign in self.steps():
-            if d != distance or sign not in signs:
-                continue
-
-            @pl.when(here)
-            def _(zz=zz, sign=sign):
-                if p != FIRST_OUT:
-                    self.x_add(p, zz)
-                for xx in self.cols(p):
-                    pl.when(inside(z - sign))(lambda xx=xx: self.z_take(p, zz, xx, zz))
-                    self.z_out(p, zz, xx, sign).start()
+        return (x, 1 - x) if p == self.turned else (x,)
+
+    def z_wait(self, p, zz, xx, k, cond):
+        pl.when(cond)(lambda: self.z_copy(p, zz, xx, 1, k).wait_recv())
+        return self.slot(p, k, xx), cond
+
+    def z_step(self, p, k):
+        s, z, x, c = self.where
+        zz = farthest_first(z, k)
+        sign = jnp.where(zz > z, 1, -1)
+        before = inside(z - sign)
+        terms = [] if p == self.turned else [self.x_wait(p, zz)]
+        for xx in self.cols(p):
+            dst = self.view(p, zz, xx, c)
+            dst[...] = add_into(dst, terms + [self.z_wait(p, zz, xx, zz, before)]).astype(BF16)
+            self.z_out(p, zz, xx, sign).start()
 
     def z_last(self, p, xx):
         z = self.where[1]
-        pl.when(z > 0)(lambda: self.z_take(p, z, xx, z))
-        pl.when(z < NZ - 1)(lambda: self.z_take(p, z, xx, NZ))
+        return [self.z_wait(p, z, xx, z, z > 0), self.z_wait(p, z, xx, NZ, z < NZ - 1)]
 
     def turn(self, p):
         s, z, x, c = self.where
-        self.z_last(p, 1 - x)
+        dst = self.view(p, z, 1 - x, c)
+        dst[...] = add_into(dst, self.z_last(p, 1 - x)).astype(BF16)
         self.x_copy(p, z).start()
 
     def close(self, p):
         s, z, x, c = self.where
-        if p == FIRST_OUT:
-            self.z_last(p, x)
-            self.x_add(p, z)
+        dst = self.view(p, z, x, c)
+        total = add_into(dst, [self.x_wait(p, z)] + self.z_last(p, x))
+        if p == LENT_SUM:
+            dst[...] = total.astype(BF16)
+            self.home_copy().start()
         else:
-            self.x_add(p, z)
-            self.z_last(p, x)
-        self.store(p, self.view(p, z, x, c))
-
-    def drain(self, p):
-        for i in range(2 * NZ):
-            self.core_copy(p, i).wait_send()
-        for _, zz, here, sign in self.steps():
-            if p != FIRST_OUT:
-                pl.when(here)(lambda zz=zz: self.x_copy(p, zz).wait_send())
+            self.store(p, total)
+
+    def drain(self):
+        for p in range(PIECES):
+            for i in range(2 * NZ):
+                self.core_copy(p, i).wait_send()
+        for p in self.straight + [self.turned]:
+            self.drain_links(p)
+        if self.section == 0:
+            self.lend(0, True)
+            self.lend(1, True)
+        else:
+            self.home_copy().wait_send()
+
+    def drain_links(self, p):
+        z = self.where[1]
+        for i in range(NZ - 1):
+            zz = farthest_first(z, i)
+            if p != self.turned:
+                self.x_copy(p, zz).wait_send()
             for xx in self.cols(p):
-                pl.when(here)(lambda zz=zz, xx=xx, sign=sign: self.z_out(p, zz, xx, sign).wait_send())
-        self.x_copy(p, self.where[1]).wait_send()
+                self.z_out(p, zz, xx, jnp.where(zz > z, 1, -1)).wait_send()
+        self.x_copy(p, z).wait_send()
 
 
 def head_windows():
@@ -543,8 +682,8 @@
     tokens,
     cotangent,
     lengths,
-    gain_block,
-    scale,
+    norm_gains,
+    query_gain,
     wq,
     wo,
     wu,
@@ -557,8 +696,10 @@
     d_d,
     small_out,
     held,
+    lent,
     gain_all,
     gain_rows,
+    query_block,
     hb,
     a1,
     qf,
@@ -583,6 +724,7 @@
     got_x,
     got_z,
     got_zz,
+    got_home,
     *sems,
 ):
     where = s, z, x, c = place()
@@ -590,27 +732,38 @@
     slots = cotangent.shape[1]
     half = width // 2
     group = 8 * HD
-    g_sems, r_sems = sems[:4], sems[4:10]
-    swap_s, swap_r, hand_s, hand_r, back_s, back_r, end_s, end_r, load_sem = sems[10:]
+    factor = LOG_BASE / math.sqrt(HD)
+    g_sems, r_sems = sems[:4], sems[4:14]
+    swap_s, swap_r, hand_s, hand_r, back_s, back_r, end_s, end_r, load_sem, out_sem = sems[14:]
     across_y = device(1 - s, z, x, c)
-
-    def weight_view(p, zz, xx, cc):
-        return held.at[p, pl.ds(pl.multiple_of((zz * 4 + xx * 2 + cc) * n, 16), n)]
 
     def view(p, zz, xx, cc):
         if p == GAINS:
             return gain_all.at[zz * 4 + xx * 2 + cc]
-        return weight_view(p, zz, xx, cc)
-
-    def store(p, block):
-        value = block[...].astype(F32)
-        if p < 3:
-            d_q[:, p * width : (p + 1) * width] = value
-        else:
-            (d_o, d_u, d_d)[p - 3][...] = value
-
-    gather = Gather(where, view, g_sems)
-    scatter = Scatter(where, weight_view, (got_core, got_x, got_z, got_zz), r_sems, store)
+        if p == LENT:
+            return lent.at[zz * 2 + xx]
+        return held.at[p, pl.ds(pl.multiple_of((zz * 4 + xx * 2 + cc) * n, 16), n)]
+
+    def sum_view(p, zz, xx, cc):
+        return view(LENT if p == LENT_SUM else p, zz, xx, cc)
+
+    def staged(p):
+        return (qf if p < 3 else mid).at[pl.ds(p % 3 * n, n)]
+
+    def in_hbm(p, first, others):
+        return first.at[:, pl.ds(p * width, width)] if p < 3 else others[p - 3]
+
+    def store_copy(p):
+        return pltpu.make_async_copy(staged(p), in_hbm(p, d_q, (d_o, d_u, d_d)), out_sem.at[p])
+
+    def store(p, value):
+        staged(p)[...] = value
+        store_copy(p).start()
+
+    gathers = [Gather(where, k, view, g_sems) for k in range(2)]
+    scatters = [
+        Scatter(where, k, sum_view, (got_core, got_x, got_z, got_zz, got_home), r_sems, store) for k in range(2)
+    ]
 
 
     def row_loop(fn):
@@ -653,7 +806,7 @@
 
     def emit_query(lanes, value):
         qf[:, lanes] = value
-        qb[:, lanes] = (value * scale[0:1, lanes]).astype(BF16)
+        qb[:, lanes] = (value * gain_rows[2:3, lanes]).astype(BF16)
 
     def emit_up(lanes, value):
         up[:, lanes] = value
@@ -718,7 +871,7 @@
             lanes = pl.ds(pl.multiple_of(g * group + k * 128, 128), 128)
             products = t_q[k] * qf[r, lanes]
             sums[2, :, lanes] += jnp.sum(products.reshape(slots // 8, 8, 128), 0)
-            qb[r, lanes] = (t_q[k] * scale[0:1, lanes]).astype(BF16)
+            qb[r, lanes] = (t_q[k] * gain_rows[2:3, lanes]).astype(BF16)
             kb[r, lanes] = t_k[k].astype(BF16)
             vb[r, lanes] = t_v[k].astype(BF16)
 
@@ -743,13 +896,42 @@
     def emit_give(r, value):
         give[r] = value.astype(BF16)
 
+    def window_of(k, size):
+        start = min(size * k // 128 * 128, width - 256)
+        return start, size * k - start
+
+    def rolled(block, shift):
+        return pltpu.roll(block, shift, 1) if shift else block
+
     def spread_gains():
         gain_rows[...] = jnp.zeros_like(gain_rows)
+        none = jnp.zeros((8, 128), F32)
         for f in range(4 * NZ):
-            start = min(n * f // 128 * 128, width - 256)
-            block = jnp.concatenate([gain_all[f], jnp.zeros((8, 128), F32)], -1)
-            block = pltpu.roll(block, n * f - start, 1) if n * f > start else block
-            gain_rows[:, start : start + 256] += block
+            start, shift = window_of(f, n)
+            gain_rows[:, start : start + 256] += rolled(jnp.concatenate([gain_all[f], none], -1), shift)
+        value = query_block[...]
+        scale = (jnp.maximum(value, 0.0) + jnp.log1p(jnp.exp(-jnp.abs(value)))) * factor
+        lane = lax.broadcasted_iota(jnp.int32, (8, 128), 1)
+        row = lax.broadcasted_iota(jnp.int32, (8, 128), 0)
+        scale = jnp.where((lane < HD) & (row == 2), scale, 0.0)
+        for k in range(H):
+            start, shift = window_of(k, HD)
+            gain_rows[:, start : start + 256] += rolled(jnp.concatenate([scale, none], -1), shift)
+
+    def finish_small(value):
+        me = z * 4 + x * 2 + c
+        own = jnp.zeros((8, 128), F32)
+        for f in range(4 * NZ):
+            start, shift = window_of(f, n)
+            part = rolled(value[:, start : start + 256], (256 - shift) % 256)[:, :128]
+            own = own + jnp.where(me == f, part, 0.0)
+        heads = jnp.zeros((8, 128), F32)
+        for k in range(H):
+            start, shift = window_of(k, HD)
+            heads = heads + rolled(value[:, start : start + 256], (256 - shift) % 256)[:, :128]
+        gate = factor / (1.0 + jnp.exp(-query_block[...]))
+        row = lax.broadcasted_iota(jnp.int32, (8, 128), 0)
+        small_out[...] = jnp.where(row == 2, heads * gate, own)
 
     def forward_stage(p):
         if p == 0:
@@ -783,69 +965,57 @@
         return remote(give.at[:, col : col + half], dst, end_s.at[which], end_r.at[which], across_y)
 
 
+    def load(act):
+        for k in range(rows // slots):
+            r = pl.ds(k * slots, slots)
+            here = pltpu.make_async_copy(tokens.at[k], hb.at[r], load_sem.at[k])
+            there = pltpu.make_async_copy(cotangent.at[k], grad.at[r], load_sem.at[k])
+            pl.when(s == 0)(getattr(here, act))
+            pl.when(s == 1)(getattr(there, act))
+        for p in range(PIECES):
+            cp = pltpu.make_async_copy(in_hbm(p, wq, (wo, wu, wd)), staged(p), load_sem.at[rows // slots + p])
+            getattr(cp, act)()
+
+    load("start")
+    me = z * 4 + x * 2 + c
+    gain_all[me] = jnp.zeros((8, 128), F32)
+    gain_all[me, 0:2, 0:n] = norm_gains[...].astype(BF16).astype(F32)
+    query_block[...] = jnp.zeros_like(query_block)
+    query_block[:, 0:HD] = jnp.broadcast_to(query_gain[...], (8, HD))
+    sums[...] = jnp.zeros_like(sums)
+    neighbour_barrier(s, z, x, c)
+    load("wait")
     mine = pl.ds(pl.multiple_of((z * 4 + x * 2 + c) * n, 16), n)
-    for k in range(3):
-        held[k, mine] = wq[:, k * width : (k + 1) * width].astype(BF16)
-    for k, ref in enumerate((wo, wu, wd)):
-        held[3 + k, mine] = ref[...].astype(BF16)
-    gain_all[z * 4 + x * 2 + c] = gain_block[...]
-    sums[...] = jnp.zeros_like(sums)
-    def load(k, wait=False):
-        r = pl.ds(k * slots, slots)
-
-        def first():
-            cp = pltpu.make_async_copy(tokens.at[k], hb.at[r], load_sem.at[k])
-            cp.wait() if wait else cp.start()
-
-        def second():
-            cp = pltpu.make_async_copy(cotangent.at[k], grad.at[r], load_sem.at[k])
-            cp.wait() if wait else cp.start()
-
-        pl.when(s == 0)(first)
-        pl.when(s == 1)(second)
-
-    for k in range(rows // slots):
-        load(k)
-    neighbour_barrier(s, z, x, c)
-    for k in range(rows // slots):
-        load(k, True)
-
-    def gather_steps(steps):
-        for step in steps:
-            getattr(gather, step[0])(*step[1:])
-
-    @pl.loop(0, 2)
-    def _(phase):
-        @pl.when((phase == 1) & (s == 1))
-        def _():
-            for k in range(rows // slots):
-                hand(k).wait_recv()
-
-        run = []
-        for step in GATHER_STEPS:
-            run.append(step)
-            if step[0] == "finish":
-                now, run = run, []
-                pl.when(phase == 0)(lambda: gather_steps(now))
-                if step[1] != GAINS:
-                    pl.when(phase == s)(lambda: forward_stage(step[1]))
-
-        @pl.when((phase == 0) & (s == 0))
-        def _():
-            for k in range(rows // slots):
-                hand(k).start()
-
-    for p in range(PIECES + 1):
-        gather.drain(p)
+    for p in range(PIECES):
+        held[p, mine] = staged(p)[...].astype(BF16)
+
+    def forward(section):
+        for step in GATHER_STEPS[section]:
+            if step[0] == "stage":
+                forward_stage(step[1])
+            elif step[0] == "hand":
+                for k in range(rows // slots):
+                    hand(k).wait_recv()
+            else:
+                getattr(gathers[section], step[0])(*step[1:])
+
+    def hand_start():
+        for k in range(rows // slots):
+            hand(k).start()
 
     @pl.when(s == 0)
     def _():
+        forward(0)
+        hand_start()
+        gathers[0].drain()
         for k in range(rows // slots):
             hand(k).wait_send()
             back(k).wait_recv()
 
     @pl.when(s == 1)
     def _():
+        forward(1)
+        gathers[1].drain()
         end(0).start()
         out_half[...] = give[:, half:]
         for k in range(rows // slots):
@@ -877,7 +1047,7 @@
             swap[k, 0] = value
             exchange(k).start()
         else:
-            small_out[...] = value
+            finish_small(value)
 
     def finish_input(section):
         if section == 1:
@@ -907,12 +1077,14 @@
             if step[0] in compute:
                 compute[step[0]](section, *step[1:])
             else:
-                getattr(scatter, step[0])(*step[1:])
+                getattr(scatters[section], step[0])(*step[1:])
 
     pl.when(s == 0)(lambda: backward(0))
     pl.when(s == 1)(lambda: backward(1))
+    pl.when(s == 0)(scatters[0].drain)
+    pl.when(s == 1)(scatters[1].drain)
     for p in range(PIECES):
-        scatter.drain(p)
+        store_copy(p).wait()
     for k in range(4):
         exchange(k).wait_send()
 
@@ -926,6 +1098,21 @@
         for k in range(rows // slots):
             back(k).wait_send()
         end(1).wait_recv()
+
+
+def finish_kernel(small, *refs):
+    froms, tos, (d_gains, d_query), held, (in_sem, out_sem) = refs[:6], refs[6:12], refs[12:14], refs[14:20], refs[20:]
+    ins = [pltpu.make_async_copy(a, h, in_sem.at[k]) for k, (a, h) in enumerate(zip(froms, held))]
+    outs = [pltpu.make_async_copy(h, b, out_sem.at[k]) for k, (h, b) in enumerate(zip(held, tos))]
+    for cp in ins:
+        cp.start()
+    d_gains[...] = small[0:2, : d_gains.shape[1]]
+    d_query[...] = small[2:3, :HD]
+    for came, goes in zip(ins, outs):
+        came.wait()
+        goes.start()
+    for cp in outs:
+        cp.wait()
 
 
 def near_shards(
@@ -934,19 +1121,18 @@
     n, width = out_weight.shape
     count, slots, _ = tokens.shape
     rows = count * slots
-    factor = LOG_BASE / math.sqrt(HD)
-    scale = jnp.tile(jax.nn.softplus(query_gain) * factor, (8, H))
-    gains = norm_gains.astype(BF16).astype(F32).T
-    gain_block = jnp.pad(gains, ((0, 6), (0, 128 - n)))
     dma = pltpu.SemaphoreType.DMA
     whole = pl.BlockSpec(memory_space=pltpu.VMEM)
+    far = pl.BlockSpec(memory_space=pl.ANY)
     block = (n, width)
     low_rows = pltpu.VMEM((rows, width), BF16)
     wide_rows = pltpu.VMEM((rows, width), F32)
     scratch = dict(
         held=pltpu.VMEM((PIECES, 4 * NZ * n, width), BF16),
+        lent=pltpu.VMEM((2 * NZ,) + block, BF16),
         gain_all=pltpu.VMEM((4 * NZ, 8, 128), F32),
         gain_rows=pltpu.VMEM((8, width), F32),
+        query_block=pltpu.VMEM((8, 128), F32),
         hb=low_rows,
         a1=low_rows,
         qf=wide_rows,
@@ -968,21 +1154,27 @@
         sums=pltpu.VMEM((3, 8, width), F32),
         swap=pltpu.VMEM((4, 2, 8, width), F32),
         got_core=pltpu.VMEM((PIECES, 2 * NZ) + block, BF16),
-        got_x=pltpu.VMEM(((PIECES - 1) * NZ + 1,) + block, BF16),
-        got_z=pltpu.VMEM((PIECES - 1, NZ + 1) + block, BF16),
+        got_x=pltpu.VMEM((PIECES * NZ + 1,) + block, BF16),
+        got_z=pltpu.VMEM((PIECES, NZ + 1) + block, BF16),
         got_zz=pltpu.VMEM((2, NZ + 1) + block, BF16),
+        got_home=pltpu.VMEM(block, BF16),
     )
+    pieces = PIECES + 2
     semaphores = [
-        dma((PIECES + 1, 2 * NZ, 3)),
-        dma((PIECES + 1, 2 * NZ)),
-        dma((PIECES + 1, 2 * NZ)),
-        dma((PIECES + 1, 2 * NZ)),
+        dma((pieces, 2 * NZ, 4)),
+        dma((pieces, 2 * NZ)),
+        dma((pieces, 2 * NZ)),
+        dma((pieces, 2 * NZ)),
         dma((PIECES, 2 * NZ)),
         dma((PIECES, 2 * NZ)),
-        dma((PIECES, NZ)),
-        dma((PIECES, NZ)),
-        dma((PIECES, 2, NZ)),
-        dma((PIECES, 2, NZ + 1)),
+        dma((PIECES + 1, NZ)),
+        dma((PIECES + 1, NZ)),
+        dma((PIECES + 1, 2, NZ)),
+        dma((PIECES + 1, 2, NZ + 1)),
+        dma((2 * NZ,)),
+        dma((2 * NZ,)),
+        dma((1,)),
+        dma((1,)),
         dma((4,)),
         dma((4,)),
         dma((count,)),
@@ -991,31 +1183,32 @@
         dma((count,)),
         dma((2,)),
         dma((2,)),
-        dma((count,)),
+        dma((count + PIECES,)),
+        dma((PIECES,)),
     ]
     half = jax.ShapeDtypeStruct((rows, width // 2), BF16)
-    out, d_tokens, d_q, d_o, d_u, d_d, small = pl.pallas_call(
+    square = jax.ShapeDtypeStruct(block, F32)
+    shapes = (half, half, jax.ShapeDtypeStruct((n, 3 * width), F32), square, square, square)
+    *results, small = pl.pallas_call(
         lambda *refs: layers_kernel(n, *refs),
-        out_shape=(
-            half,
-            half,
-            jax.ShapeDtypeStruct((n, 3 * width), F32),
-            jax.ShapeDtypeStruct(block, F32),
-            jax.ShapeDtypeStruct(block, F32),
-            jax.ShapeDtypeStruct(block, F32),
-            jax.ShapeDtypeStruct((8, width), F32),
-        ),
-        in_specs=[pl.BlockSpec(memory_space=pl.ANY)] * 2 + [pl.BlockSpec(memory_space=pltpu.SMEM)] + [whole] * 6,
-        out_specs=(whole,) * 7,
+        out_shape=shapes + (jax.ShapeDtypeStruct((8, 128), F32),),
+        in_specs=[far, far, pl.BlockSpec(memory_space=pltpu.SMEM), whole, whole] + [far] * 4,
+        out_specs=(whole, whole) + (far,) * 4 + (whole,),
         scratch_shapes=list(scratch.values()) + semaphores,
         compiler_params=pltpu.CompilerParams(
             collective_id=1, has_side_effects=True, vmem_limit_bytes=63 << 20
         ),
         name="two_layers",
-    )(tokens, cotangent, lengths, gain_block, scale, qkv_weight, out_weight, up_weight, down_weight)
-    own = lax.dynamic_slice_in_dim(small[:2], lax.axis_index("fsdp") * n, n, 1).T
-    d_scale = jnp.sum(small[2].reshape(H, HD), 0)
-    d_query_gain = (d_scale * jax.nn.sigmoid(query_gain[0]) * factor)[None]
+    )(tokens, cotangent, lengths, norm_gains.T, query_gain, qkv_weight, out_weight, up_weight, down_weight)
+    out, d_tokens, d_q, d_o, d_u, d_d, d_gains, d_query = pl.pallas_call(
+        finish_kernel,
+        out_shape=shapes + (jax.ShapeDtypeStruct((2, n), F32), jax.ShapeDtypeStruct((1, HD), F32)),
+        in_specs=[whole] + [far] * 6,
+        out_specs=(far,) * 6 + (whole,) * 2,
+        scratch_shapes=[pltpu.VMEM(item.shape, item.dtype) for item in shapes] + [dma((6,)), dma((6,))],
+        compiler_params=pltpu.CompilerParams(vmem_limit_bytes=63 << 20),
+        name="results",
+    )(small, *results)
     shape = (count, slots, width // 2)
     return (
         out.reshape(shape),
@@ -1024,8 +1217,8 @@
         d_o[None],
         d_u[None],
         d_d[None],
-        own[None],
-        d_query_gain,
+        d_gains.T[None],
+        d_query,
     )
 
 

time: 324 us -> 303 us (0.935)
  the two profiles are of different devices: /device:TPU:17 before, /device:TPU:0 now
where the time goes in v4:
time: 303 us; the launch traced here: 297 us
  Pallas kernels  296 us (98%)
    pallas_call x1, Pallas kernels, near_shards(): pl.pallas_call(lambda *refs: layers_kernel(n, *refs), out_shape=shapes +...  291 us

profile of v4, /device:TPU:0, one launch (start us, length us, event | category | flops | bytes accessed | tf_op | source)
XLA Modules:
  0.0 296.7 jit_solution(10264042147699080325)
XLA Ops:
  0.6 291.5 %two_layers.1 = (bf16[256,640]{1,0:T(8,128)(2,1)}, bf16[256,640]{1,0:T(8,128)(2,1)}, f32[80,3840]{1,0:T(8,128)}, f32[80,1280]{1,0:T(8,128)}, f32[80,1280]{1,0:T(...) custom-call(bf16[2,128,1280]{2,1,0:T(8,128)(2,1)} %refs_0_.1, bf16[2,128,1280]{2,1,0:T(8,128)(2,1)} %refs_1_.1, s32[2]{0:T(128)} %refs_2_.1, ...), custom_call_target="tpu_custom_call" | custom-call | tf_op jit(solution)/shard_map/two_layers/pallas_call | solution.py:1192
  292.1 4.3 %results.1 = (bf16[256,640]{1,0:T(8,128)(2,1)}, bf16[256,640]{1,0:T(8,128)(2,1)}, f32[80,3840]{1,0:T(8,128)}, f32[80,1280]{1,0:T(8,128)}, f32[80,1280]{1,0:T(8,1...) custom-call(f32[8,128]{1,0:T(8,128)} %get-tuple-element.23.small, ...), custom_call_target="tpu_custom_call" | custom-call | tf_op jit(solution)/shard_map/results/pallas_call | solution.py:1203

commit v5 on v4

--- a/solution.py
+++ b/solution.py
@@ -271,9 +271,8 @@
         ("weight", 5),
         ("core_send", 5),
         ("x_send", 3),
-        ("heads", 1),
         ("z_step", 4, 1),
-        ("heads", 0),
+        ("heads",),
         ("normed",),
         ("weight", 0),
         ("z_step", 3, 0),
@@ -324,10 +323,9 @@
         ("attended",),
         ("weight", 5),
         ("core_send", 5),
-        ("heads", 0),
         ("core_add", 5),
         ("x_send", 5),
-        ("heads", 1),
+        ("heads",),
         ("normed",),
         ("input",),
         ("weight", 3),
@@ -493,12 +491,15 @@
                 getattr(self, step[0])(*step[1:], wait=True)
 
 
-def add_into(dst, terms):
-    total = dst[...].astype(F32)
-    for ref, cond in terms:
-        value = ref[...].astype(F32)
-        total = total + (value if cond is None else jnp.where(cond, value, 0.0))
-    return total
+def add_into(out, dst, terms):
+    @pl.loop(0, dst.shape[0] // 16)
+    def _(k):
+        r = pl.ds(pl.multiple_of(k * 16, 16), 16)
+        total = dst[r].astype(F32)
+        for ref, cond in terms:
+            value = ref[r].astype(F32)
+            total = total + (value if cond is None else jnp.where(cond, value, 0.0))
+        out[r] = total.astype(out.dtype)
 
 
 def farthest_first(z, k):
@@ -538,7 +539,7 @@
         def _(i):
             self.core_copy(p, i).wait_recv()
             dst = self.view(p, i // 2, i % 2, c)
-            dst[...] = add_into(dst, [(self.got_core.at[p, i], None)]).astype(BF16)
+            add_into(dst, dst, [(self.got_core.at[p, i], None)])
 
     def x_slot(self, p, zz):
         return self.got_x.at[PIECES * NZ if p == self.turned else self.straight.index(p) * NZ + zz]
@@ -574,7 +575,7 @@
 
     def home(self):
         self.home_copy().wait_recv()
-        self.store(LENT_OUT, self.got_home[...].astype(F32))
+        self.store(LENT_OUT, self.got_home, [])
 
     def x_send(self, p, first=0, last=NZ):
         s, z, x, c = self.where
@@ -623,7 +624,7 @@
         terms = [] if p == self.turned else [self.x_wait(p, zz)]
         for xx in self.cols(p):
             dst = self.view(p, zz, xx, c)
-            dst[...] = add_into(dst, terms + [self.z_wait(p, zz, xx, zz, before)]).astype(BF16)
+            add_into(dst, dst, terms + [self.z_wait(p, zz, xx, zz, before)])
             self.z_out(p, zz, xx, sign).start()
 
     def z_last(self, p, xx):
@@ -633,18 +634,18 @@
     def turn(self, p):
         s, z, x, c = self.where
         dst = self.view(p, z, 1 - x, c)
-        dst[...] = add_into(dst, self.z_last(p, 1 - x)).astype(BF16)
+        add_into(dst, dst, self.z_last(p, 1 - x))
         self.x_copy(p, z).start()
 
     def close(self, p):
         s, z, x, c = self.where
         dst = self.view(p, z, x, c)
-        total = add_into(dst, [self.x_wait(p, z)] + self.z_last(p, x))
+        terms = [self.x_wait(p, z)] + self.z_last(p, x)
         if p == LENT_SUM:
-            dst[...] = total.astype(BF16)
+            add_into(dst, dst, terms)
             self.home_copy().start()
         else:
-            self.store(p, total)
+            self.store(p, dst, terms)
 
     def drain(self):
         for p in range(PIECES):
@@ -756,8 +757,8 @@
     def store_copy(p):
         return pltpu.make_async_copy(staged(p), in_hbm(p, d_q, (d_o, d_u, d_d)), out_sem.at[p])
 
-    def store(p, value):
-        staged(p)[...] = value
+    def store(p, block, terms):
+        add_into(staged(p), block, terms)
         store_copy(p).start()
 
     gathers = [Gather(where, k, view, g_sems) for k in range(2)]
@@ -775,18 +776,31 @@
         for k in range(width // TILE):
             emit(slice(k * TILE, (k + 1) * TILE), value[:, k * TILE : (k + 1) * TILE])
 
-    def project(p, a, emit):
-        tiles(emit, jnp.dot(a[...], held[p], preferred_element_type=F32))
+    def project(p, a, emit, halves):
+        if not halves:
+            tiles(emit, jnp.dot(a[...], held[p], preferred_element_type=F32))
+            return
+
+        @pl.loop(0, 2)
+        def _(k):
+            lanes = pl.ds(pl.multiple_of(k * half, 128), half)
+            emit(lanes, jnp.dot(a[...], held[p, :, lanes], preferred_element_type=F32))
 
     def project_back(pieces, emit):
-        total = None
-        for p, a in pieces:
-            term = contract_cols(a[...], held[p])
-            total = term if total is None else total + term
-        tiles(emit, total)
+        @pl.loop(0, 2)
+        def _(k):
+            lanes = pl.ds(pl.multiple_of(k * half, 128), half)
+            total = None
+            for p, a in pieces:
+                term = contract_cols(a[...], held[p, lanes, :])
+                total = term if total is None else total + term
+            emit(lanes, total)
 
     def weight_grad(p, a, g):
-        held[p] = contract_rows(a[...], g[...]).astype(BF16)
+        @pl.loop(0, 2)
+        def _(k):
+            lanes = pl.ds(pl.multiple_of(k * half, 128), half)
+            held[p, lanes] = contract_rows(a[:, lanes], g[...]).astype(BF16)
 
     def recip_of(value):
         return lax.rsqrt(jnp.mean(value * value, -1, keepdims=True) + NORM_EPS)
@@ -822,8 +836,8 @@
         lane = lax.broadcasted_iota(jnp.int32, (1, span), 1)
         return ((lane >= offset) & (lane < offset + HD)).astype(F32).astype(BF16)
 
-    def attention(body, first, last):
-        @pl.loop(2 * first, 2 * last)
+    def attention(body):
+        @pl.loop(0, 2 * rows // slots)
         def _(it):
             seq, g = it // 2, it % 2
             r = pl.ds(pl.multiple_of(seq * slots, slots), slots)
@@ -933,23 +947,23 @@
         row = lax.broadcasted_iota(jnp.int32, (8, 128), 0)
         small_out[...] = jnp.where(row == 2, heads * gate, own)
 
-    def forward_stage(p):
+    def forward_stage(p, halves):
         if p == 0:
             spread_gains()
             norm(hb, 0, a1)
-            project(0, a1, emit_query)
+            project(0, a1, emit_query, halves)
         elif p == 1:
-            project(1, a1, put(kb))
+            project(1, a1, put(kb), halves)
         elif p == 2:
-            project(2, a1, put(vb))
-            attention(attend, 0, rows // slots)
+            project(2, a1, put(vb), halves)
+            attention(attend)
         elif p == 3:
-            project(3, ob, emit_mid)
+            project(3, ob, emit_mid, halves)
             norm(mid, 1, a2)
         elif p == 4:
-            project(4, a2, emit_up)
+            project(4, a2, emit_up, halves)
         else:
-            project(5, hid, emit_out)
+            project(5, hid, emit_out, halves)
 
 
     def hand(k):
@@ -992,7 +1006,7 @@
     def forward(section):
         for step in GATHER_STEPS[section]:
             if step[0] == "stage":
-                forward_stage(step[1])
+                forward_stage(step[1], True)
             elif step[0] == "hand":
                 for k in range(rows // slots):
                     hand(k).wait_recv()
@@ -1065,7 +1079,7 @@
         normed_two=lambda section: project_back([(4, dup)], put(up)),
         middle=lambda section: norm_grad(1, mid, grad, emit_dmid),
         attended=lambda section: project_back([(3, low)], put(dob)),
-        heads=lambda section, k: attention(attend_back, k, k + 1),
+        heads=lambda section: attention(attend_back),
         normed=lambda section: project_back([(0, qb), (1, kb), (2, vb)], put(up)),
         input=finish_input,
         weight=lambda section, p: weight_grad(p, *grads[p]),

time: 303 us -> 287 us (0.947); the launches traced: 297 us -> 285 us
  Pallas kernels: 296 us -> 284 us
    pallas_call x1, Pallas kernels: 291 us -> 279 us  [near_shards(): pl.pallas_call(lambda *refs: layers_kernel(n, *refs), out_shape=shapes +...]
where the time goes in v5:
time: 287 us; the launch traced here: 285 us
  Pallas kernels  284 us (99%)
    pallas_call x1, Pallas kernels, near_shards(): pl.pallas_call(lambda *refs: layers_kernel(n, *refs), out_shape=shapes +...  279 us

profile of v5, /device:TPU:0, one launch (start us, length us, event | category | flops | bytes accessed | tf_op | source)
XLA Modules:
  0.0 284.6 jit_solution(12156946397103631768)
XLA Ops:
  0.6 279.5 %two_layers.1 = (bf16[256,640]{1,0:T(8,128)(2,1)}, bf16[256,640]{1,0:T(8,128)(2,1)}, f32[80,3840]{1,0:T(8,128)}, f32[80,1280]{1,0:T(8,128)}, f32[80,1280]{1,0:T(...) custom-call(bf16[2,128,1280]{2,1,0:T(8,128)(2,1)} %refs_0_.1, bf16[2,128,1280]{2,1,0:T(8,128)(2,1)} %refs_1_.1, s32[2]{0:T(128)} %refs_2_.1, ...), custom_call_target="tpu_custom_call" | custom-call | tf_op jit(solution)/shard_map/two_layers/pallas_call | solution.py:1206
  280.1 4.3 %results.1 = (bf16[256,640]{1,0:T(8,128)(2,1)}, bf16[256,640]{1,0:T(8,128)(2,1)}, f32[80,3840]{1,0:T(8,128)}, f32[80,1280]{1,0:T(8,128)}, f32[80,1280]{1,0:T(8,1...) custom-call(f32[8,128]{1,0:T(8,128)} %get-tuple-element.23.small, ...), custom_call_target="tpu_custom_call" | custom-call | tf_op jit(solution)/shard_map/results/pallas_call | solution.py:1217

commit v6 on v5

--- a/solution.py
+++ b/solution.py
@@ -485,9 +485,9 @@
                 i = zz * 2 + xx
                 remote(block, block, self.core_send.at[p, i], self.core_recv.at[p, i], device(s, z, x, 1 - c)).wait_recv()
 
-    def drain(self):
+    def drain(self, pieces):
         for step in GATHER_STEPS[self.section]:
-            if step[0] not in ("finish", "stage", "hand"):
+            if step[0] not in ("finish", "stage", "hand") and step[1] in pieces:
                 getattr(self, step[0])(*step[1:], wait=True)
 
 
@@ -1021,7 +1021,7 @@
     def _():
         forward(0)
         hand_start()
-        gathers[0].drain()
+        gathers[0].drain(range(LENT + 1))
         for k in range(rows // slots):
             hand(k).wait_send()
             back(k).wait_recv()
@@ -1029,8 +1029,8 @@
     @pl.when(s == 1)
     def _():
         forward(1)
-        gathers[1].drain()
         end(0).start()
+        gathers[1].drain((LENT, 5))
         out_half[...] = give[:, half:]
         for k in range(rows // slots):
             row = lax.broadcasted_iota(jnp.int32, (slots, 1), 0)
@@ -1070,6 +1070,7 @@
         if section == 1:
             for k in range(rows // slots):
                 back(k).start()
+            gathers[1].drain((0, 1, 2, 3, 4, GAINS))
         else:
             end(1).start()
             token_half[...] = give[:, :half]

time: 287 us -> 286 us (level)
  no operation moved by 1% of the time
where the time goes in v6:
time: 286 us; the launch traced here: 284 us
  Pallas kernels  283 us (99%)
    pallas_call x1, Pallas kernels, near_shards(): pl.pallas_call(lambda *refs: layers_kernel(n, *refs), out_shape=shapes +...  279 us

profile of v6, /device:TPU:0, one launch (start us, length us, event | category | flops | bytes accessed | tf_op | source)
XLA Modules:
  0.0 284.3 jit_solution(11661085197075793802)
XLA Ops:
  0.6 279.2 %two_layers.1 = (bf16[256,640]{1,0:T(8,128)(2,1)}, bf16[256,640]{1,0:T(8,128)(2,1)}, f32[80,3840]{1,0:T(8,128)}, f32[80,1280]{1,0:T(8,128)}, f32[80,1280]{1,0:T(...) custom-call(bf16[2,128,1280]{2,1,0:T(8,128)(2,1)} %refs_0_.1, bf16[2,128,1280]{2,1,0:T(8,128)(2,1)} %refs_1_.1, s32[2]{0:T(128)} %refs_2_.1, ...), custom_call_target="tpu_custom_call" | custom-call | tf_op jit(solution)/shard_map/two_layers/pallas_call | solution.py:1207
  279.8 4.3 %results.1 = (bf16[256,640]{1,0:T(8,128)(2,1)}, bf16[256,640]{1,0:T(8,128)(2,1)}, f32[80,3840]{1,0:T(8,128)}, f32[80,1280]{1,0:T(8,128)}, f32[80,1280]{1,0:T(8,1...) custom-call(f32[8,128]{1,0:T(8,128)} %get-tuple-element.23.small, ...), custom_call_target="tpu_custom_call" | custom-call | tf_op jit(solution)/shard_map/results/pallas_call | solution.py:1218
